TPU v7x, 32 devices: a whole 2x2x4 slice. The times are simulated.
32 devices in a mesh: dp: 8 (over z, y), head: 4 (over x, core).
Axes of the slice: x: 2, y: 2, z: 4, core: 2. Of those that a mesh axis runs over, the one named last changes fastest.
Arguments:
- tokens: bfloat16 [8, 2048, 512], P('dp', 'head'), may hold values from -6 to 6
- memory: bfloat16 [8, 1024, 512], P('dp', 'head'), may hold values from -6 to 6
- lengths: int32 [8], P('dp'), may hold values from 256 to 2048, as said below
- self_qkv: bfloat16 [512, 1536], replicated, may hold values from -0.25 to 0.25
- self_out: bfloat16 [512, 512], replicated, may hold values from -6 to 6
- cross_q: bfloat16 [512, 512], replicated, may hold values from -0.25 to 0.25
- cross_kv: bfloat16 [512, 1024], replicated, may hold values from -0.25 to 0.25
- cross_out: bfloat16 [512, 512], replicated, may hold values from -6 to 6
- ffn_in: bfloat16 [512, 2048], replicated, may hold values from -0.25 to 0.25
- ffn_in_bias: bfloat16 [2048], replicated, may hold values from -3 to 3
- ffn_out: bfloat16 [2048, 512], replicated, may hold values from -0.125 to 0.125
- ffn_out_bias: bfloat16 [512], replicated, may hold values from -3 to 3
- slot_weight: bfloat16 [1024, 512], replicated, may hold values from -0.1875 to 0.1875
- slot_bias: bfloat16 [512], replicated, may hold values from -3 to 3
- norm_gain: float32 [3, 512], replicated, may hold values from 0.5 to 1.5
- norm_shift: float32 [3, 512], replicated, may hold values from -3 to 3
- cotangent: bfloat16 [8, 2048, 512], P('dp', 'head'), may hold values from -6 to 6
Outputs:
- slots: bfloat16 [8, 2048, 512], P('dp', 'head')
- token_grad: bfloat16 [8, 2048, 512], P('dp', 'head')
- memory_grad: bfloat16 [8, 1024, 512], P('dp', 'head')
- self_qkv_grad: float32 [512, 1536], replicated
- self_out_grad: float32 [512, 512], replicated
- cross_q_grad: float32 [512, 512], replicated
- cross_kv_grad: float32 [512, 1024], replicated
- cross_out_grad: float32 [512, 512], replicated
- ffn_in_grad: float32 [512, 2048], replicated
- ffn_in_bias_grad: float32 [2048], replicated
- ffn_out_grad: float32 [2048, 512], replicated
- ffn_out_bias_grad: float32 [512], replicated
- slot_weight_grad: float32 [1024, 512], replicated
- slot_bias_grad: float32 [512], replicated
- norm_gain_grad: float32 [3, 512], replicated
- norm_shift_grad: float32 [3, 512], replicated
Inputs may be any that keep to these rules, and one draw needn't show every extreme that they name: `lengths`: some canvas has exactly 2048 live tokens, and another exactly 256.
All inputs are finite; a program needn't handle non-finite values.
Results may differ from a plain program's by a relative error of at most 0.025.
Values may be sent and summed in bfloat16 or wider, within the bound.
No kernel may reach another device: no remote copies, remote signals or barrier semaphores. Data moves between devices by JAX's collectives and lax.ppermute only.
A program may use at most 128 MiB of HBM per device.

v0:
```python
import jax
import jax.numpy as jnp
from jax import lax
from jax.sharding import PartitionSpec as P

D = 512
HEAD_DIM = 64
LEN = 2048
SRC = 1024


epsilon = 1e-05
masked_score = -1e30


def shifted(block, axis, distance):
    devices = range(lax.axis_size(axis))
    route = [(i - distance, i) for i in devices if i - distance in devices]
    return lax.ppermute(block, axis, route)


def layer_norm(values, gain, shift):
    centred = values - jnp.mean(values, axis=-1, keepdims=True)
    spread = jnp.mean(centred * centred, axis=-1, keepdims=True)
    return centred * lax.rsqrt(spread + epsilon) * gain + shift


def norm_backward(values, gain, shift, upstream):
    unused, pullback = jax.vjp(layer_norm, values, gain, shift)
    return pullback(upstream)


def project(operand, matrix):
    return jnp.einsum("cld,de->cle", operand, matrix, preferred_element_type=jnp.float32)


def project_back(gradients, matrix):
    return jnp.einsum("cle,de->cld", gradients, matrix, preferred_element_type=jnp.float32)


def weight_grad(activations, gradients):
    return jnp.einsum("cld,cle->de", activations, gradients, preferred_element_type=jnp.float32)


def column_sum(gradients):
    return jnp.sum(gradients.astype(jnp.float32), axis=(0, 1))


def attend_forward(query_heads, key_heads, value_heads, live_keys):
    row_count = query_heads.shape[1]
    feature_width = query_heads.shape[2]
    head_count = feature_width // HEAD_DIM
    block_rows = min(512, row_count)
    block_count = row_count // block_rows
    scale_factor = HEAD_DIM ** (-0.5)

    def per_canvas(packed):
        query_part, key_part, value_part, live_part = packed
        key_split = key_part.reshape(-1, head_count, HEAD_DIM)
        value_split = value_part.reshape(-1, head_count, HEAD_DIM)
        query_blocks = query_part.reshape(block_count, block_rows, head_count, HEAD_DIM)

        def per_block(query_block):
            scores = (
                jnp.einsum(
                    "qhe,khe->hqk", query_block, key_split, preferred_element_type=jnp.float32
                )
                * scale_factor
            )
            scores = jnp.where(live_part[None, None, :], scores, masked_score)
            highest = jnp.max(scores, axis=-1, keepdims=True)
            exp_scores = jnp.exp(scores - highest)
            totals = jnp.sum(exp_scores, axis=-1, keepdims=True)
            attn_prob = (exp_scores / totals).astype(jnp.bfloat16)
            context = jnp.einsum(
                "hqk,khe->qhe", attn_prob, value_split, preferred_element_type=jnp.float32
            )
            return (context.reshape(block_rows, feature_width), (highest + jnp.log(totals))[..., 0])

        contexts, logsums = lax.map(per_block, query_blocks)
        return (contexts.reshape(row_count, feature_width), logsums)

    return lax.map(per_canvas, (query_heads, key_heads, value_heads, live_keys))


def attend_backward(query_heads, key_heads, value_heads, live_keys, logsums, grad_heads):
    row_count = query_heads.shape[1]
    feature_width = query_heads.shape[2]
    head_count = feature_width // HEAD_DIM
    block_rows = min(512, row_count)
    block_count = row_count // block_rows
    scale_factor = HEAD_DIM ** (-0.5)

    def per_canvas(packed):
        query_part, key_part, value_part, live_part, logsum_part, grad_part = packed
        key_split = key_part.reshape(-1, head_count, HEAD_DIM)
        value_split = value_part.reshape(-1, head_count, HEAD_DIM)
        query_blocks = query_part.reshape(block_count, block_rows, head_count, HEAD_DIM)
        grad_blocks = grad_part.reshape(block_count, block_rows, head_count, HEAD_DIM)

        def per_block(running, inputs):
            key_acc, value_acc = running
            query_block, grad_block, logsum_block = inputs
            scores = (
                jnp.einsum(
                    "qhe,khe->hqk", query_block, key_split, preferred_element_type=jnp.float32
                )
                * scale_factor
            )
            scores = jnp.where(live_part[None, None, :], scores, masked_score)
            attn_prob = jnp.exp(scores - logsum_block[..., None])
            prob_grad = jnp.einsum(
                "qhe,khe->hqk", grad_block, value_split, preferred_element_type=jnp.float32
            )
            centre = jnp.sum(attn_prob * prob_grad, axis=-1, keepdims=True)
            score_grad = (attn_prob * (prob_grad - centre)).astype(jnp.bfloat16)
            query_grad = (
                jnp.einsum(
                    "hqk,khe->qhe", score_grad, key_split, preferred_element_type=jnp.float32
                )
                * scale_factor
            )
            key_acc = (
                key_acc
                + jnp.einsum(
                    "hqk,qhe->khe", score_grad, query_block, preferred_element_type=jnp.float32
                )
                * scale_factor
            )
            value_acc = value_acc + jnp.einsum(
                "hqk,qhe->khe",
                attn_prob.astype(jnp.bfloat16),
                grad_block,
                preferred_element_type=jnp.float32,
            )
            return ((key_acc, value_acc), query_grad.reshape(block_rows, feature_width))

        zero_keys = jnp.zeros(key_split.shape, jnp.float32)
        (key_acc, value_acc), query_grads = lax.scan(
            per_block, (zero_keys, zero_keys), (query_blocks, grad_blocks, logsum_part)
        )
        return (
            query_grads.reshape(row_count, feature_width),
            key_acc.reshape(-1, feature_width),
            value_acc.reshape(-1, feature_width),
        )

    return lax.map(
        per_canvas, (query_heads, key_heads, value_heads, live_keys, logsums, grad_heads)
    )


def shards(
    tokens,
    memory,
    lengths,
    self_qkv,
    self_out,
    cross_q,
    cross_kv,
    cross_out,
    ffn_in,
    ffn_in_bias,
    ffn_out,
    ffn_out_bias,
    slot_weight,
    slot_bias,
    norm_gain,
    norm_shift,
    cotangent,
):
    local_rows = tokens.shape[1]
    positions = lax.axis_index("head") * local_rows + jnp.arange(local_rows, dtype=jnp.int32)
    live_keys = jnp.arange(LEN, dtype=jnp.int32)[None, :] < lengths[:, None]
    memory_live = jnp.zeros((memory.shape[0], SRC), jnp.int32) == 0
    live_slots = (positions[None, :] < lengths[:, None] - 1)[..., None]
    projected = project(tokens, self_qkv).astype(jnp.bfloat16)
    query_heads, key_heads, value_heads = (
        lax.all_to_all(projected[..., :D], "head", split_axis=2, concat_axis=1, tiled=True),
        lax.all_to_all(projected[..., D : 2 * D], "head", split_axis=2, concat_axis=1, tiled=True),
        lax.all_to_all(projected[..., 2 * D :], "head", split_axis=2, concat_axis=1, tiled=True),
    )
    context_heads, self_logsums = attend_forward(query_heads, key_heads, value_heads, live_keys)
    context = lax.all_to_all(
        context_heads.astype(jnp.bfloat16), "head", split_axis=1, concat_axis=2, tiled=True
    )
    first_input = tokens.astype(jnp.float32) + project(context, self_out)
    first_norm = layer_norm(first_input, norm_gain[0], norm_shift[0])
    first_low = first_norm.astype(jnp.bfloat16)
    cross_queries = project(first_low, cross_q).astype(jnp.bfloat16)
    memory_proj = project(memory, cross_kv).astype(jnp.bfloat16)
    cross_query_heads, cross_key_heads, cross_value_heads = (
        lax.all_to_all(cross_queries, "head", split_axis=2, concat_axis=1, tiled=True),
        lax.all_to_all(memory_proj[..., :D], "head", split_axis=2, concat_axis=1, tiled=True),
        lax.all_to_all(memory_proj[..., D:], "head", split_axis=2, concat_axis=1, tiled=True),
    )
    cross_heads_out, cross_logsums = attend_forward(
        cross_query_heads, cross_key_heads, cross_value_heads, memory_live
    )
    cross_context = lax.all_to_all(
        cross_heads_out.astype(jnp.bfloat16), "head", split_axis=1, concat_axis=2, tiled=True
    )
    second_input = first_norm + project(cross_context, cross_out)
    second_norm = layer_norm(second_input, norm_gain[1], norm_shift[1])
    second_low = second_norm.astype(jnp.bfloat16)
    hidden_pre = project(second_low, ffn_in) + ffn_in_bias.astype(jnp.float32)
    hidden_low = jax.nn.gelu(hidden_pre).astype(jnp.bfloat16)
    third_input = second_norm + project(hidden_low, ffn_out) + ffn_out_bias.astype(jnp.float32)
    third_norm = layer_norm(third_input, norm_gain[2], norm_shift[2])
    third_low = third_norm.astype(jnp.bfloat16)
    arriving = shifted(third_low[:, :1], "head", -1)
    following = jnp.concatenate([third_low[:, 1:], arriving], axis=1)
    slot_pre = (
        project(third_low, slot_weight[:D])
        + project(following, slot_weight[D:])
        + slot_bias.astype(jnp.float32)
    )
    slots = jnp.where(live_slots, slot_pre, 0.0).astype(jnp.bfloat16)
    slot_grad = jnp.where(live_slots, cotangent.astype(jnp.float32), 0.0).astype(jnp.bfloat16)
    grad_slot_bias = column_sum(slot_grad)
    grad_slot_weight = jnp.concatenate(
        [weight_grad(third_low, slot_grad), weight_grad(following, slot_grad)], axis=0
    )
    own_grad = project_back(slot_grad, slot_weight[:D])
    following_grad = project_back(slot_grad, slot_weight[D:])
    carried = shifted(following_grad[:, -1:], "head", 1)
    third_grad = own_grad + jnp.concatenate([carried, following_grad[:, :-1]], axis=1)
    third_input_grad, gain_grad_late, shift_grad_late = norm_backward(
        third_input, norm_gain[2], norm_shift[2], third_grad
    )
    ffn_grad = third_input_grad.astype(jnp.bfloat16)
    grad_ffn_out_bias = column_sum(ffn_grad)
    grad_ffn_out = weight_grad(hidden_low, ffn_grad)
    unused, gelu_pull = jax.vjp(jax.nn.gelu, hidden_pre)
    hidden_grad = gelu_pull(project_back(ffn_grad, ffn_out))[0].astype(jnp.bfloat16)
    grad_ffn_in_bias = column_sum(hidden_grad)
    grad_ffn_in = weight_grad(second_low, hidden_grad)
    second_grad = third_input_grad + project_back(hidden_grad, ffn_in)
    second_input_grad, gain_grad_middle, shift_grad_middle = norm_backward(
        second_input, norm_gain[1], norm_shift[1], second_grad
    )
    cross_branch_grad = second_input_grad.astype(jnp.bfloat16)
    grad_cross_out = weight_grad(cross_context, cross_branch_grad)
    cross_context_grad = project_back(cross_branch_grad, cross_out).astype(jnp.bfloat16)
    cross_grad_heads = lax.all_to_all(
        cross_context_grad, "head", split_axis=2, concat_axis=1, tiled=True
    )
    cross_query_hgrad, cross_key_hgrad, cross_value_hgrad = attend_backward(
        cross_query_heads,
        cross_key_heads,
        cross_value_heads,
        memory_live,
        cross_logsums,
        cross_grad_heads,
    )
    cross_query_grad, cross_key_grad, cross_value_grad = (
        lax.all_to_all(
            cross_query_hgrad.astype(jnp.bfloat16), "head", split_axis=1, concat_axis=2, tiled=True
        ),
        lax.all_to_all(
            cross_key_hgrad.astype(jnp.bfloat16), "head", split_axis=1, concat_axis=2, tiled=True
        ),
        lax.all_to_all(
            cross_value_hgrad.astype(jnp.bfloat16), "head", split_axis=1, concat_axis=2, tiled=True
        ),
    )
    memory_proj_grad = jnp.concatenate([cross_key_grad, cross_value_grad], axis=-1)
    grad_cross_kv = weight_grad(memory, memory_proj_grad)
    memory_grad = project_back(memory_proj_grad, cross_kv).astype(jnp.bfloat16)
    grad_cross_q = weight_grad(first_low, cross_query_grad)
    first_grad = second_input_grad + project_back(cross_query_grad, cross_q)
    first_input_grad, gain_grad_early, shift_grad_early = norm_backward(
        first_input, norm_gain[0], norm_shift[0], first_grad
    )
    self_branch_grad = first_input_grad.astype(jnp.bfloat16)
    grad_self_out = weight_grad(context, self_branch_grad)
    context_grad = project_back(self_branch_grad, self_out).astype(jnp.bfloat16)
    self_grad_heads = lax.all_to_all(context_grad, "head", split_axis=2, concat_axis=1, tiled=True)
    query_hgrad, key_hgrad, value_hgrad = attend_backward(
        query_heads, key_heads, value_heads, live_keys, self_logsums, self_grad_heads
    )
    query_grad, key_grad, value_grad = (
        lax.all_to_all(
            query_hgrad.astype(jnp.bfloat16), "head", split_axis=1, concat_axis=2, tiled=True
        ),
        lax.all_to_all(
            key_hgrad.astype(jnp.bfloat16), "head", split_axis=1, concat_axis=2, tiled=True
        ),
        lax.all_to_all(
            value_hgrad.astype(jnp.bfloat16), "head", split_axis=1, concat_axis=2, tiled=True
        ),
    )
    projected_grad = jnp.concatenate([query_grad, key_grad, value_grad], axis=-1)
    grad_self_qkv = weight_grad(tokens, projected_grad)
    token_grad = (first_input_grad + project_back(projected_grad, self_qkv)).astype(jnp.bfloat16)
    combined = lax.psum(
        (
            grad_slot_weight,
            grad_slot_bias,
            grad_ffn_in,
            grad_ffn_in_bias,
            grad_ffn_out,
            grad_ffn_out_bias,
            gain_grad_late,
            shift_grad_late,
            grad_cross_q,
            grad_cross_kv,
            grad_cross_out,
            gain_grad_middle,
            shift_grad_middle,
            grad_self_qkv,
            grad_self_out,
            gain_grad_early,
            shift_grad_early,
        ),
        ("dp", "head"),
    )
    late_sums = combined[0:8]
    middle_sums = combined[8:13]
    early_sums = combined[13:17]
    norm_gain_grad = jnp.stack([early_sums[2], middle_sums[3], late_sums[6]], axis=0)
    norm_shift_grad = jnp.stack([early_sums[3], middle_sums[4], late_sums[7]], axis=0)
    return (
        slots,
        token_grad,
        memory_grad,
        early_sums[0],
        early_sums[1],
        middle_sums[0],
        middle_sums[1],
        middle_sums[2],
        late_sums[2],
        late_sums[3],
        late_sums[4],
        late_sums[5],
        late_sums[0],
        late_sums[1],
        norm_gain_grad,
        norm_shift_grad,
    )


def solution(mesh):
    return jax.shard_map(
        shards,
        mesh=mesh,
        in_specs=(
            P("dp", "head", None),
            P("dp", "head", None),
            P("dp"),
            P(),
            P(),
            P(),
            P(),
            P(),
            P(),
            P(),
            P(),
            P(),
            P(),
            P(),
            P(),
            P(),
            P("dp", "head", None),
        ),
        out_specs=(
            P("dp", "head", None),
            P("dp", "head", None),
            P("dp", "head", None),
            P(),
            P(),
            P(),
            P(),
            P(),
            P(),
            P(),
            P(),
            P(),
            P(),
            P(),
            P(),
            P(),
        ),
        check_vma=False,
    )
```

profile of v0, /device:TPU:0, one launch (start us, length us, event | category | flops | bytes accessed | tf_op | source)
XLA Modules:
  0.0 918.3 jit_solution(15608242300226209841)
XLA Ops:
  14.0 4.5 reduce.23
  27.4 4.6 reduce.22
  34.4 4.4 all-to-all-start.1
  41.2 4.5 reduce.21
  77.6 32.5 %while.98 = (s32[]{:T(128)}, bf16[4,512,128]{2,1,0:T(8,128)(2,1)}, f32[4,2,512]{2,1,0:T(2,128)S(1)}, bf16[4,512,2,64]{1,3,2,0:T(8,128)(2,1)}, bf16[2048,2,64]{0,...) while((s32[]{:T(128)}, bf16[4,512,128]{2,1,0:T(8,128)(2,1)}, ...), condition=%wide.region_3.4_spmd.clone, body=%wide.region_0.3_spmd.clone.sunk | while | flops 562037760 | bytes 27041900 | solution.py:80
  112.9 13.7 %reduce.24 = bf16[2048,128]{1,0:T(8,128)(2,1)} reduce(bf16[2048,1,128]{2,1,0:T(2,128)(2,1)} %bitcast.465, bf16[]{:T(256)} %broadcast.403), dimensions={1}, to_apply=%bitcast.366.reduce_sub_computation | reduce | bytes 1048578
  133.9 8.0 all-to-all-done.3
  165.6 5.5 reduce.25
  193.0 18.5 %while.97 = (s32[]{:T(128)}, bf16[4,512,128]{2,1,0:T(8,128)(2,1)}, f32[4,2,512]{2,1,0:T(2,128)S(1)}, bf16[4,512,2,64]{1,3,2,0:T(8,128)(2,1)}, bf16[1024,2,64]{0,...) while((s32[]{:T(128)}, bf16[4,512,128]{2,1,0:T(8,128)(2,1)}, f32[4,2,512]{2,1,0:T(2,128)S(1)}, ...), condition=%wide.region_9.10_spmd, body=%wide.region_6.9_spmd.sunk | while | flops 277871616 | bytes 13926497 | solution.py:80
  214.2 13.3 %reduce.28 = bf16[2048,128]{1,0:T(8,128)(2,1)} reduce(bf16[2048,1,128]{2,1,0:T(2,128)(2,1)} %bitcast.467, bf16[]{:T(256)} %broadcast.403), dimensions={1}, to_apply=%bitcast.365.reduce_sub_computation | reduce | bytes 1048578
  261.0 4.4 convert_reduce_fusion
  270.9 4.7 reduce.29
  283.5 6.3 all-to-all-done.8
  296.3 33.2 %while.99 = (s32[]{:T(128)}, f32[1024,2,64]{0,2,1:T(8,128)S(1)}, f32[1024,2,64]{0,2,1:T(8,128)S(1)}, bf16[4,512,128]{2,1,0:T(8,128)(2,1)}, bf16[4,512,2,64]{1,3,...) while((s32[]{:T(128)}, f32[1024,2,64]{0,2,1:T(8,128)S(1)}, ...), condition=%wide.region_20.21_spmd.clone, body=%wide.region_18.20_spmd.clone.sunk | while | flops 684456960 | bytes 37646512 | solution.py:139
  332.2 12.5 %reduce.30 = bf16[2048,128]{1,0:T(8,128)(2,1)S(1)} reduce(bf16[2048,1,128]{2,1,0:T(2,128)(2,1)} %bitcast.469, bf16[]{:T(256)} %broadcast.403), dimensions={1}, to_apply=%bitcast.364.reduce_sub_computation | reduce | bytes 1048578
  349.9 6.4 fusion.109
  375.2 5.5 reduce.31
  387.0 5.3 fusion.150
  421.0 65.0 %while.100 = (s32[]{:T(128)}, f32[2048,2,64]{0,2,1:T(8,128)S(1)}, f32[2048,2,64]{0,2,1:T(8,128)}, bf16[4,512,128]{2,1,0:T(8,128)(2,1)}, bf16[4,512,2,64]{1,3,2,0...) while((s32[]{:T(128)}, f32[2048,2,64]{0,2,1:T(8,128)S(1)}, ...), condition=%wide.region_25.26_spmd.clone, body=%wide.region_23.25_spmd.clone.sunk | while | flops 1375077376 | bytes 71995576 | solution.py:139
  488.6 12.9 %reduce.34 = bf16[2048,128]{1,0:T(8,128)(2,1)S(1)} reduce(bf16[2048,1,128]{2,1,0:T(2,128)(2,1)} %bitcast.471, bf16[]{:T(256)} %broadcast.403), dimensions={1}, to_apply=%bitcast.363.reduce_sub_computation | reduce | bytes 1048578
  512.4 11.4 %reduce.33 = bf16[2048,128]{1,0:T(8,128)(2,1)S(1)} reduce(bf16[2048,1,128]{2,1,0:T(2,128)(2,1)S(1)} %bitcast.472, bf16[]{:T(256)} %broadcast.403), dimensions={1}, to_apply=%bitcast.302.reduce_sub_computation | reduce | bytes 1048578
  542.5 13.3 %reduce.32 = bf16[2048,128]{1,0:T(8,128)(2,1)} reduce(bf16[2048,1,128]{2,1,0:T(2,128)(2,1)} %bitcast.462, bf16[]{:T(256)} %broadcast.403), dimensions={1}, to_apply=%bitcast.300.reduce_sub_computation | reduce | bytes 1048578
  586.9 44.7 %all-reduce = (f32[2048]{0:T(1024)}, f32[512]{0:T(512)}, f32[512]{0:T(512)}, f32[1,512]{1,0:T(1,128)S(1)}, f32[1,512]{1,0:T(1,128)S(1)}, /*index=5*/f32[1,512]{1...) all-reduce(f32[2048]{0:T(1024)S(1)} %copy-done.55, ...), channel_id=1, replica_groups=mesh['dp'=8,'head'=4] {'dp','head'}, use_global_device_ids=true, to_apply=%region_33.34 | all-reduce | flops 6144 | bytes 49152 | tf_op jit(solution)/shard_map/psum | solution.py:296
  636.0 256.0 %all-reduce.4.cloned.1.call-done = (f32[512,1536]{0,1:T(8,128)}, f32[512,512]{1,0:T(8,128)}, f32[512,512]{1,0:T(8,128)}, f32[512,1024]{0,1:T(8,128)}, f32[512,51...) async-done(((f32[512,1536]{0,1:T(8,128)}, f32[512,512]{1,0:T(8,128)}, f32[512,512]{1,0:T(8,128)}, f32[512,1024]{0,1:T(8,128)}, ...) | async-done | bytes 18874384 | tf_op jit(solution)/shard_map/psum | solution.py:296
  (473 shorter events, 460.0 us)
Async XLA Ops:
  7.2 246.1 %copy-start = (bf16[2048,512]{1,0:T(8,128)(2,1)S(1)}, bf16[2048,512]{1,0:T(8,128)(2,1)}, u32[]{:S(2)}) copy-start(bf16[2048,512]{1,0:T(8,128)(2,1)} %param.35) | copy-start | bytes 6291460
  20.8 13.7 %all-to-all-start.2 = ((bf16[4,2,32768]{2,1,0:T(2,128)(2,1)}), bf16[4,2,32768]{2,1,0:T(2,128)(2,1)}, u32[]{:S(2)}, u32[]{:S(2)}) async-start(bf16[4,2,32768]{2,1,0:T(2,128)(2,1)} %reshape.684), calls=%async_computation.2 | async-start | bytes 1048576 | tf_op jit(solution)/shard_map/all_to_all | solution.py:181
  34.4 13.6 %all-to-all-start.1 = ((bf16[4,2,32768]{2,1,0:T(2,128)(2,1)}), bf16[4,2,32768]{2,1,0:T(2,128)(2,1)}, u32[]{:S(2)}, u32[]{:S(2)}) async-start(bf16[4,2,32768]{2,1,0:T(2,128)(2,1)} %reshape.682), calls=%async_computation.1 | async-start | bytes 1048576 | tf_op jit(solution)/shard_map/all_to_all | solution.py:180
  48.0 23.1 %all-to-all-start = ((bf16[4,2,32768]{2,1,0:T(2,128)(2,1)}), bf16[4,2,32768]{2,1,0:T(2,128)(2,1)}, u32[]{:S(2)}, u32[]{:S(2)}) async-start(bf16[4,2,32768]{2,1,0:T(2,128)(2,1)} %reshape.680), calls=%async_computation | async-start | bytes 1048576 | tf_op jit(solution)/shard_map/all_to_all | solution.py:179
  110.1 40.7 %copy-start.5 = (bf16[2048,2,64]{0,2,1:T(8,128)(2,1)}, bf16[2048,2,64]{0,2,1:T(8,128)(2,1)S(1)}, u32[]{:S(2)}) copy-start(bf16[2048,2,64]{0,2,1:T(8,128)(2,1)S(1)} %get-tuple-element.1036) | copy-start | bytes 1572868
  110.2 40.7 %copy-start.44 = (f32[4,2,512]{2,1,0:T(2,128)}, f32[4,2,512]{2,1,0:T(2,128)S(1)}, u32[]{:S(2)}) copy-start(f32[4,2,512]{2,1,0:T(2,128)S(1)} %get-tuple-element.972) | copy-start | bytes 49156
  128.6 13.3 %all-to-all-start.3 = ((bf16[4,2,32768]{2,1,0:T(2,128)(2,1)}), bf16[4,2,32768]{2,1,0:T(2,128)(2,1)}, u32[]{:S(2)}, u32[]{:S(2)}) async-start(bf16[4,2,32768]{2,1,0:T(2,128)(2,1)} %reshape.686), calls=%async_computation.3 | async-start | bytes 1048576 | tf_op jit(solution)/shard_map/all_to_all | solution.py:184
  141.9 13.4 %all-to-all-start.6 = ((bf16[4,2,16384]{2,1,0:T(2,128)(2,1)}), bf16[4,2,16384]{2,1,0:T(2,128)(2,1)S(1)}, u32[]{:S(2)}, u32[]{:S(2)}) async-start(bf16[4,2,16384]{2,1,0:T(2,128)(2,1)} %reshape.692), calls=%async_computation.6 | async-start | bytes 524288 | tf_op jit(solution)/shard_map/all_to_all | solution.py:195
  155.3 18.0 %all-to-all-start.5 = ((bf16[4,2,16384]{2,1,0:T(2,128)(2,1)}), bf16[4,2,16384]{2,1,0:T(2,128)(2,1)}, u32[]{:S(2)}, u32[]{:S(2)}) async-start(bf16[4,2,16384]{2,1,0:T(2,128)(2,1)} %reshape.690), calls=%async_computation.5 | async-start | bytes 524288 | tf_op jit(solution)/shard_map/all_to_all | solution.py:194
  173.3 13.2 %all-to-all-start.4 = ((bf16[4,2,32768]{2,1,0:T(2,128)(2,1)}), bf16[4,2,32768]{2,1,0:T(2,128)(2,1)}, u32[]{:S(2)}, u32[]{:S(2)}) async-start(bf16[4,2,32768]{2,1,0:T(2,128)(2,1)} %reshape.688), calls=%async_computation.4 | async-start | bytes 1048576 | tf_op jit(solution)/shard_map/all_to_all | solution.py:193
  229.4 13.0 %all-to-all-start.7 = ((bf16[4,2,32768]{2,1,0:T(2,128)(2,1)}), bf16[4,2,32768]{2,1,0:T(2,128)(2,1)}, u32[]{:S(2)}, u32[]{:S(2)}) async-start(bf16[4,2,32768]{2,1,0:T(2,128)(2,1)} %reshape.694), calls=%async_computation.7 | async-start | bytes 1048576 | tf_op jit(solution)/shard_map/all_to_all | solution.py:200
  235.3 20.3 %collective-permute-start.1 = (f32[1,1,512]{2,1,0:T(1,128)S(1)}, f32[1,1,512]{2,1,0:T(1,128)S(1)}, u32[]{:S(2)}, u32[]{:S(2)}) collective-permute-start(f32[1,1,512]{2,1,0:T(1,128)S(1)} %slice.80), channel_id=1, source_target_pairs={{0,1},{1,2},{2,3},{4,5},{5,6},{6,7},{8,9},{9,10},{10,11},{12,13},{... | collective-permute-start | bytes 6152 | tf_op jit(solution)/shard_map/ppermute | solution.py:19
  268.4 27.8 %copy-start.10 = (bf16[1024,2,64]{0,2,1:T(8,128)(2,1)S(1)}, bf16[1024,2,64]{0,2,1:T(8,128)(2,1)}, u32[]{:S(2)}) copy-start(bf16[1024,2,64]{0,2,1:T(8,128)(2,1)} %copy-done.9) | copy-start | bytes 786436
  276.7 13.1 %all-to-all-start.8 = ((bf16[4,2,32768]{2,1,0:T(2,128)(2,1)}), bf16[4,2,32768]{2,1,0:T(2,128)(2,1)}, u32[]{:S(2)}, u32[]{:S(2)}) async-start(bf16[4,2,32768]{2,1,0:T(2,128)(2,1)} %reshape.696), calls=%async_computation.8 | async-start | bytes 1048576 | tf_op jit(solution)/shard_map/all_to_all | solution.py:245
  282.2 227.2 %collective-permute-start = (bf16[1,1,512]{2,1,0:T(2,128)(2,1)}, bf16[1,1,512]{2,1,0:T(2,128)(2,1)}, u32[]{:S(2)}, u32[]{:S(2)}) collective-permute-start(bf16[1,1,512]{2,1,0:T(2,128)(2,1)} %slice.79), channel_id=1, source_target_pairs={{1,0},{2,1},{3,2},{5,4},{6,5},{7,6},{9,8},{10,9},{11,10},{13,12},{... | collective-permute-start | bytes 3080 | tf_op jit(solution)/shard_map/ppermute | solution.py:19
  345.6 13.2 %all-to-all-start.9 = ((bf16[4,2,32768]{2,1,0:T(2,128)(2,1)}), bf16[4,2,32768]{2,1,0:T(2,128)(2,1)}, u32[]{:S(2)}, u32[]{:S(2)}) async-start(bf16[4,2,32768]{2,1,0:T(2,128)(2,1)} %reshape.698), calls=%async_computation.9 | async-start | bytes 1048576 | tf_op jit(solution)/shard_map/all_to_all | solution.py:257
  382.9 14.4 %all-to-all-start.10 = ((bf16[4,2,32768]{2,1,0:T(2,128)(2,1)}), bf16[4,2,32768]{2,1,0:T(2,128)(2,1)}, u32[]{:S(2)}, u32[]{:S(2)}) async-start(bf16[4,2,32768]{2,1,0:T(2,128)(2,1)} %reshape.700), calls=%async_computation.10 | async-start | bytes 1048576 | tf_op jit(solution)/shard_map/all_to_all | solution.py:278
  397.2 18.8 %all-to-all-start.14 = ((bf16[4,2,16384]{2,1,0:T(2,128)(2,1)}), bf16[4,2,16384]{2,1,0:T(2,128)(2,1)}, u32[]{:S(2)}, u32[]{:S(2)}) async-start(bf16[4,2,16384]{2,1,0:T(2,128)(2,1)} %reshape.710), calls=%async_computation.14 | async-start | bytes 524288 | tf_op jit(solution)/shard_map/all_to_all | solution.py:260
  416.1 86.4 %all-to-all-start.15 = ((bf16[4,2,16384]{2,1,0:T(2,128)(2,1)}), bf16[4,2,16384]{2,1,0:T(2,128)(2,1)}, u32[]{:S(2)}, u32[]{:S(2)}) async-start(bf16[4,2,16384]{2,1,0:T(2,128)(2,1)} %reshape.708), calls=%async_computation.15 | async-start | bytes 524288 | tf_op jit(solution)/shard_map/all_to_all | solution.py:263
  502.4 22.4 %all-to-all-start.11 = ((bf16[4,2,32768]{2,1,0:T(2,128)(2,1)}), bf16[4,2,32768]{2,1,0:T(2,128)(2,1)}, u32[]{:S(2)}, u32[]{:S(2)}) async-start(bf16[4,2,32768]{2,1,0:T(2,128)(2,1)} %reshape.706), calls=%async_computation.11 | async-start | bytes 1048576 | tf_op jit(solution)/shard_map/all_to_all | solution.py:283
  524.8 32.9 %all-to-all-start.12 = ((bf16[4,2,32768]{2,1,0:T(2,128)(2,1)}), bf16[4,2,32768]{2,1,0:T(2,128)(2,1)}, u32[]{:S(2)}, u32[]{:S(2)}) async-start(bf16[4,2,32768]{2,1,0:T(2,128)(2,1)} %reshape.704), calls=%async_computation.12 | async-start | bytes 1048576 | tf_op jit(solution)/shard_map/all_to_all | solution.py:286
  557.7 15.1 %all-to-all-start.13 = ((bf16[4,2,32768]{2,1,0:T(2,128)(2,1)}), bf16[4,2,32768]{2,1,0:T(2,128)(2,1)}, u32[]{:S(2)}, u32[]{:S(2)}) async-start(bf16[4,2,32768]{2,1,0:T(2,128)(2,1)} %reshape.702), calls=%async_computation.13 | async-start | bytes 1048576 | tf_op jit(solution)/shard_map/all_to_all | solution.py:289
  561.8 330.1 %all-reduce.4.cloned.1.call-start = ((), (), s32[]{:S(2)}) async-start(), calls=%async_computation.16 | async-start | bytes 37748736 | tf_op jit(solution)/shard_map/psum | solution.py:296
  583.2 49.0 %copy-start.41 = (bf16[1,512,4,128]{1,3,2,0:T(8,128)(2,1)S(1)}, bf16[1,512,4,128]{1,3,2,0:T(8,128)(2,1)}, u32[]{:S(2)}) copy-start(bf16[1,512,4,128]{1,3,2,0:T(8,128)(2,1)} %copy.196) | copy-start | bytes 1572868
  (67 other events, 654.5 us)
Sparse Core Ops, SparseCore 0:
  579.6 312.2 all-reduce.3
where the time goes:
time: 935 us; the launch traced here: 918 us
  waiting for transfers between devices  280 us (30%)
  local copies, waits for them, and re-layouts  178 us (19%)
  matrix products  170 us (18%)
  other arithmetic  159 us (17%)
  starting transfers between devices  70 us (7%)
  blocking collectives  44.7 us (5%)
  between operations  16.1 us (2%)
    psum x1, waiting for transfers between devices, shards(): lax.psum((grad_slot_weight, grad_slot_bias, grad_ffn_in, grad_ffn_in_bias...  256 us
    unnamed x20, other arithmetic  116 us
    unnamed x185, local copies, waits for them, and re-layouts  108 us
    psum x1, blocking collectives, shards(): lax.psum((grad_slot_weight, grad_slot_bias, grad_ffn_in, grad_ffn_in_bias...  44.7 us
    dot_general x16, matrix products, per_block(): jnp.einsum('qhe,khe->hqk', query_block, key_split, preferred_element_type...  32 us
    dot_general x9, matrix products, weight_grad(): jnp.einsum('cld,cle->de', activations, gradients, preferred_element_type=...  29.4 us
    dot_general x8, matrix products, per_block(): jnp.einsum('hqk,qhe->khe', attn_prob.astype(jnp.bfloat16), grad_block, pr...  18.8 us
  transfers between devices with their start and end apart: 19, of which 8 were waited for; matrix products, arithmetic and copies ran while one was open for 37% of the time, Pallas kernels for 0%

commit v1 on v0

v1 whole, which is shorter than its diff:
```python
import jax
import jax.numpy as jnp
import numpy as np
from jax import lax
from jax.experimental import pallas as pl
from jax.experimental.pallas import tpu as pltpu
from jax.sharding import PartitionSpec as P

HEAD_DIM = 64
WIDE = 128
epsilon = 1e-05
masked_score = -1e30
log2_e = 1.4426950408889634
f32 = jnp.float32
bf16 = jnp.bfloat16


def dot(a, b, ca=1, cb=0):
    return lax.dot_general(a, b, (((ca,), (cb,)), ((), ())), preferred_element_type=f32)


def params(mib=56):
    return pltpu.CompilerParams(vmem_limit_bytes=mib * 2**20)


def in_lanes(base, lane, column):
    high = column.astype(bf16).astype(f32)
    rest = column - high
    middle = rest.astype(bf16).astype(f32)
    low = rest - middle
    base = jnp.where(lane == HEAD_DIM + 1, high, base)
    base = jnp.where(lane == HEAD_DIM + 2, middle, base)
    return jnp.where(lane == HEAD_DIM + 3, low, base)


def attend_forward(queries, keys_t, values_t, extra):
    rows, wide = queries.shape
    heads = wide // WIDE
    block = 256
    count = rows // block

    def kernel(q_ref, k_ref, v_ref, e_ref, o_ref, qa_ref):
        def step(i, carry):
            h = i // count
            at = pl.ds(pl.multiple_of((i % count) * block, block), block)
            lanes = pl.ds(pl.multiple_of(h * WIDE, WIDE), WIDE)
            feats = pl.ds(pl.multiple_of(h * HEAD_DIM, HEAD_DIM), HEAD_DIM)
            lane = lax.broadcasted_iota(jnp.int32, (block, WIDE), 1)
            extra_rows = e_ref[...]
            q = q_ref[at, lanes]
            q = jnp.where(lane == HEAD_DIM, 1.0, q.astype(f32))
            scores = dot(q.astype(bf16), jnp.concatenate([k_ref[feats, :], extra_rows], axis=0))
            top = jnp.max(scores, axis=1, keepdims=True)
            p = jnp.exp2(scores - top)
            total = jnp.sum(p, axis=1, keepdims=True)
            o_t = dot(jnp.concatenate([v_ref[feats, :], extra_rows], axis=0), p.astype(bf16), 1, 1)
            o_t = o_t / o_t[HEAD_DIM + 1 : HEAD_DIM + 2, :]
            sub = lax.broadcasted_iota(jnp.int32, o_t.shape, 0)
            o_t = jnp.where(sub < HEAD_DIM, o_t, 0.0)
            o_ref[at, lanes] = o_t.T.astype(bf16)
            qa_ref[at, lanes] = in_lanes(q, lane, -(top + jnp.log2(total))).astype(bf16)
            return carry

        lax.fori_loop(0, heads * count, step, 0)

    return pl.pallas_call(
        kernel,
        out_shape=(
            jax.ShapeDtypeStruct((rows, wide), bf16),
            jax.ShapeDtypeStruct((rows, wide), bf16),
        ),
        compiler_params=params(),
        name="attend_forward",
    )(queries, keys_t, values_t, extra)


def attend_backward(queries, keys_t, values_t, extra, outs, grads):
    rows, wide = queries.shape
    heads = wide // WIDE
    keys = keys_t.shape[1]
    block = 512
    feat = heads * HEAD_DIM

    def kernel(q_ref, k_ref, v_ref, e_ref, o_ref, g_ref, dq_ref, dk_ref, dv_ref, acc):
        def head(h, carry):
            lanes = pl.ds(pl.multiple_of(h * WIDE, WIDE), WIDE)
            feats = pl.ds(pl.multiple_of(h * HEAD_DIM, HEAD_DIM), HEAD_DIM)
            lane = lax.broadcasted_iota(jnp.int32, (rows, WIDE), 1)
            q = q_ref[:, lanes]
            g = g_ref[:, lanes].astype(f32)
            centre = jnp.sum(g * o_ref[:, lanes].astype(f32), axis=1, keepdims=True)
            ga = in_lanes(g, lane, -centre).astype(bf16)
            q_t = q.T[:HEAD_DIM]
            g_t = g_ref[:, lanes].T[:HEAD_DIM]
            acc[...] = jnp.zeros_like(acc)

            def keyblock(j, c):
                at = pl.ds(pl.multiple_of(j * block, block), block)
                extra_rows = e_ref[:, at]
                k = k_ref[feats, at]
                v = v_ref[feats, at]
                p = jnp.exp2(dot(q, jnp.concatenate([k, extra_rows], axis=0)))
                dp = dot(ga, jnp.concatenate([v, extra_rows], axis=0))
                ds = (p * dp).astype(bf16)
                dv_ref[feats, at] = dot(g_t, p.astype(bf16)).astype(bf16)
                dk_ref[feats, at] = (dot(q_t, ds) * (1.0 / log2_e)).astype(bf16)
                acc[...] += dot(k, ds, 1, 1)
                return c

            lax.fori_loop(0, keys // block, keyblock, 0, unroll=True)
            dq_ref[feats, :] = (acc[...] * HEAD_DIM**-0.5).astype(bf16)
            return carry

        lax.fori_loop(0, heads, head, 0)

    return pl.pallas_call(
        kernel,
        out_shape=(
            jax.ShapeDtypeStruct((feat, rows), bf16),
            jax.ShapeDtypeStruct((feat, keys), bf16),
            jax.ShapeDtypeStruct((feat, keys), bf16),
        ),
        scratch_shapes=[pltpu.VMEM((HEAD_DIM, rows), f32)],
        compiler_params=params(),
        name="attend_backward",
    )(queries, keys_t, values_t, extra, outs, grads)


def swap(block, axis, bit):
    devices = range(lax.axis_size(axis))
    return lax.ppermute(block, axis, [(i, i ^ bit) for i in devices])


def has(axis, bit):
    return (lax.axis_index(axis) // bit) % 2


def halve(block, axis, bit):
    half = block.shape[0] // 2
    mine = has(axis, bit)
    sent = lax.dynamic_slice_in_dim(block, (1 - mine) * half, half)
    kept = lax.dynamic_slice_in_dim(block, mine * half, half)
    return kept, swap(sent, axis, bit)


def double(block, other, axis, bit):
    half = block.shape[0]
    mine = has(axis, bit)
    whole = jnp.zeros((2 * half,) + block.shape[1:], block.dtype)
    whole = lax.dynamic_update_slice_in_dim(whole, block, mine * half, 0)
    return lax.dynamic_update_slice_in_dim(whole, other, (1 - mine) * half, 0)


def add(a, b):
    return (a.astype(f32) + b.astype(f32)).astype(a.dtype)


def sum_rows(block):
    bits = []
    size = 1
    while size < lax.axis_size("dp"):
        bits.append(("dp", size))
        size *= 2
    far = []
    size = 2
    while size < lax.axis_size("head"):
        far.append(("head", size))
        size *= 2
    kept, other = halve(block, "head", 1)
    block = add(kept, other)
    rows = block.shape[0] // 2
    parts = [block[:rows], block[rows:]]
    orders = [far + bits, bits[:1] + far + bits[1:]]
    for n in range(len(orders[0])):
        both = [halve(part, *order[n]) for part, order in zip(parts, orders)]
        parts = [add(kept, other) for kept, other in both]
    for n in reversed(range(len(orders[0]))):
        both = [swap(part, *order[n]) for part, order in zip(parts, orders)]
        parts = [double(p, o, *order[n]) for p, o, order in zip(parts, both, orders)]
    block = jnp.concatenate(parts, axis=0)
    return double(block, swap(block, "head", 1), "head", 1)


def sum_small(block):
    size = 1
    while size < lax.axis_size("head"):
        block = block + swap(block, "head", size)
        size *= 2
    size = 1
    while size < lax.axis_size("dp"):
        block = block + swap(block, "dp", size)
        size *= 2
    return block


def gather_head(block):
    block = double(block, swap(block, "head", 2), "head", 2)
    rows = block.shape[0] // 2
    other = swap(block, "head", 1)
    mine = has("head", 1)
    first = jnp.where(mine == 0, block, other)
    second = jnp.where(mine == 0, other, block)
    return jnp.concatenate([first[:rows], second[:rows], first[rows:], second[rows:]], axis=0)


def scatter_head(partial):
    rows = partial.shape[0] // 4
    blocks = partial.reshape(2, 2, rows, -1)
    core = has("head", 1)
    pair = lax.dynamic_index_in_dim(blocks, core, 1, keepdims=False)
    sent = lax.dynamic_index_in_dim(blocks, 1 - core, 1, keepdims=False)
    pair = add(pair, swap(sent, "head", 1))
    side = has("head", 2)
    own = lax.dynamic_index_in_dim(pair, side, 0, keepdims=False)
    sent = lax.dynamic_index_in_dim(pair, 1 - side, 0, keepdims=False)
    return own.astype(f32) + swap(sent, "head", 2).astype(f32)


def shifted(block, axis, distance):
    devices = range(lax.axis_size(axis))
    route = [(i - distance, i) for i in devices if i - distance in devices]
    return lax.ppermute(block, axis, route)


def normed(values):
    centred = values - jnp.mean(values, axis=-1, keepdims=True)
    spread = jnp.mean(centred * centred, axis=-1, keepdims=True)
    scale = lax.rsqrt(spread + epsilon)
    return centred * scale, scale


def norm_backward(xhat, scale, gain, upstream):
    g = upstream * gain
    dv = scale * (
        g - jnp.mean(g, axis=-1, keepdims=True) - xhat * jnp.mean(g * xhat, axis=-1, keepdims=True)
    )
    return dv, jnp.sum(upstream * xhat, axis=0), jnp.sum(upstream, axis=0)


def pad_heads(matrix, axis):
    shape = list(matrix.shape)
    heads = shape[axis] // HEAD_DIM
    split = shape[:axis] + [heads, HEAD_DIM] + shape[axis + 1 :]
    pads = [(0, 0)] * len(split)
    pads[axis + 1] = (0, WIDE - HEAD_DIM)
    joined = shape[:axis] + [heads * WIDE] + shape[axis + 1 :]
    return jnp.pad(matrix.reshape(split), pads).reshape(joined)


def shards(
    tokens,
    memory,
    lengths,
    self_qkv,
    self_out,
    cross_q,
    cross_kv,
    cross_out,
    ffn_in,
    ffn_in_bias,
    ffn_out,
    ffn_out_bias,
    slot_weight,
    slot_bias,
    norm_gain,
    norm_shift,
    cotangent,
):
    tokens, memory, cotangent, length = tokens[0], memory[0], cotangent[0], lengths[0]
    rows, d = tokens.shape
    all_tokens = gather_head(tokens)
    all_memory = gather_head(memory)
    keys = all_tokens.shape[0]
    sources = all_memory.shape[0]
    positions = lax.axis_index("head") * rows + jnp.arange(rows, dtype=jnp.int32)
    live_slots = (positions < length - 1)[:, None]
    scale = HEAD_DIM**-0.5 * log2_e
    extra_index = jnp.arange(HEAD_DIM)[:, None]
    ones_rows = ((extra_index >= 1) & (extra_index <= 3)).astype(f32)
    dead = (jnp.arange(keys, dtype=jnp.int32) >= length)[None, :]
    self_extra = jnp.where((extra_index == 0) & dead, masked_score, ones_rows).astype(bf16)
    cross_extra = jnp.broadcast_to(ones_rows, (HEAD_DIM, sources)).astype(bf16)

    wq_pad = pad_heads(self_qkv[:, :d], 1)
    wout_pad = pad_heads(self_out, 0)
    cq_pad = pad_heads(cross_q, 1)
    cout_pad = pad_heads(cross_out, 0)

    queries = (dot(tokens, wq_pad) * scale).astype(bf16)
    kv_t = dot(self_qkv[:, d:], all_tokens, 0, 1).astype(bf16)
    keys_t, values_t = kv_t[:d], kv_t[d:]
    context, queries = attend_forward(queries, keys_t, values_t, self_extra)
    first_hat, first_scale = normed(tokens.astype(f32) + dot(context, wout_pad))
    first_norm = first_hat * norm_gain[0] + norm_shift[0]
    first_low = first_norm.astype(bf16)

    cross_queries = (dot(first_low, cq_pad) * scale).astype(bf16)
    mem_t = dot(cross_kv, all_memory, 0, 1).astype(bf16)
    mem_keys_t, mem_values_t = mem_t[:d], mem_t[d:]
    cross_context, cross_queries = attend_forward(
        cross_queries, mem_keys_t, mem_values_t, cross_extra
    )
    second_hat, second_scale = normed(first_norm + dot(cross_context, cout_pad))
    second_norm = second_hat * norm_gain[1] + norm_shift[1]
    second_low = second_norm.astype(bf16)
    hidden_pre = dot(second_low, ffn_in) + ffn_in_bias.astype(f32)
    hidden, gelu_pull = jax.vjp(jax.nn.gelu, hidden_pre)
    hidden_low = hidden.astype(bf16)
    third_hat, third_scale = normed(
        second_norm + dot(hidden_low, ffn_out) + ffn_out_bias.astype(f32)
    )
    third_low = (third_hat * norm_gain[2] + norm_shift[2]).astype(bf16)
    arriving = shifted(third_low[:1], "head", -1)
    following = jnp.concatenate([third_low[1:], arriving], axis=0)
    slot_pre = (
        dot(third_low, slot_weight[:d])
        + dot(following, slot_weight[d:])
        + slot_bias.astype(f32)
    )
    slots = jnp.where(live_slots, slot_pre, 0.0).astype(bf16)

    slot_grad = jnp.where(live_slots, cotangent.astype(f32), 0.0).astype(bf16)
    grad_slot_bias = jnp.sum(slot_grad.astype(f32), axis=0)
    following_grad = dot(slot_grad, slot_weight[d:], 1, 1)
    carried = shifted(following_grad[-1:], "head", 1)
    third_grad = dot(slot_grad, slot_weight[:d], 1, 1) + jnp.concatenate(
        [carried, following_grad[:-1]], axis=0
    )
    third_in_grad, gain_late, shift_late = norm_backward(
        third_hat, third_scale, norm_gain[2], third_grad
    )
    ffn_grad = third_in_grad.astype(bf16)
    grad_out_bias = jnp.sum(ffn_grad.astype(f32), axis=0)
    hidden_grad = gelu_pull(dot(ffn_grad, ffn_out, 1, 1))[0].astype(bf16)
    grad_in_bias = jnp.sum(hidden_grad.astype(f32), axis=0)
    late = sum_rows(
        jnp.concatenate(
            [
                dot(third_low, slot_grad, 0, 0).astype(bf16),
                dot(following, slot_grad, 0, 0).astype(bf16),
                dot(hidden_low, ffn_grad, 0, 0).astype(bf16),
                dot(hidden_grad, second_low, 0, 0).astype(bf16),
            ],
            axis=0,
        )
    )
    second_grad = third_in_grad + dot(hidden_grad, ffn_in, 1, 1)
    second_in_grad, gain_middle, shift_middle = norm_backward(
        second_hat, second_scale, norm_gain[1], second_grad
    )
    cross_branch = second_in_grad.astype(bf16)
    cross_dq_t, mem_dk_t, mem_dv_t = attend_backward(
        cross_queries,
        mem_keys_t,
        mem_values_t,
        cross_extra,
        cross_context,
        dot(cross_branch, cout_pad, 1, 1).astype(bf16),
    )
    mem_grad_t = jnp.concatenate([mem_dk_t, mem_dv_t], axis=0)
    memory_grad = scatter_head(dot(mem_grad_t, cross_kv, 0, 1).astype(bf16))
    first_grad = second_in_grad + dot(cross_dq_t, cross_q, 0, 1)
    first_in_grad, gain_early, shift_early = norm_backward(
        first_hat, first_scale, norm_gain[0], first_grad
    )
    self_branch = first_in_grad.astype(bf16)
    cross_out_grad = dot(cross_context, cross_branch, 0, 0).astype(bf16)
    middle = sum_rows(
        jnp.concatenate(
            [
                cross_out_grad.reshape(-1, WIDE, d)[:, :HEAD_DIM].reshape(d, d),
                dot(cross_dq_t, first_low).astype(bf16),
                dot(mem_grad_t, all_memory).astype(bf16),
            ],
            axis=0,
        )
    )
    small = sum_small(
        jnp.concatenate(
            [
                grad_in_bias,
                grad_out_bias,
                grad_slot_bias,
                gain_early,
                gain_middle,
                gain_late,
                shift_early,
                shift_middle,
                shift_late,
            ]
        )
    )
    dq_t, dk_t, dv_t = attend_backward(
        queries,
        keys_t,
        values_t,
        self_extra,
        context,
        dot(self_branch, wout_pad, 1, 1).astype(bf16),
    )
    kv_grad_t = jnp.concatenate([dk_t, dv_t], axis=0)
    token_grad = (
        first_in_grad
        + dot(dq_t, self_qkv[:, :d], 0, 1)
        + scatter_head(dot(kv_grad_t, self_qkv[:, d:], 0, 1).astype(bf16))
    )
    self_out_grad = dot(context, self_branch, 0, 0).astype(bf16)
    early = sum_rows(
        jnp.concatenate(
            [
                self_out_grad.reshape(-1, WIDE, d)[:, :HEAD_DIM].reshape(d, d),
                dot(dq_t, tokens).astype(bf16),
                dot(kv_grad_t, all_tokens).astype(bf16),
            ],
            axis=0,
        )
    )
    ff = ffn_in.shape[1]
    return (
        slots[None],
        token_grad.astype(bf16)[None],
        memory_grad.astype(bf16)[None],
        early[d:].T.astype(f32),
        early[:d].astype(f32),
        middle[d : 2 * d].T.astype(f32),
        middle[2 * d :].T.astype(f32),
        middle[:d].astype(f32),
        late[2 * d + ff :].T.astype(f32),
        small[:ff],
        late[2 * d : 2 * d + ff].astype(f32),
        small[ff : ff + d],
        late[: 2 * d].astype(f32),
        small[ff + d : ff + 2 * d],
        small[ff + 2 * d : ff + 5 * d].reshape(3, d),
        small[ff + 5 * d :].reshape(3, d),
    )


def solution(mesh):
    split = P("dp", "head", None)
    return jax.shard_map(
        shards,
        mesh=mesh,
        in_specs=(split, split, P("dp")) + (P(),) * 13 + (split,),
        out_specs=(split,) * 3 + (P(),) * 13,
        check_vma=False,
    )
```

time: 935 us -> 437 us (0.47); the launches traced: 918 us -> 431 us
  waiting for transfers between devices: 280 us -> 90.6 us
  matrix products: 170 us -> 49.6 us
  local copies, waits for them, and re-layouts: 178 us -> 61.4 us
  other arithmetic: 159 us -> 50.2 us
  Pallas kernels: 0 us -> 86.5 us
  blocking collectives: 44.7 us -> 0 us
  starting transfers between devices: 70 us -> 89.1 us
  between operations: 16.1 us -> 3.88 us
    psum x1 -> x0, waiting for transfers between devices: 256 us -> none  [shards(): lax.psum((grad_slot_weight, grad_slot_bias, grad_ffn_in, grad_ffn_in_bias...]
    dot_general x83 -> x30, matrix products: 170 us -> 49.6 us  [dot(): lax.dot_general(a, b, (((ca,), (cb,)), ((), ())), preferred_element_type=...]
    unnamed x20 -> x1, other arithmetic: 116 us -> 0.01 us
    ppermute x0 -> x67, waiting for transfers between devices: none -> 90.6 us  [swap(): return lax.ppermute(block, axis, [(i, i ^ bit) for i in devices])]
    pallas_call x0 -> x4, Pallas kernels: none -> 86.5 us  [the longest x2 45.6 us: attend_forward(): pl.pallas_call(kernel, out_shape=(jax.ShapeDtypeStruct((rows, wide), bf16...]
    ppermute x0 -> x67, starting transfers between devices: none -> 86.4 us  [swap(): return lax.ppermute(block, axis, [(i, i ^ bit) for i in devices])]
    unnamed x185 -> x147, local copies, waits for them, and re-layouts: 108 us -> 30.2 us
    all_to_all x16 -> x0, starting transfers between devices: 66.3 us -> none  [the longest x1 4.35 us: shards(): lax.all_to_all(projected[..., D:2 * D], 'head', split_axis=2, concat_axis...]
  transfers between devices with their start and end apart: 19 -> 69, of which waited for: 8 -> 39; matrix products, arithmetic and copies ran while one was open for 37% -> 23% of each run, Pallas kernels for 0% -> 11%
where the time goes in v1:
time: 437 us; the launch traced here: 431 us
  waiting for transfers between devices  90.6 us (21%)
  starting transfers between devices  89.1 us (20%)
  Pallas kernels  86.5 us (20%)
  local copies, waits for them, and re-layouts  61.4 us (14%)
  other arithmetic  50.2 us (11%)
  matrix products  49.6 us (11%)
    ppermute x67, waiting for transfers between devices, swap(): return lax.ppermute(block, axis, [(i, i ^ bit) for i in devices])  90.6 us
    ppermute x67, starting transfers between devices, swap(): return lax.ppermute(block, axis, [(i, i ^ bit) for i in devices])  86.4 us
    dot_general x30, matrix products, dot(): lax.dot_general(a, b, (((ca,), (cb,)), ((), ())), preferred_element_type=...  49.6 us
    pallas_call x2, Pallas kernels, attend_forward(): pl.pallas_call(kernel, out_shape=(jax.ShapeDtypeStruct((rows, wide), bf16...  45.6 us
    pallas_call x2, Pallas kernels, attend_backward(): pl.pallas_call(kernel, out_shape=(jax.ShapeDtypeStruct((feat, rows), bf16...  40.9 us
    unnamed x147, local copies, waits for them, and re-layouts  30.2 us
    concatenate x1, other arithmetic, shards(): jnp.concatenate([dot(third_low, slot_grad, 0, 0).astype(bf16), dot(follow...  13.9 us
    convert_element_type x23, other arithmetic, add(): return (a.astype(f32) + b.astype(f32)).astype(a.dtype)  9.62 us
  transfers between devices with their start and end apart: 69, of which 39 were waited for; matrix products, arithmetic and copies ran while one was open for 23% of the time, Pallas kernels for 11%

profile of v1, /device:TPU:0, one launch (start us, length us, event | category | flops | bytes accessed | tf_op | source)
XLA Modules:
  0.0 431.3 jit_solution(14235260903352297036)
XLA Ops:
  0.7 3.0 collective-permute-start
  34.0 5.5 %convert_bitcast_fusion.1 = bf16[1024,2048]{1,0:T(8,128)(2,1)S(1)} fusion(bf16[512,1536]{1,0:T(8,128)(2,1)S(1)} %copy-done.29, bf16[512,512]{1,0:T(8,128)(2,1)S(1)} %get-tuple-element.148, bf16[512,512]{1,0:T(8,128)(2,1)S(1)} %get-tuple-element.120, bf16[512,512]{1,0:T(8,128)(2,1)S(1)} %get-tuple-element.149, bf16[512,512]{1,0:T(8,128)(2,1)S(1)} %get-tuple-element.119), kind=kOutput, calls=%fused_computation.14 | convolution fusion | flops 2157969408 | bytes 7340032 | tf_op jit(solution)/shard_map/dot_general | solution.py:19
  41.8 28.2 %attend_forward.2 = (bf16[512,1024]{1,0:T(8,128)(2,1)}, bf16[512,1024]{1,0:T(8,128)(2,1)}) custom-call(bf16[512,1024]{1,0:T(8,128)(2,1)} %fusion.8.q_ref, bf16[512,2048]{1,0:T(8,128)(2,1)} %get-tuple-element.97.k_ref, bf16[512,2048]{1,0:T(8,128)(2,1)} %get-tuple-element.96.v_ref, bf16[64,2048]{1,0:T(8,128)(2,1)} %select_convert_fusion.e_ref), custom_call_target="tpu_custom_call" | custom-call | tf_op jit(solution)/shard_map/attend_forward/pallas_call | solution.py:66
  74.9 17.4 %attend_forward.3 = (bf16[512,1024]{1,0:T(8,128)(2,1)}, bf16[512,1024]{1,0:T(8,128)(2,1)}) custom-call(bf16[512,1024]{1,0:T(8,128)(2,1)} %multiply_convert_fusion.1.q_ref, bf16[512,1024]{1,0:T(8,128)(2,1)} %get-tuple-element.105.k_ref, bf16[512,1024]{1,0:T(8,128)(2,1)} %get-tuple-element.104.v_ref, bf16[64,1024]{1,0:T(8,128)(2,1)} %broadcast_in_dim.72.e_ref), custom_call_target="tpu_custom_call" | custom-call | tf_op jit(solution)/shard_map/attend_forward/pallas_call | solution.py:66
  102.2 4.2 convert_reduce_fusion
  110.2 15.0 %attend_backward.2 = (bf16[512,512]{1,0:T(8,128)(2,1)}, bf16[512,1024]{1,0:T(8,128)(2,1)}, bf16[512,1024]{1,0:T(8,128)(2,1)}) custom-call(bf16[512,1024]{1,0:T(8,128)(2,1)} %get-tuple-element.28.q_ref, bf16[512,1024]{1,0:T(8,128)(2,1)} %get-tuple-element.105.k_ref, bf16[512,1024]{1,0:T(8,128)(2,1)} %get-tuple-element.104.v_ref, ...), custom_call_target="tpu_custom_call" | custom-call | tf_op jit(solution)/shard_map/attend_backward/pallas_call | solution.py:116
  129.2 25.9 %attend_backward.3 = (bf16[512,512]{1,0:T(8,128)(2,1)}, bf16[512,2048]{1,0:T(8,128)(2,1)}, bf16[512,2048]{1,0:T(8,128)(2,1)}) custom-call(bf16[512,1024]{1,0:T(8,128)(2,1)} %get-tuple-element.30.q_ref, bf16[512,2048]{1,0:T(8,128)(2,1)} %get-tuple-element.97.k_ref, bf16[512,2048]{1,0:T(8,128)(2,1)} %get-tuple-element.96.v_ref, ...), custom_call_target="tpu_custom_call" | custom-call | tf_op jit(solution)/shard_map/attend_backward/pallas_call | solution.py:116
  192.7 13.9 %pad_maximum_fusion = bf16[5120,512]{1,0:T(8,128)(2,1)S(1)} fusion(bf16[2048,512]{1,0:T(8,128)(2,1)S(1)} %convolution_convert_fusion.1, bf16[2048,512]{1,0:T(8,128)(2,1)S(1)} %convolution_convert_fusion.2, bf16[512,512]{1,0:T(8,128)(2,1)S(1)} %convolution_convert_fusion.10, bf16[512,512]{1,0:T(8,128)(2,1)S(1)} %convolution_convert_fusion.11), kind=kLoop, calls=%fused_computation.2 | loop fusion | flops 20971520 | bytes 10485760 | tf_op jit(solution)/shard_map/concatenate | solution.py:337
  228.6 16.2 %collective-permute-done.11 = bf16[256,512]{1,0:T(8,128)(2,1)S(1)} collective-permute-done((bf16[256,512]{1,0:T(8,128)(2,1)S(1)}, bf16[256,512]{1,0:T(8,128)(2,1)S(1)}, u32[]{:S(2)}, u32[]{:S(2)}) %collective-permute-start.11) | collective-permute-done | bytes 262176 | tf_op jit(solution)/shard_map/ppermute | solution.py:131
  247.3 5.4 %collective-permute-done.37 = bf16[256,512]{1,0:T(8,128)(2,1)S(1)} collective-permute-done((bf16[256,512]{1,0:T(8,128)(2,1)S(1)}, bf16[256,512]{1,0:T(8,128)(2,1)S(1)}, u32[]{:S(2)}, u32[]{:S(2)}) %collective-permute-start.37) | collective-permute-done | bytes 262176 | tf_op jit(solution)/shard_map/ppermute | solution.py:131
  259.5 3.2 collective-permute-done.38
  273.7 3.1 collective-permute-start.22
  305.7 3.3 collective-permute-done.25
  321.7 8.1 %collective-permute-done.55 = bf16[640,512]{1,0:T(8,128)(2,1)S(1)} collective-permute-done((bf16[640,512]{1,0:T(8,128)(2,1)S(1)}, bf16[640,512]{1,0:T(8,128)(2,1)S(1)}, u32[]{:S(2)}, u32[]{:S(2)}) %collective-permute-start.55) | collective-permute-done | bytes 655392 | tf_op jit(solution)/shard_map/ppermute | solution.py:131
  332.7 4.5 %collective-permute-done.56 = bf16[320,512]{1,0:T(8,128)(2,1)S(1)} collective-permute-done((bf16[320,512]{1,0:T(8,128)(2,1)S(1)}, bf16[320,512]{1,0:T(8,128)(2,1)S(1)}, u32[]{:S(2)}, u32[]{:S(2)}) %collective-permute-start.56) | collective-permute-done | bytes 327712 | tf_op jit(solution)/shard_map/ppermute | solution.py:131
  341.0 3.4 collective-permute-done.57
  354.1 3.0 collective-permute-done.59
  366.4 5.2 %collective-permute-done.61 = bf16[320,512]{1,0:T(8,128)(2,1)S(1)} collective-permute-done((bf16[320,512]{1,0:T(8,128)(2,1)S(1)}, bf16[320,512]{1,0:T(8,128)(2,1)S(1)}, u32[]{:S(2)}, u32[]{:S(2)}) %collective-permute-start.61) | collective-permute-done | bytes 327712 | tf_op jit(solution)/shard_map/ppermute | solution.py:131
  375.7 9.3 %collective-permute-done.62 = bf16[640,512]{1,0:T(8,128)(2,1)S(1)} collective-permute-done((bf16[640,512]{1,0:T(8,128)(2,1)S(1)}, bf16[640,512]{1,0:T(8,128)(2,1)S(1)}, u32[]{:S(2)}, u32[]{:S(2)}) %collective-permute-start.62) | collective-permute-done | bytes 655392 | tf_op jit(solution)/shard_map/ppermute | solution.py:131
  398.1 3.5 copy.48
  407.1 2.9 copy.50
  412.2 3.4 constant_dynamic-update-slice_fusion
  415.6 6.9 %slice_convert_fusion = (f32[2048,512]{1,0:T(8,128)}, f32[512,2048]{0,1:T(8,128)}) fusion(bf16[5120,512]{1,0:T(8,128)(2,1)} %constant_dynamic-update-slice_fusion), kind=kLoop, calls=%fused_computation.20 | loop fusion | flops 2097152 | bytes 12582912 | tf_op jit(solution)/shard_map/convert_element_type | solution.py:430
  425.3 5.5 %copy.51 = f32[512,2048]{1,0:T(8,128)} copy(f32[512,2048]{0,1:T(8,128)} %get-tuple-element.95) | data formatting | bytes 8388608
  (509 shorter events, 227.1 us)
Async XLA Ops:
  0.7 25.6 %collective-permute-start = (bf16[512,512]{1,0:T(8,128)(2,1)}, bf16[512,512]{1,0:T(8,128)(2,1)}, u32[]{:S(2)}, u32[]{:S(2)}) collective-permute-start(bf16[512,512]{1,0:T(8,128)(2,1)} %bitcast.127), channel_id=1, source_target_pairs={{0,2},{1,3},{2,0},{3,1},{4,6},{5,7},{6,4},{7,5},{8,10},{9,11},{10,... | collective-permute-start | bytes 1572872 | tf_op jit(solution)/shard_map/ppermute | solution.py:131
  3.7 17.9 %collective-permute-start.2 = (bf16[256,512]{1,0:T(8,128)(2,1)}, bf16[256,512]{1,0:T(8,128)(2,1)}, u32[]{:S(2)}, u32[]{:S(2)}) collective-permute-start(bf16[256,512]{1,0:T(8,128)(2,1)} %bitcast.138), channel_id=1, source_target_pairs={{0,2},{1,3},{2,0},{3,1},{4,6},{5,7},{6,4},{7,5},{8,10},{9,11},{10,... | collective-permute-start | bytes 786440 | tf_op jit(solution)/shard_map/ppermute | solution.py:131
  7.1 91.3 %collective-permute-start.5 = (f32[1,512]{1,0:T(1,128)S(1)}, f32[1,512]{1,0:T(1,128)S(1)}, u32[]{:S(2)}, u32[]{:S(2)}) collective-permute-start(f32[1,512]{1,0:T(1,128)S(1)} %slice.231), channel_id=1, source_target_pairs={{0,1},{1,2},{2,3},{4,5},{5,6},{6,7},{8,9},{9,10},{10,11},{12,13},{... | collective-permute-start | bytes 6152 | tf_op jit(solution)/shard_map/ppermute | solution.py:222
  180.9 40.0 %collective-permute-start.6 = (bf16[2,512,512]{2,1,0:T(8,128)(2,1)}, bf16[2,512,512]{2,1,0:T(8,128)(2,1)}, u32[]{:S(2)}, u32[]{:S(2)}) collective-permute-start(bf16[2,512,512]{2,1,0:T(8,128)(2,1)} %dynamic-slice_bitcast_fusion), channel_id=1, source_target_pairs={{0,1},{1,0},{2,3},{3,2},{4,5},{5,4},{6,7},{7,6},{8,9},{9,8},{10,11... | collective-permute-start | bytes 3145736 | tf_op jit(solution)/shard_map/ppermute | solution.py:131
  182.9 34.9 %collective-permute-start.8 = (bf16[2,256,512]{2,1,0:T(8,128)(2,1)}, bf16[2,256,512]{2,1,0:T(8,128)(2,1)}, u32[]{:S(2)}, u32[]{:S(2)}) collective-permute-start(bf16[2,256,512]{2,1,0:T(8,128)(2,1)} %dynamic-slice_bitcast_fusion.1), channel_id=1, source_target_pairs={{0,1},{1,0},{2,3},{3,2},{4,5},{5,4},{6,7},{7,6},{8,9},{9,8},{10,11... | collective-permute-start | bytes 1572872 | tf_op jit(solution)/shard_map/ppermute | solution.py:131
  184.1 38.8 %collective-permute-start.10 = (bf16[1024,512]{1,0:T(8,128)(2,1)}, bf16[1024,512]{1,0:T(8,128)(2,1)}, u32[]{:S(2)}, u32[]{:S(2)}) collective-permute-start(bf16[1024,512]{1,0:T(8,128)(2,1)} %constant_dynamic-slice_fusion.26), channel_id=1, source_target_pairs={{0,1},{1,0},{2,3},{3,2},{4,5},{5,4},{6,7},{7,6},{8,9},{9,8},{10,11... | collective-permute-start | bytes 3145736 | tf_op jit(solution)/shard_map/ppermute | solution.py:131
  186.9 38.2 %collective-permute-start.28 = (bf16[1024,512]{1,0:T(8,128)(2,1)}, bf16[1024,512]{1,0:T(8,128)(2,1)}, u32[]{:S(2)}, u32[]{:S(2)}) collective-permute-start(bf16[1024,512]{1,0:T(8,128)(2,1)} %constant_dynamic-slice_fusion.17), channel_id=1, source_target_pairs={{0,1},{1,0},{2,3},{3,2},{4,5},{5,4},{6,7},{7,6},{8,9},{9,8},{10,11... | collective-permute-start | bytes 3145736 | tf_op jit(solution)/shard_map/ppermute | solution.py:131
  191.2 15.5 %collective-permute-start.66 = (f32[6144]{0:T(1024)S(1)}, f32[6144]{0:T(1024)S(1)}, u32[]{:S(2)}, u32[]{:S(2)}) collective-permute-start(f32[6144]{0:T(1024)S(1)} %add.613), channel_id=1, source_target_pairs={{0,4},{4,0},{8,12},{12,8},{16,20},{20,16},{24,28},{28,24},{1,5},{5... | collective-permute-start | bytes 73736 | tf_op jit(solution)/shard_map/ppermute | solution.py:131
  215.4 96.9 %collective-permute-start.46 = (bf16[2560,512]{1,0:T(8,128)(2,1)}, bf16[2560,512]{1,0:T(8,128)(2,1)}, u32[]{:S(2)}, u32[]{:S(2)}) collective-permute-start(bf16[2560,512]{1,0:T(8,128)(2,1)} %constant_dynamic-slice_fusion.8), channel_id=1, source_target_pairs={{0,1},{1,0},{2,3},{3,2},{4,5},{5,4},{6,7},{7,6},{8,9},{9,8},{10,11... | collective-permute-start | bytes 7864328 | tf_op jit(solution)/shard_map/ppermute | solution.py:131
  219.2 173.5 %collective-permute-start.9 = (bf16[256,512]{1,0:T(8,128)(2,1)S(1)}, bf16[256,512]{1,0:T(8,128)(2,1)S(1)}, u32[]{:S(2)}, u32[]{:S(2)}) collective-permute-start(bf16[256,512]{1,0:T(8,128)(2,1)S(1)} %dynamic-slice_bitcast_fusion.3), channel_id=1, source_target_pairs={{0,2},{1,3},{2,0},{3,1},{4,6},{5,7},{6,4},{7,5},{8,10},{9,11},{10,... | collective-permute-start | bytes 786440 | tf_op jit(solution)/shard_map/ppermute | solution.py:131
  222.5 171.0 %collective-permute-start.7 = (bf16[512,512]{1,0:T(8,128)(2,1)S(1)}, bf16[512,512]{1,0:T(8,128)(2,1)S(1)}, u32[]{:S(2)}, u32[]{:S(2)}) collective-permute-start(bf16[512,512]{1,0:T(8,128)(2,1)S(1)} %dynamic-slice_bitcast_fusion.2), channel_id=1, source_target_pairs={{0,2},{1,3},{2,0},{3,1},{4,6},{5,7},{6,4},{7,5},{8,10},{9,11},{10,... | collective-permute-start | bytes 1572872 | tf_op jit(solution)/shard_map/ppermute | solution.py:131
  224.6 20.8 %collective-permute-start.19 = (bf16[256,512]{1,0:T(8,128)(2,1)S(1)}, bf16[256,512]{1,0:T(8,128)(2,1)S(1)}, u32[]{:S(2)}, u32[]{:S(2)}) collective-permute-start(bf16[256,512]{1,0:T(8,128)(2,1)S(1)} %constant_dynamic-slice_fusion.21), channel_id=1, source_target_pairs={{0,4},{4,0},{8,12},{12,8},{16,20},{20,16},{24,28},{28,24},{1,5},{5... | collective-permute-start | bytes 786440 | tf_op jit(solution)/shard_map/ppermute | solution.py:131
  225.2 19.6 %collective-permute-start.11 = (bf16[256,512]{1,0:T(8,128)(2,1)S(1)}, bf16[256,512]{1,0:T(8,128)(2,1)S(1)}, u32[]{:S(2)}, u32[]{:S(2)}) collective-permute-start(bf16[256,512]{1,0:T(8,128)(2,1)S(1)} %constant_dynamic-slice_fusion.25), channel_id=1, source_target_pairs={{0,2},{1,3},{2,0},{3,1},{4,6},{5,7},{6,4},{7,5},{8,10},{9,11},{10,... | collective-permute-start | bytes 786440 | tf_op jit(solution)/shard_map/ppermute | solution.py:131
  245.4 9.1 %collective-permute-start.29 = (bf16[256,512]{1,0:T(8,128)(2,1)S(1)}, bf16[256,512]{1,0:T(8,128)(2,1)S(1)}, u32[]{:S(2)}, u32[]{:S(2)}) collective-permute-start(bf16[256,512]{1,0:T(8,128)(2,1)S(1)} %constant_dynamic-slice_fusion.16), channel_id=1, source_target_pairs={{0,2},{1,3},{2,0},{3,1},{4,6},{5,7},{6,4},{7,5},{8,10},{9,11},{10,... | collective-permute-start | bytes 786440 | tf_op jit(solution)/shard_map/ppermute | solution.py:131
  316.6 13.2 %collective-permute-start.55 = (bf16[640,512]{1,0:T(8,128)(2,1)S(1)}, bf16[640,512]{1,0:T(8,128)(2,1)S(1)}, u32[]{:S(2)}, u32[]{:S(2)}) collective-permute-start(bf16[640,512]{1,0:T(8,128)(2,1)S(1)} %constant_dynamic-slice_fusion.3), channel_id=1, source_target_pairs={{0,4},{4,0},{8,12},{12,8},{16,20},{20,16},{24,28},{28,24},{1,5},{5... | collective-permute-start | bytes 1966088 | tf_op jit(solution)/shard_map/ppermute | solution.py:131
  317.4 14.1 %collective-permute-start.47 = (bf16[640,512]{1,0:T(8,128)(2,1)S(1)}, bf16[640,512]{1,0:T(8,128)(2,1)S(1)}, u32[]{:S(2)}, u32[]{:S(2)}) collective-permute-start(bf16[640,512]{1,0:T(8,128)(2,1)S(1)} %constant_dynamic-slice_fusion.7), channel_id=1, source_target_pairs={{0,2},{1,3},{2,0},{3,1},{4,6},{5,7},{6,4},{7,5},{8,10},{9,11},{10,... | collective-permute-start | bytes 1966088 | tf_op jit(solution)/shard_map/ppermute | solution.py:131
  319.8 54.0 %collective-permute-start.18 = (bf16[256,512]{1,0:T(8,128)(2,1)S(1)}, bf16[256,512]{1,0:T(8,128)(2,1)S(1)}, u32[]{:S(2)}, u32[]{:S(2)}) collective-permute-start(bf16[256,512]{1,0:T(8,128)(2,1)S(1)} %constant_dynamic-update-slice_fusion.48), channel_id=1, source_target_pairs={{0,2},{1,3},{2,0},{3,1},{4,6},{5,7},{6,4},{7,5},{8,10},{9,11},{10,... | collective-permute-start | bytes 786440 | tf_op jit(solution)/shard_map/ppermute | solution.py:131
  362.5 9.1 %collective-permute-start.61 = (bf16[320,512]{1,0:T(8,128)(2,1)S(1)}, bf16[320,512]{1,0:T(8,128)(2,1)S(1)}, u32[]{:S(2)}, u32[]{:S(2)}) collective-permute-start(bf16[320,512]{1,0:T(8,128)(2,1)S(1)} %constant_dynamic-update-slice_fusion.6), channel_id=1, source_target_pairs={{0,2},{1,3},{2,0},{3,1},{4,6},{5,7},{6,4},{7,5},{8,10},{9,11},{10,... | collective-permute-start | bytes 983048 | tf_op jit(solution)/shard_map/ppermute | solution.py:131
  371.7 16.4 %collective-permute-start.44 = (bf16[256,512]{1,0:T(8,128)(2,1)S(1)}, bf16[256,512]{1,0:T(8,128)(2,1)S(1)}, u32[]{:S(2)}, u32[]{:S(2)}) collective-permute-start(bf16[256,512]{1,0:T(8,128)(2,1)S(1)} %constant_dynamic-update-slice_fusion.22), channel_id=1, source_target_pairs={{0,4},{4,0},{8,12},{12,8},{16,20},{20,16},{24,28},{28,24},{1,5},{5... | collective-permute-start | bytes 786440 | tf_op jit(solution)/shard_map/ppermute | solution.py:131
  372.7 12.3 %collective-permute-start.62 = (bf16[640,512]{1,0:T(8,128)(2,1)S(1)}, bf16[640,512]{1,0:T(8,128)(2,1)S(1)}, u32[]{:S(2)}, u32[]{:S(2)}) collective-permute-start(bf16[640,512]{1,0:T(8,128)(2,1)S(1)} %constant_dynamic-update-slice_fusion.4), channel_id=1, source_target_pairs={{0,4},{4,0},{8,12},{12,8},{16,20},{20,16},{24,28},{28,24},{1,5},{5... | collective-permute-start | bytes 1966088 | tf_op jit(solution)/shard_map/ppermute | solution.py:131
  373.8 11.9 %collective-permute-start.54 = (bf16[640,512]{1,0:T(8,128)(2,1)S(1)}, bf16[640,512]{1,0:T(8,128)(2,1)S(1)}, u32[]{:S(2)}, u32[]{:S(2)}) collective-permute-start(bf16[640,512]{1,0:T(8,128)(2,1)S(1)} %constant_dynamic-update-slice_fusion.12), channel_id=1, source_target_pairs={{0,2},{1,3},{2,0},{3,1},{4,6},{5,7},{6,4},{7,5},{8,10},{9,11},{10,... | collective-permute-start | bytes 1966088 | tf_op jit(solution)/shard_map/ppermute | solution.py:131
  385.7 8.8 %collective-permute-start.27 = (bf16[1024,512]{1,0:T(8,128)(2,1)S(1)}, bf16[1024,512]{1,0:T(8,128)(2,1)S(1)}, u32[]{:S(2)}, u32[]{:S(2)}) collective-permute-start(bf16[1024,512]{1,0:T(8,128)(2,1)S(1)} %get-tuple-element.113), channel_id=1, source_target_pairs={{0,1},{1,0},{2,3},{3,2},{4,5},{5,4},{6,7},{7,6},{8,9},{9,8},{10,11... | collective-permute-start | bytes 3145736 | tf_op jit(solution)/shard_map/ppermute | solution.py:131
  388.1 24.1 %collective-permute-start.63 = (bf16[2560,512]{1,0:T(8,128)(2,1)}, bf16[2560,512]{1,0:T(8,128)(2,1)}, u32[]{:S(2)}, u32[]{:S(2)}) collective-permute-start(bf16[2560,512]{1,0:T(8,128)(2,1)} %get-tuple-element.98), channel_id=1, source_target_pairs={{0,1},{1,0},{2,3},{3,2},{4,5},{5,4},{6,7},{7,6},{8,9},{9,8},{10,11... | collective-permute-start | bytes 7864328 | tf_op jit(solution)/shard_map/ppermute | solution.py:131
  392.7 8.9 %collective-permute-start.45 = (bf16[1024,512]{1,0:T(8,128)(2,1)}, bf16[1024,512]{1,0:T(8,128)(2,1)}, u32[]{:S(2)}, u32[]{:S(2)}) collective-permute-start(bf16[1024,512]{1,0:T(8,128)(2,1)} %get-tuple-element.109), channel_id=1, source_target_pairs={{0,1},{1,0},{2,3},{3,2},{4,5},{5,4},{6,7},{7,6},{8,9},{9,8},{10,11... | collective-permute-start | bytes 3145736 | tf_op jit(solution)/shard_map/ppermute | solution.py:131
  (110 other events, 737.6 us)

commit v2 on v1

v2 whole, which is shorter than its diff:
```python
import jax
import jax.numpy as jnp
from jax import lax
from jax.experimental import pallas as pl
from jax.experimental.pallas import tpu as pltpu
from jax.sharding import PartitionSpec as P

HEAD_DIM = 64
WIDE = 128
PAIR = 16
epsilon = 1e-05
masked_score = -1e30
log2_e = 1.4426950408889634
scale = HEAD_DIM**-0.5 * log2_e
largest_safe = 100.0
f32 = jnp.float32
bf16 = jnp.bfloat16
VMEM = pl.BlockSpec(memory_space=pltpu.VMEM)
ANY = pl.BlockSpec(memory_space=pl.ANY)


def dot(a, b, ca=1, cb=0):
    return lax.dot_general(a, b, (((ca,), (cb,)), ((), ())), preferred_element_type=f32)


def shape(rows, columns, dtype=bf16):
    return jax.ShapeDtypeStruct((rows, columns), dtype)


def kernel_call(body, name, outs, args, mib, specs=None, out_specs=None, scratch=()):
    return pl.pallas_call(
        body,
        out_shape=tuple(outs),
        in_specs=specs or [VMEM] * len(args),
        out_specs=tuple(out_specs or [VMEM] * len(outs)),
        scratch_shapes=list(scratch),
        compiler_params=pltpu.CompilerParams(vmem_limit_bytes=mib * 2**20),
        name=name,
    )(*args)


def span(start, size):
    return pl.ds(pl.multiple_of(start, size), size)


def in_parts(base, index, first, values):
    high = values.astype(bf16).astype(f32)
    rest = values - high
    middle = rest.astype(bf16).astype(f32)
    low = rest - middle
    base = jnp.where(index == first, high, base)
    base = jnp.where(index == first + 1, middle, base)
    return jnp.where(index == first + 2, low, base)


def feats(h):
    return span(h * HEAD_DIM, HEAD_DIM)


def with_one(q_t):
    sub = lax.broadcasted_iota(jnp.int32, q_t.shape, 0)
    return jnp.concatenate([q_t, jnp.where(sub == 0, 1.0, 0.0).astype(bf16)], axis=0)


def scores_of(q_more, k, e):
    return dot(jnp.concatenate([k, e], axis=0), q_more, 0, 0)


def weighted(p, v, e):
    return dot(jnp.concatenate([v, e[:PAIR]], axis=0), p.astype(bf16))


def plain_sums(q_more, keyed):
    totals = [None] * len(q_more)
    for k_ref, v_ref, e_ref in keyed:
        e = e_ref[...]
        for n, (h, q) in enumerate(q_more):
            p = jnp.exp2(scores_of(q, k_ref[feats(h)], e))
            part = weighted(p, v_ref[feats(h)], e)
            totals[n] = part if totals[n] is None else totals[n] + part
    return totals


def finish(h, pair, totals, tops, o_ref, qa_ref):
    outs = []
    for n, (total, top) in enumerate(zip(totals, tops)):
        weight = total[HEAD_DIM + 1 : HEAD_DIM + 2]
        outs.append(total[:HEAD_DIM] / weight)
        logs = jnp.log2(weight) if top is None else top + jnp.log2(weight)
        q = pair[n].astype(f32)
        sub = lax.broadcasted_iota(jnp.int32, q.shape, 0)
        more = in_parts(jnp.where(sub == 0, 1.0, 0.0), sub, 1, -logs)
        both = jnp.concatenate([more, q] if n else [q, more], axis=0)
        qa_ref[:, span((h + n) * WIDE, WIDE)] = both.astype(bf16).T
    o_ref[:, span(h * HEAD_DIM, WIDE)] = jnp.concatenate(outs, axis=0).astype(bf16).T


def attend_all(q_ref, keyed, first_sums, o_ref, qa_ref):
    heads = q_ref.shape[0] // HEAD_DIM
    group = 4

    def most(values):
        squares = jnp.sum(values * values, axis=0, keepdims=True)
        return jnp.max(squares, axis=1, keepdims=True)

    def step(i, carry):
        at = [i * group + n for n in range(group)]
        bound = jnp.zeros((1, 1), f32)
        for h in at:
            most_q = most(q_ref[feats(h)].astype(f32))
            for k_ref, _, _ in keyed:
                bound = jnp.maximum(bound, most_q * most(k_ref[feats(h)].astype(f32)))
        safe = bound[0, 0] < largest_safe**2

        @pl.when(safe)
        def _():
            held = [q_ref[feats(h)] for h in at]
            rest = keyed if first_sums is None else keyed[1:]
            totals = plain_sums([(h, with_one(q)) for h, q in zip(at, held)], rest)
            if first_sums is not None:
                totals = [total + first_sums[h] for total, h in zip(totals, at)]
            for n in range(0, group, 2):
                finish(at[n], held[n : n + 2], totals[n : n + 2], (None, None), o_ref, qa_ref)

        @pl.when(jnp.logical_not(safe))
        def _():
            def slow(n, c):
                held, totals, tops = [], [], []
                for m in range(2):
                    h = i * group + 2 * n + m
                    q_t = q_ref[feats(h)]
                    q = with_one(q_t)
                    top = jnp.full((1, q.shape[1]), -jnp.inf, f32)
                    for k_ref, _, e_ref in keyed:
                        s = scores_of(q, k_ref[feats(h)], e_ref[...])
                        top = jnp.maximum(top, jnp.max(s, axis=0, keepdims=True))
                    total = 0.0
                    for k_ref, v_ref, e_ref in keyed:
                        e = e_ref[...]
                        p = jnp.exp2(scores_of(q, k_ref[feats(h)], e) - top)
                        total = total + weighted(p, v_ref[feats(h)], e)
                    held.append(q_t)
                    totals.append(total)
                    tops.append(top)
                finish(i * group + 2 * n, held, totals, tops, o_ref, qa_ref)
                return c

            lax.fori_loop(0, group // 2, slow, 0)

        return carry

    lax.fori_loop(0, heads // group, step, 0)


def project_rows(weight, blocks, outs):
    w_t = weight.T
    features = w_t.shape[0] // len(outs)
    start = 0
    for block in blocks:
        size = block.shape[0]
        for n, out in enumerate(outs):
            w = w_t[n * features : (n + 1) * features]
            out[:, start : start + size] = dot(w, block[...], 1, 1).astype(bf16)
        start += size


def attend_near(tokens, other, self_qkv, extra):
    rows, d = tokens.shape
    heads = d // HEAD_DIM
    group = 4

    def body(a_ref, b_ref, w_ref, e_ref, q_ref, k_ref, v_ref, sums_ref):
        q_ref[...] = (dot(w_ref[:, :d].T, a_ref[...], 1, 1) * scale).astype(bf16)
        project_rows(w_ref[:, d:], (a_ref, b_ref), (k_ref, v_ref))

        def step(i, carry):
            at = [i * group + n for n in range(group)]
            q_more = [(h, with_one(q_ref[feats(h)])) for h in at]
            for h, total in zip(at, plain_sums(q_more, [(k_ref, v_ref, e_ref)])):
                sums_ref[h] = total
            return carry

        lax.fori_loop(0, heads // group, step, 0)

    outs = [shape(d, rows), shape(d, 2 * rows), shape(d, 2 * rows)]
    outs.append(jax.ShapeDtypeStruct((heads, HEAD_DIM + PAIR, rows), f32))
    return kernel_call(body, "attend_near", outs, (tokens, other, self_qkv, extra), 20)


def attend_far(facing, other, self_qkv, q_t, near, sums, near_extra, extra):
    rows, d = facing.shape
    heads = d // HEAD_DIM

    def body(a_ref, b_ref, w_ref, q_ref, nk, nv, s_ref, ne, e_ref, k_ref, v_ref, o_ref, qa_ref):
        project_rows(w_ref[:, d:], (a_ref, b_ref), (k_ref, v_ref))
        attend_all(q_ref, [(nk, nv, ne), (k_ref, v_ref, e_ref)], s_ref, o_ref, qa_ref)

    outs = [shape(d, 2 * rows), shape(d, 2 * rows), shape(rows, d), shape(rows, heads * WIDE)]
    args = (facing, other, self_qkv, q_t, *near, sums, near_extra, extra)
    return kernel_call(body, "attend_far", outs, args, 20)


def attend_memory(blocks, cross_kv, inputs, cross_q, extra):
    rows, d = inputs.shape
    heads = d // HEAD_DIM
    sources = sum(block.shape[0] for block in blocks)
    count = len(blocks)

    def body(*refs):
        w_ref, x_ref, wq_ref, e_ref, k_ref, v_ref, o_ref, qa_ref, q_ref = refs[count:]
        q_ref[...] = (dot(wq_ref[...].T, x_ref[...], 1, 1) * scale).astype(bf16)
        project_rows(w_ref[...], refs[:count], (k_ref, v_ref))
        attend_all(q_ref, [(k_ref, v_ref, e_ref)], None, o_ref, qa_ref)

    outs = [shape(d, sources), shape(d, sources), shape(rows, d), shape(rows, heads * WIDE)]
    args = (*blocks, cross_kv, inputs, cross_q, extra)
    scratch = [pltpu.VMEM((d, rows), bf16)]
    return kernel_call(body, "attend_memory", outs, args, 20, scratch=scratch)


def attend_backward(queries, keyed, outs, grads, first, heads, name):
    rows = queries.shape[0]
    sizes = [k.shape[1] for k, _, _ in keyed]
    group = 2
    features = heads * HEAD_DIM

    def body(q_ref, o_ref, g_ref, *refs):
        key_refs = [refs[3 * j : 3 * j + 3] for j in range(len(keyed))]
        dq_ref, dk_ref, dv_ref = refs[3 * len(keyed) :]
        lane = lax.broadcasted_iota(jnp.int32, (rows, WIDE), 1)
        low_half = lane < HEAD_DIM

        def step(i, carry):
            lanes = span((first + i * group) * HEAD_DIM, WIDE)
            g_low = g_ref[:, lanes]
            g = g_low.astype(f32)
            product = g * o_ref[:, lanes].astype(f32)
            g_t = g_low.T
            held = []
            for u in range(group):
                mine = low_half if u == 0 else jnp.logical_not(low_half)
                centre = jnp.sum(jnp.where(mine, product, 0.0), axis=1, keepdims=True)
                more = in_parts(jnp.zeros_like(g), lane, HEAD_DIM * (1 - u) + 1, -centre)
                q = q_ref[:, span((first + i * group + u) * WIDE, WIDE)]
                own = slice(u * HEAD_DIM, (u + 1) * HEAD_DIM)
                g_more = jnp.where(mine, g, more).astype(bf16)
                held.append((q, g_more, q.T[own], g_t[own]))
            totals = [None] * group
            start = 0
            for (k_ref, v_ref, e_ref), size in zip(key_refs, sizes):
                at = pl.ds(start, size)
                e = e_ref[...]
                for u, (q, g_more, q_t, g_own) in enumerate(held):
                    k = k_ref[feats(first + i * group + u)]
                    v = v_ref[feats(first + i * group + u)]
                    k_more = jnp.concatenate([e, k] if u else [k, e], axis=0)
                    v_more = jnp.concatenate([e, v] if u else [v, e], axis=0)
                    p = jnp.exp2(dot(q, k_more))
                    ds = (p * dot(g_more, v_more)).astype(bf16)
                    to = feats(i * group + u)
                    dv_ref[to, at] = dot(g_own, p.astype(bf16)).astype(bf16)
                    dk_ref[to, at] = (dot(q_t, ds) * (1.0 / log2_e)).astype(bf16)
                    part = dot(k, ds, 1, 1)
                    totals[u] = part if totals[u] is None else totals[u] + part
                start += size
            for u in range(group):
                dq_ref[feats(i * group + u)] = (totals[u] * HEAD_DIM**-0.5).astype(bf16)
            return carry

        lax.fori_loop(0, heads // group, step, 0)

    keys = sum(sizes)
    made = [shape(features, rows), shape(features, keys), shape(features, keys)]
    args = (queries, outs, grads, *[array for part in keyed for array in part])
    return kernel_call(body, name, made, args, 20)


def project_back(pairs, weights, name):
    sizes = [dks[0].shape[1] // 4 for dks, _ in pairs]
    d = weights[0].shape[0]
    rows = sum(sizes)
    args = list(weights) + [part for dks, dvs in pairs for part in (*dks, *dvs)]

    def body(*refs):
        ins = list(refs[len(weights) : len(args)])
        near, facing, other = refs[len(args) :]
        start = 0
        for (dks, dvs), size, w_ref in zip(pairs, sizes, refs):
            grads = [ins.pop(0) for _ in range(len(dks) + len(dvs))]
            for n, (out, at) in enumerate(((near, 0), (other, 0), (facing, 0), (other, rows))):
                total = None
                feature = w_ref.shape[1] - sum(ref.shape[0] for ref in grads)
                for ref in grads:
                    features = ref.shape[0]
                    w = w_ref[:, feature : feature + features]
                    part = dot(ref[:, n * size : (n + 1) * size], w, 0, 1)
                    total = part if total is None else total + part
                    feature += features
                out[pl.ds(at + start, size)] = total.astype(bf16)
            start += size

    outs = [shape(rows, d), shape(rows, d), shape(2 * rows, d)]
    return kernel_call(body, name, outs, args, 12)


def core_index():
    return lax.axis_index("head") % 2


def late_grads(third, slot_grads, hidden, ffn_grad, hidden_grad, second):
    rows, d = third.shape
    half = hidden.shape[1] // 2

    def body(t_ref, s_ref, h_ref, f_ref, g_ref, n_ref, send_ref, keep_ref):
        core = core_index()
        for side, out_ref in ((1 - core, send_ref), (core, keep_ref)):
            columns = span(side * half, half)
            out_ref[:d] = dot(t_ref[...], s_ref[side], 0, 0).astype(bf16)
            out_ref[d : d + half] = dot(h_ref[:, columns], f_ref[...], 0, 0).astype(bf16)
            out_ref[d + half :] = dot(g_ref[:, columns], n_ref[...], 0, 0).astype(bf16)

    out = shape(d + 2 * half, d)
    args = (third, slot_grads, hidden, ffn_grad, hidden_grad, second)
    return kernel_call(body, "late_grads", [out, out], args, 16)


def keyed_grad(ref, rows, blocks):
    total, start = None, 0
    for block in blocks:
        size = block.shape[0]
        part = dot(ref[rows, start : start + size], block)
        total = part if total is None else total + part
        start += size
    return total.astype(bf16)


def middle_grads(outs, out_grads, dq_t, inputs, dk_t, dv_t, blocks, context, branch, small):
    d = branch.shape[1]
    half = d // 2
    count = len(blocks)
    args = (*blocks, outs, out_grads, dq_t, inputs, dk_t, dv_t, context, branch, small)

    def body(*refs):
        o_ref, og_ref, q_ref, x_ref, k_ref, v_ref, c_ref, b_ref, s_ref, *to = refs[count:]
        core = core_index()
        for side, out_ref in ((1 - core, to[0]), (core, to[1])):
            at = span(side * half, half)
            out_ref[:half] = dot(o_ref[:, at], og_ref[...], 0, 0).astype(bf16)
            out_ref[half:d] = dot(q_ref[at], x_ref[...]).astype(bf16)
            for n, ref in enumerate((k_ref, v_ref)):

                @pl.when(side == n)
                def _():
                    memory = [block[...] for block in refs[:count]]
                    out_ref[d : 2 * d] = keyed_grad(ref, slice(None), memory)

            out_ref[2 * d : 2 * d + half] = dot(c_ref[:, at], b_ref[...], 0, 0).astype(bf16)
            rows = s_ref.shape[0]
            out_ref[2 * d + half + rows :] = jnp.zeros((half - rows, d), bf16)
            mine = jnp.where(side == 0, s_ref[...], 0.0)
            out_ref[2 * d + half : 2 * d + half + rows] = mine.astype(bf16)

    out = shape(3 * d, d)
    return kernel_call(body, "middle_grads", [out, out], args, 16)


def early_grads(dqs_t, dks_t, dvs_t, blocks):
    rows, d = blocks[0].shape
    half = d // 2
    calls = len(dqs_t)
    part_rows = d // calls
    count = len(blocks)

    def body(*refs):
        rest = refs[count:]
        core = core_index()
        for side, out_ref in ((1 - core, rest[-2]), (core, rest[-1])):
            at = span(side * half, half)
            cut = [block[:, at] for block in refs[:count]]
            for n in range(calls):
                to = pl.ds(n * part_rows, part_rows)
                out_ref[to] = dot(rest[n][...], cut[0]).astype(bf16)
                for m in (1, 2):
                    to = pl.ds(m * d + n * part_rows, part_rows)
                    out_ref[to] = keyed_grad(rest[m * calls + n], slice(None), cut)

    out = shape(3 * d, half)
    args = (*blocks, *dqs_t, *dks_t, *dvs_t)
    return kernel_call(body, "early_grads", [out, out], args, 16)


def place_in(group, head_bits):
    place = 0
    for n, bit in enumerate(group):
        if bit < head_bits:
            value = lax.axis_index("head") // (1 << bit) % 2
        else:
            value = lax.axis_index("dp") // (1 << (bit - head_bits)) % 2
        place = place + value * (1 << n)
    return place


def count_bits(axis):
    return (lax.axis_size(axis) - 1).bit_length()


def add_up(jobs, group_of, name, joint=False):
    outs, args = [], []
    head_bits = count_bits("head")
    count = len(group_of)
    for parts, group in zip(jobs, group_of):
        size = 1 << len(group)
        rows, d = parts[0].shape
        rows = rows // (size * count if joint else size)
        cut = (count, size, rows, d) if joint else (size, rows, d)
        args += [part.reshape(cut) for part in parts]
        outs += [shape(rows, d)] * size
    outs = outs * count if joint else outs

    def body(*refs):
        ins, results = list(refs[: len(args)]), list(refs[len(args) :])
        for m, group in enumerate(group_of):
            place = place_in(group, head_bits)
            if joint:
                first, *others = [ref.at[m] for ref in ins]
            else:
                first, *others = [ins.pop(0) for _ in jobs[m]]
            for n in range(1 << len(group)):
                total = first[place ^ n].astype(f32)
                for ref in others:
                    total += ref[place ^ n].astype(f32)
                results.pop(0)[...] = total.astype(bf16)

    blocks = list(kernel_call(body, name, outs, args, 8))
    return [[blocks.pop(0) for _ in range(1 << len(group))] for group in group_of]


def add_joint(jobs, group, name):
    head_bits = count_bits("head")
    size = 1 << len(group)
    rows, d = jobs[0][0].shape
    args = [part.reshape(size, rows // size, d) for parts in jobs for part in parts]

    def body(*refs):
        place = place_in(group, head_bits)
        ins, results = list(refs[: len(args)]), refs[len(args) :]
        for m, parts in enumerate(jobs):
            first, *others = [ins.pop(0) for _ in parts]
            for n in range(size):
                total = first[place ^ n].astype(f32)
                for ref in others:
                    total += ref[place ^ n].astype(f32)
                results[n][m] = total.astype(bf16)

    out = jax.ShapeDtypeStruct((len(jobs), rows // size, d), bf16)
    return list(kernel_call(body, name, [out] * size, args, 8))


def put_together(jobs, group_of, name):
    head_bits = count_bits("head")
    args = [part for parts in jobs for part in parts]
    outs = [
        jax.ShapeDtypeStruct((len(parts),) + parts[0].shape, parts[0].dtype) for parts in jobs
    ]

    def body(*refs):
        ins, results = list(refs[: len(args)]), refs[len(args) :]
        for parts, group, out in zip(jobs, group_of, results):
            place = place_in(group, head_bits)
            for n in range(len(parts)):
                out[place ^ n] = ins.pop(0)[...]

    joined = kernel_call(body, name, outs, args, 8)
    return [out.reshape(-1, out.shape[-1]) for out in joined]


def split_joint(parts, group, name):
    head_bits = count_bits("head")
    jobs, rows, d = parts[0].shape
    outs = [jax.ShapeDtypeStruct((len(parts), rows, d), bf16)] * jobs

    def body(*refs):
        place = place_in(group, head_bits)
        for m in range(jobs):
            for n in range(len(parts)):
                refs[len(parts) + m][place ^ n] = refs[n][m]

    joined = kernel_call(body, name, outs, parts, 8)
    return [out.reshape(-1, d) for out in joined]


def send_to(block, mask):
    devices = range(lax.axis_size("dp") * lax.axis_size("head"))
    return lax.ppermute(block, ("dp", "head"), [(i, i ^ mask) for i in devices])


def mask_of(group, n):
    return sum(1 << bit for m, bit in enumerate(group) if n >> m & 1)


def spread(blocks, group):
    return [blocks[0]] + [send_to(blocks[n], mask_of(group, n)) for n in range(1, len(blocks))]


def share(block, group):
    return [block] + [send_to(block, mask_of(group, n)) for n in range(1, 1 << len(group))]


def groups_of():
    bits = list(range(1, count_bits("dp") + count_bits("head")))
    plane = [1, count_bits("head")]
    rest = [bit for bit in bits if bit not in plane]
    return plane, [rest[n : n + 2] for n in range(0, len(rest), 2)]


class Sum:
    def __init__(self, send, keep, name, two):
        self.name, self.two = name, two
        self.plane, self.lines = groups_of()
        self.steps = 0
        self.jobs = [[keep, send_to(send, 1)]]

    def label(self):
        self.steps += 1
        return "%s_%d" % (self.name, self.steps)

    def tie(self, token):
        first = self.jobs[0][0]
        self.jobs[0][0] = lax.optimization_barrier((first, token))[0]

    def orders(self):
        a, b = self.plane
        return [[[a], [b]], [[b], [a]]] if self.two else [[self.plane]]

    def cut_plane(self, n):
        groups = [order[n] for order in self.orders()]
        blocks = add_up(self.jobs, groups, self.label(), self.two and n == 0)
        self.jobs = [spread(block, group) for block, group in zip(blocks, groups)]
        return blocks[0][0]

    def cut_line(self, n):
        jobs = self.jobs
        if n > 0:
            jobs = [[part.reshape(-1, part.shape[-1]) for part in jobs[0]]]
        blocks = add_joint(jobs, self.lines[n], self.label())
        self.jobs = [spread(blocks, self.lines[n])]
        return blocks[0]

    def sum_line(self):
        parts = self.jobs[0]
        whole = parts[0].shape
        flat = [part.reshape(-1, whole[-1]) for part in parts]
        total = add_up([flat], [[]], self.label())[0][0]
        self.jobs = [share(total.reshape(whole), self.lines[-1])]
        return total

    def join_line(self, n):
        if n == 0:
            self.jobs = [[part] for part in split_joint(self.jobs[0], self.lines[0], self.label())]
        else:
            self.jobs = [[put_together(self.jobs, [self.lines[n]], self.label())[0]]]
            whole = self.jobs[0][0]
            self.jobs = [share(whole.reshape(len(self.orders()), -1, whole.shape[-1]), self.lines[n - 1])]
            return whole
        groups = [order[-1] for order in self.orders()]
        token = self.jobs[0][0]
        self.jobs = [share(job[0], group) for job, group in zip(self.jobs, groups)]
        return token

    def join_plane(self, n):
        groups = [order[n] for order in self.orders()]
        wholes = put_together(self.jobs, groups, self.label())
        if n > 0:
            groups = [order[n - 1] for order in self.orders()]
            self.jobs = [share(whole, group) for whole, group in zip(wholes, groups)]
        else:
            self.own = wholes
            self.got = [send_to(whole, 1) for whole in wholes]
        return wholes[0]


def cast_outputs(total, shapes, pieces, name):
    count = len(total.own)
    part_rows = total.own[0].shape[0]

    def body(*refs):
        core = core_index()
        own, got, rest = refs[:count], refs[count : 2 * count], refs[2 * count :]
        outs, held, sems = rest[: len(shapes)], rest[len(shapes) : -1], rest[-1]
        copies = []
        for side, start, size, n, place, turned, at in pieces:
            part, row = divmod(start, part_rows)
            rows = pl.ds(row, size)
            block = jnp.where(core == side, own[part][rows], got[part][rows])
            to = pl.ds(place, size)
            if turned:
                index = (pl.ds(at, block.shape[1]), to)
                held[n][index] = block.T.astype(f32)
            else:
                index = (to, slice(None))
                held[n][index] = block.astype(f32)
            copies.append(
                pltpu.make_async_copy(
                    held[n].at[index], outs[n].at[index], sems.at[len(copies)]
                )
            )
            copies[-1].start()
        for copy in copies:
            copy.wait()

    scratch = [pltpu.VMEM(s.shape, f32) for s in shapes]
    scratch.append(pltpu.SemaphoreType.DMA((len(pieces),)))
    outs = [ANY] * len(shapes)
    args = (*total.own, *total.got)
    mib = 6 + sum(s.shape[0] * s.shape[1] * 4 for s in shapes) // 2**20
    return kernel_call(body, name, shapes, args, mib, None, outs, scratch)


def late_outputs(total, d, ff):
    half, size = ff // 2, d // 2
    pieces = []
    for side in range(2):
        for start in range(0, d, size):
            pieces.append((side, start, size, 0, side * d + start, False, 0))
        for start in range(0, half, size):
            pieces.append((side, d + start, size, 1, side * half + start, False, 0))
            pieces.append((side, d + half + start, size, 2, side * half + start, True, 0))
    shapes = [shape(2 * d, d, f32), shape(ff, d, f32), shape(d, ff, f32)]
    return cast_outputs(total, shapes, pieces, "late_outputs")


def middle_outputs(total, d, count):
    half = d // 2
    pieces = []
    for side in range(2):
        pieces.append((side, 0, half, 0, side * half, False, 0))
        pieces.append((side, half, half, 1, side * half, True, 0))
        pieces.append((side, d, half, 2, side * d, True, 0))
        pieces.append((side, d + half, half, 2, side * d + half, True, 0))
        pieces.append((side, 2 * d, half, 3, side * half, False, 0))
    pieces.append((0, 2 * d + half, count, 4, 0, False, 0))
    shapes = [shape(d, d, f32), shape(d, d, f32), shape(d, 2 * d, f32), shape(d, d, f32)]
    shapes.append(shape(count, d, f32))
    return cast_outputs(total, shapes, pieces, "middle_outputs")


def early_outputs(total, d):
    half = d // 2
    pieces = []
    for side in range(2):
        for start in range(0, 3 * d, half):
            pieces.append((side, start, half, 0, start, True, side * half))
    return cast_outputs(total, [shape(d, 3 * d, f32)], pieces, "early_outputs")[0]


def swap(block, axis, bit):
    devices = range(lax.axis_size(axis))
    return lax.ppermute(block, axis, [(i, i ^ bit) for i in devices])


def after(value, *tokens):
    return lax.optimization_barrier((value, *tokens))[0]


def shifted(block, axis, distance):
    devices = range(lax.axis_size(axis))
    route = [(i - distance, i) for i in devices if i - distance in devices]
    return lax.ppermute(block, axis, route)


def normed(values):
    centred = values - jnp.mean(values, axis=-1, keepdims=True)
    spread = jnp.mean(centred * centred, axis=-1, keepdims=True)
    inverse = lax.rsqrt(spread + epsilon)
    return centred * inverse, inverse


def norm_backward(xhat, inverse, gain, upstream):
    g = upstream * gain
    mean_g = jnp.mean(g, axis=-1, keepdims=True)
    dv = inverse * (g - mean_g - xhat * jnp.mean(g * xhat, axis=-1, keepdims=True))
    return dv, jnp.sum(upstream * xhat, axis=0), jnp.sum(upstream, axis=0)


def shards(
    tokens,
    memory,
    lengths,
    self_qkv,
    self_out,
    cross_q,
    cross_kv,
    cross_out,
    ffn_in,
    ffn_in_bias,
    ffn_out,
    ffn_out_bias,
    slot_weight,
    slot_bias,
    norm_gain,
    norm_shift,
    cotangent,
):
    tokens, memory, cotangent, length = tokens[0], memory[0], cotangent[0], lengths[0]
    rows, d = tokens.shape
    ff = ffn_in.shape[1]
    me = lax.axis_index("head")

    other_tokens, facing_tokens = swap(tokens, "head", 1), swap(tokens, "head", 2)
    local = jnp.arange(rows, dtype=jnp.int32)
    positions = me * rows + local
    live_slots = (positions < length - 1)[:, None]
    extra_index = jnp.arange(HEAD_DIM)[:, None]
    ones_rows = ((extra_index >= 1) & (extra_index <= 3)).astype(f32)

    def extra_of(members):
        key_positions = jnp.concatenate([(me ^ n) * rows + local for n in members])
        dead = (key_positions >= length)[None, :]
        return jnp.where((extra_index == 0) & dead, masked_score, ones_rows).astype(bf16)

    near_extra, far_extra = extra_of((0, 1)), extra_of((2, 3))
    cross_extra = jnp.broadcast_to(ones_rows, (HEAD_DIM, 4 * memory.shape[0])).astype(bf16)

    q_t, *near_keyed, near_sums = attend_near(tokens, other_tokens, self_qkv, near_extra)
    cotangent = after(cotangent, near_sums)
    slot_grad = jnp.where(live_slots, cotangent, 0.0).astype(bf16)
    before = shifted(slot_grad[-1:], "head", 1)
    slot_grads = jnp.stack([slot_grad, jnp.concatenate([before, slot_grad[:-1]], axis=0)])
    third_grad = dot(slot_grads[0], slot_weight[:d], 1, 1) + dot(
        slot_grads[1], slot_weight[d:], 1, 1
    )
    grad_slot_bias = jnp.sum(slot_grad.astype(f32), axis=0)

    facing_tokens = after(facing_tokens, third_grad)
    token_blocks = (tokens, other_tokens, facing_tokens, swap(facing_tokens, "head", 1))
    facing_memory = swap(after(memory, facing_tokens), "head", 2)
    *far_keyed, context, queries = attend_far(
        *token_blocks[2:], self_qkv, q_t, near_keyed, near_sums, near_extra, far_extra
    )
    facing_memory = after(facing_memory, queries)
    memory_blocks = (
        memory,
        swap(memory, "head", 1),
        facing_memory,
        swap(facing_memory, "head", 1),
    )
    first_hat, first_inv = normed(tokens.astype(f32) + dot(context, self_out))
    first_norm = first_hat * norm_gain[0] + norm_shift[0]
    first_low = first_norm.astype(bf16)

    mem_k, mem_v, cross_context, cross_queries = attend_memory(
        memory_blocks, cross_kv, first_low, cross_q, cross_extra
    )
    second_hat, second_inv = normed(first_norm + dot(cross_context, cross_out))
    second_norm = second_hat * norm_gain[1] + norm_shift[1]
    second_low = second_norm.astype(bf16)
    hidden_pre = dot(second_low, ffn_in) + ffn_in_bias.astype(f32)
    hidden, gelu_pull = jax.vjp(jax.nn.gelu, hidden_pre)
    hidden_low = hidden.astype(bf16)
    third_hat, third_inv = normed(
        second_norm + dot(hidden_low, ffn_out) + ffn_out_bias.astype(f32)
    )
    third_low = (third_hat * norm_gain[2] + norm_shift[2]).astype(bf16)
    arriving = shifted(third_low[:1], "head", -1)
    following = jnp.concatenate([third_low[1:], arriving], axis=0)
    slot_pre = (
        dot(third_low, slot_weight[:d])
        + dot(following, slot_weight[d:])
        + slot_bias.astype(f32)
    )
    slots = jnp.where(live_slots, slot_pre, 0.0).astype(bf16)

    third_in_grad, gain_late, shift_late = norm_backward(
        third_hat, third_inv, norm_gain[2], third_grad
    )
    ffn_grad = third_in_grad.astype(bf16)
    grad_out_bias = jnp.sum(ffn_grad.astype(f32), axis=0)
    hidden_grad = gelu_pull(dot(ffn_grad, ffn_out, 1, 1))[0].astype(bf16)
    grad_in_bias = jnp.sum(hidden_grad.astype(f32), axis=0)
    late_send, late_keep = late_grads(
        third_low, slot_grads, hidden_low, ffn_grad, hidden_grad, second_low
    )
    late = Sum(late_send, late_keep, "late", True)
    second_grad = third_in_grad + dot(hidden_grad, ffn_in, 1, 1)
    second_in_grad, gain_middle, shift_middle = norm_backward(
        second_hat, second_inv, norm_gain[1], second_grad
    )
    cross_branch = second_in_grad.astype(bf16)
    cross_grad = dot(cross_branch, cross_out, 1, 1).astype(bf16)
    heads = d // HEAD_DIM
    cross_dq, mem_dk, mem_dv = attend_backward(
        cross_queries,
        [(mem_k, mem_v, cross_extra)],
        cross_context,
        after(cross_grad, late_send),
        0,
        heads,
        "cross_backward",
    )
    late.tie(cross_dq)
    token = late.cut_plane(0)
    first_grad = second_in_grad + dot(cross_dq, cross_q, 0, 1)
    first_in_grad, gain_early, shift_early = norm_backward(
        first_hat, first_inv, norm_gain[0], first_grad
    )
    self_branch = first_in_grad.astype(bf16)
    self_grad = dot(self_branch, self_out, 1, 1).astype(bf16)
    small = [grad_in_bias, grad_out_bias, grad_slot_bias, gain_early, gain_middle, gain_late]
    small = jnp.concatenate(small + [shift_early, shift_middle, shift_late]).reshape(-1, d)
    count = small.shape[0]
    padded = -(-count // PAIR) * PAIR
    middle_send, middle_keep = middle_grads(
        cross_context,
        cross_branch,
        cross_dq,
        first_low,
        mem_dk,
        mem_dv,
        memory_blocks,
        context,
        self_branch,
        after(jnp.pad(small, ((0, padded - count), (0, 0))), token),
    )
    middle = Sum(middle_send, middle_keep, "middle", True)
    token = middle_send
    keyed = [(*near_keyed, near_extra), (*far_keyed, far_extra)]

    def self_backward(first, token):
        return attend_backward(
            queries, keyed, context, after(self_grad, token), first, heads // 2, "self_backward"
        )

    self_parts = [self_backward(0, token)]
    late.tie(self_parts[0][0])
    token = late.cut_plane(1)
    middle.tie(token)
    token = middle.cut_plane(0)
    self_parts.append(self_backward(heads // 2, token))
    dqs, dks, dvs = zip(*self_parts)
    late.tie(dqs[1])
    token = late.cut_line(0)
    early_send, early_keep = early_grads(
        dqs, dks, dvs, (after(tokens, token), *token_blocks[1:])
    )
    early = Sum(early_send, early_keep, "early", False)
    middle.tie(early_send)
    token = middle.cut_plane(1)
    early.tie(token)
    token = early.cut_plane(0)
    near, facing, other = project_back(
        [(dks, dvs), ((mem_dk,), (mem_dv,))],
        [after(self_qkv, token), cross_kv],
        "input_partial",
    )
    got = send_to(other, 1)
    near = near.astype(f32) + got[: near.shape[0]].astype(f32)
    lines = len(late.lines)
    late.tie(facing)
    for n in range(1, lines):
        token = late.cut_line(n)
        late.tie(token)
    token = late.sum_line()
    middle.tie(token)
    for n in range(lines):
        token = middle.cut_line(n)
        middle.tie(token)
    facing = add_up([[facing, after(got[near.shape[0] :], token)]], [[]], "facing")[0][0]
    got = send_to(facing, 2)
    early.tie(facing)
    for n in range(lines):
        token = early.cut_line(n)
        early.tie(token)
    late.tie(token)
    for n in reversed(range(lines)):
        token = late.join_line(n)
    near = near + after(got, token).astype(f32)
    size = dqs[0].shape[0]
    own_part = first_in_grad + near[:rows]
    for n, part in enumerate(dqs):
        own_part = own_part + dot(part, self_qkv[:, n * size : (n + 1) * size], 0, 1)
    token_grad = own_part
    memory_grad = near[rows:]
    order = [(middle, "sum_line", None), (late, "join_plane", 1), (early, "sum_line", None)]
    order += [(middle, "join_line", n) for n in reversed(range(lines))]
    order += [(early, "join_line", n) for n in reversed(range(lines))]
    order += [(late, "join_plane", 0), (middle, "join_plane", 1), (early, "join_plane", 0)]
    order += [(middle, "join_plane", 0)]
    for total, step, n in order:
        total.tie(token)
        token = getattr(total, step)(*([] if n is None else [n]))
    grad_self_qkv = early_outputs(early, d)
    grad_cross_out, grad_cross_q, grad_cross_kv, grad_self_out, sums = middle_outputs(
        middle, d, padded
    )
    grad_slot_weight, grad_ffn_out, grad_ffn_in = late_outputs(late, d, ff)
    small = sums.reshape(-1)
    return (
        slots[None],
        token_grad.astype(bf16)[None],
        memory_grad.astype(bf16)[None],
        grad_self_qkv,
        grad_self_out,
        grad_cross_q,
        grad_cross_kv,
        grad_cross_out,
        grad_ffn_in,
        small[:ff],
        grad_ffn_out,
        small[ff : ff + d],
        grad_slot_weight,
        small[ff + d : ff + 2 * d],
        small[ff + 2 * d : ff + 5 * d].reshape(3, d),
        small[ff + 5 * d : ff + 8 * d].reshape(3, d),
    )


def solution(mesh):
    split = P("dp", "head", None)
    return jax.shard_map(
        shards,
        mesh=mesh,
        in_specs=(split, split, P("dp")) + (P(),) * 13 + (split,),
        out_specs=(split,) * 3 + (P(),) * 13,
        check_vma=False,
    )
```

time: 437 us -> 271 us (0.62)
  local copies, waits for them, and re-layouts: 61.4 us -> 10.8 us
  other arithmetic: 50.2 us -> 5.65 us
  matrix products: 49.6 us -> 16.9 us
  waiting for transfers between devices: 90.6 us -> 64.2 us
  Pallas kernels: 86.5 us -> 80.6 us
  starting transfers between devices: 89.1 us -> 84.7 us
    ppermute x67 -> x6, waiting for transfers between devices: 90.6 us -> 0.57 us  [swap(): return lax.ppermute(block, axis, [(i, i ^ bit) for i in devices])]
    ppermute x67 -> x6, starting transfers between devices: 86.4 us -> 5.79 us  [swap(): return lax.ppermute(block, axis, [(i, i ^ bit) for i in devices])]
    ppermute x0 -> x50, starting transfers between devices: none -> 75 us  [send_to(): return lax.ppermute(block, ('dp', 'head'), [(i, i ^ mask) for i in devices])]
    ppermute x0 -> x50, waiting for transfers between devices: none -> 63.3 us  [send_to(): return lax.ppermute(block, ('dp', 'head'), [(i, i ^ mask) for i in devices])]
    dot_general x30 -> x15, matrix products: 49.6 us -> 16.9 us  [dot(): lax.dot_general(a, b, (((ca,), (cb,)), ((), ())), preferred_element_type=...]
    convert_element_type x31 -> x6, other arithmetic: 27.3 us -> 3.01 us  [the longest x1 2.04 us: shards(): self_branch = first_in_grad.astype(bf16)]
    unnamed x147 -> x122, local copies, waits for them, and re-layouts: 30.2 us -> 7.81 us
    concatenate x6 -> x0, other arithmetic: 17.4 us -> none  [the longest x1 13.9 us: shards(): jnp.concatenate([dot(third_low, slot_grad, 0, 0).astype(bf16), dot(follow...]
  transfers between devices with their start and end apart: 69 -> 58, of which waited for: 39 -> 21; matrix products, arithmetic and copies ran while one was open for 23% -> 6% of each run, Pallas kernels for 11% -> 19%
where the time goes in v2:
time: 271 us; the launch traced here: 266 us
  starting transfers between devices  84.7 us (31%)
  Pallas kernels  80.6 us (30%)
  waiting for transfers between devices  64.2 us (24%)
  matrix products  16.9 us (6%)
  local copies, waits for them, and re-layouts  10.8 us (4%)
  other arithmetic  5.65 us (2%)
  between operations  2.92 us (1%)
    pallas_call x33, Pallas kernels, kernel_call(): pl.pallas_call(body, out_shape=tuple(outs), in_specs=specs or [VMEM] * le...  80.6 us
    ppermute x50, starting transfers between devices, send_to(): return lax.ppermute(block, ('dp', 'head'), [(i, i ^ mask) for i in devices])  75 us
    ppermute x50, waiting for transfers between devices, send_to(): return lax.ppermute(block, ('dp', 'head'), [(i, i ^ mask) for i in devices])  63.3 us
    dot_general x15, matrix products, dot(): lax.dot_general(a, b, (((ca,), (cb,)), ((), ())), preferred_element_type=...  16.9 us
    unnamed x122, local copies, waits for them, and re-layouts  7.81 us
    ppermute x6, starting transfers between devices, swap(): return lax.ppermute(block, axis, [(i, i ^ bit) for i in devices])  5.79 us
  transfers between devices with their start and end apart: 58, of which 21 were waited for; matrix products, arithmetic and copies ran while one was open for 6% of the time, Pallas kernels for 19%

profile of v2, /device:TPU:0, one launch (start us, length us, event | category | flops | bytes accessed | tf_op | source)
XLA Modules:
  0.0 265.8 jit_solution(5093869775760391871)
XLA Ops:
  9.9 5.6 %attend_near.1 = (bf16[512,512]{1,0:T(8,128)(2,1)S(1)}, bf16[512,1024]{1,0:T(8,128)(2,1)S(1)}, bf16[512,1024]{1,0:T(8,128)(2,1)S(1)}, f32[8,80,512]{2,1,0:T(8,128)S(1)}) custom-call(bf16[512,512]{1,0:T(8,128)(2,1)S(1)} %bitcast.105, bf16[512,512]{1,0:T(8,128)(2,1)S(1)} %copy-done.34, bf16[512,1536]{1,0:T(8,128)(2,1)S(1)} %copy-done.2, ...), custom_call_target="tpu_custom_call" | custom-call | tf_op jit(solution)/shard_map/attend_near/pallas_call | solution.py:31
  22.2 7.6 %attend_far.1 = (bf16[512,1024]{1,0:T(8,128)(2,1)S(1)}, bf16[512,1024]{1,0:T(8,128)(2,1)S(1)}, bf16[512,512]{1,0:T(8,128)(2,1)S(1)}, bf16[512,1024]{1,0:T(8,128)(2,1)S(1)}) custom-call(bf16[512,512]{1,0:T(8,128)(2,1)} %collective-permute-done.a_ref.refs_2_, bf16[512,512]{1,0:T(8,128)(2,1)S(1)} %collective-permute-done.3.b_ref.refs_3_, ...), custom_call_target="tpu_custom_call" | custom-call | tf_op jit(solution)/shard_map/attend_far/pallas_call | solution.py:31
  32.4 7.5 %attend_memory.1 = (bf16[512,1024]{1,0:T(8,128)(2,1)S(1)}, bf16[512,1024]{1,0:T(8,128)(2,1)S(1)}, bf16[512,512]{1,0:T(8,128)(2,1)S(1)}, bf16[512,1024]{1,0:T(8,128)(2,1)S(1)}) custom-call(bf16[256,512]{1,0:T(8,128)(2,1)S(1)} %bitcast.119, bf16[256,512]{1,0:T(8,128)(2,1)} %collective-permute-done.4.refs_1_, ...), custom_call_target="tpu_custom_call" | custom-call | tf_op jit(solution)/shard_map/attend_memory/pallas_call | solution.py:31
  46.0 3.8 %convert_reduce_fusion = (f32[2048]{0:T(1024)S(1)}, bf16[512,2048]{1,0:T(8,128)(2,1)S(1)}) fusion(f32[512,2048]{1,0:T(8,128)S(1)} %get-tuple-element.287, f32[2048]{0:T(1024)S(1)} %convert_element_type.103, bf16[512,512]{1,0:T(8,128)(2,1)S(1)} %get-tuple-element.261.f_ref, bf16[2048,512]{1,0:T(8,128)(2,1)S(1)} %copy-done.55), kind=kOutput, calls=%fused_computation.9 | convolution fusion | flops 1097857024 | bytes 8929280 | tf_op jit(solution)/shard_map/dot_general | solution.py:23
  56.0 11.0 %cross_backward.1 = (bf16[512,512]{1,0:T(8,128)(2,1)S(1)}, bf16[512,1024]{1,0:T(8,128)(2,1)S(1)}, bf16[512,1024]{1,0:T(8,128)(2,1)S(1)}) custom-call(bf16[512,1024]{1,0:T(8,128)(2,1)S(1)} %get-tuple-element.142.q_ref, bf16[512,512]{1,0:T(8,128)(2,1)S(1)} %get-tuple-element.141.o_ref.refs_4_, bf16[512,512]{1,0:T(8,128)(2,1)S(1)} %convolution_convert_fusion.1.g_ref, ...), custom_call_target="tpu_custom_call" | custom-call | tf_op jit(solution)/shard_map/cross_backward/pallas_call | solution.py:31
  75.3 3.9 %middle_grads.1 = (bf16[1536,512]{1,0:T(8,128)(2,1)S(1)}, bf16[1536,512]{1,0:T(8,128)(2,1)S(1)}) custom-call(bf16[256,512]{1,0:T(8,128)(2,1)S(1)} %bitcast.120, bf16[256,512]{1,0:T(8,128)(2,1)} %collective-permute-done.4.refs_1_, bf16[256,512]{1,0:T(8,128)(2,1)S(1)} %copy-done.41, bf16[256,512]{1,0:T(8,128)(2,1)S(1)} %copy-done.43, ...), custom_call_target="tpu_custom_call" | custom-call | tf_op jit(solution)/shard_map/middle_grads/pallas_call | solution.py:31
  83.4 10.4 %self_backward.2 = (bf16[256,512]{1,0:T(8,128)(2,1)S(1)}, bf16[256,2048]{1,0:T(8,128)(2,1)S(1)}, bf16[256,2048]{1,0:T(8,128)(2,1)S(1)}) custom-call(bf16[512,1024]{1,0:T(8,128)(2,1)S(1)} %copy-done.25, bf16[512,512]{1,0:T(8,128)(2,1)S(1)} %copy-done.10, bf16[512,512]{1,0:T(8,128)(2,1)S(1)} %convolution_convert_fusion.g_ref, ...), custom_call_target="tpu_custom_call" | custom-call | tf_op jit(solution)/shard_map/self_backward/pallas_call | solution.py:31
  100.7 10.5 %self_backward.3 = (bf16[256,512]{1,0:T(8,128)(2,1)S(1)}, bf16[256,2048]{1,0:T(8,128)(2,1)S(1)}, bf16[256,2048]{1,0:T(8,128)(2,1)S(1)}) custom-call(bf16[512,1024]{1,0:T(8,128)(2,1)S(1)} %copy-done.25, bf16[512,512]{1,0:T(8,128)(2,1)S(1)} %copy-done.10, bf16[512,512]{1,0:T(8,128)(2,1)S(1)} %convolution_convert_fusion.g_ref, ...), custom_call_target="tpu_custom_call" | custom-call | tf_op jit(solution)/shard_map/self_backward/pallas_call | solution.py:31
  111.4 3.7 %early_grads.1 = (bf16[1536,256]{1,0:T(8,128)(2,1)S(1)}, bf16[1536,256]{1,0:T(8,128)(2,1)S(1)}) custom-call(bf16[512,512]{1,0:T(8,128)(2,1)S(1)} %bitcast.106, bf16[512,512]{1,0:T(8,128)(2,1)S(1)} %copy-done.35, bf16[512,512]{1,0:T(8,128)(2,1)} %collective-permute-done.a_ref.refs_2_, bf16[512,512]{1,0:T(8,128)(2,1)S(1)} %copy-done.37, ...), custom_call_target="tpu_custom_call" | custom-call | tf_op jit(solution)/shard_map/early_grads/pallas_call | solution.py:31
  117.3 9.5 %collective-permute-done.14 = bf16[384,512]{1,0:T(8,128)(2,1)S(1)} collective-permute-done((bf16[384,512]{1,0:T(8,128)(2,1)S(1)}, bf16[384,512]{1,0:T(8,128)(2,1)S(1)}, u32[]{:S(2)}, u32[]{:S(2)}) %collective-permute-start.14) | collective-permute-done | bytes 393248 | tf_op jit(solution)/shard_map/ppermute | solution.py:494
  128.7 3.5 %input_partial.1 = (bf16[768,512]{1,0:T(8,128)(2,1)S(1)}, bf16[768,512]{1,0:T(8,128)(2,1)S(1)}, bf16[1536,512]{1,0:T(8,128)(2,1)S(1)}) custom-call(bf16[512,1536]{1,0:T(8,128)(2,1)S(1)} %copy-done.4, bf16[512,1024]{1,0:T(8,128)(2,1)S(1)} %copy-done.19, bf16[256,2048]{1,0:T(8,128)(2,1)S(1)} %get-tuple-element.175.refs_6_.refs_2_, ...), custom_call_target="tpu_custom_call" | custom-call | tf_op jit(solution)/shard_map/input_partial/pallas_call | solution.py:31
  132.2 9.8 %collective-permute-start.18 = (bf16[2,80,512]{2,1,0:T(8,128)(2,1)S(1)}, bf16[2,80,512]{2,1,0:T(8,128)(2,1)S(1)}, u32[]{:S(2)}, u32[]{:S(2)}) collective-permute-start(bf16[2,80,512]{2,1,0:T(8,128)(2,1)S(1)} %get-tuple-element.193), channel_id=1, source_target_pairs={{0,8},{1,9},{2,10},{3,11},{4,12},{5,13},{6,14},{7,15},{8,0},{9,1},... | collective-permute-start | bytes 491528 | tf_op jit(solution)/shard_map/ppermute | solution.py:494
  146.2 4.1 %collective-permute-done.18 = bf16[2,80,512]{2,1,0:T(8,128)(2,1)S(1)} collective-permute-done((bf16[2,80,512]{2,1,0:T(8,128)(2,1)S(1)}, bf16[2,80,512]{2,1,0:T(8,128)(2,1)S(1)}, u32[]{:S(2)}, u32[]{:S(2)}) %collective-permute-start.18) | collective-permute-done | bytes 163872 | tf_op jit(solution)/shard_map/ppermute | solution.py:494
  152.4 5.0 %collective-permute-done.20 = bf16[2,80,512]{2,1,0:T(8,128)(2,1)S(1)} collective-permute-done((bf16[2,80,512]{2,1,0:T(8,128)(2,1)S(1)}, bf16[2,80,512]{2,1,0:T(8,128)(2,1)S(1)}, u32[]{:S(2)}, u32[]{:S(2)}) %collective-permute-start.20) | collective-permute-done | bytes 163872 | tf_op jit(solution)/shard_map/ppermute | solution.py:494
  164.8 3.5 %collective-permute-start.29 = (bf16[2,80,512]{2,1,0:T(8,128)(2,1)S(1)}, bf16[2,80,512]{2,1,0:T(8,128)(2,1)S(1)}, u32[]{:S(2)}, u32[]{:S(2)}) collective-permute-start(bf16[2,80,512]{2,1,0:T(8,128)(2,1)S(1)} %bitcast.142), channel_id=1, source_target_pairs={{0,24},{1,25},{2,26},{3,27},{4,28},{5,29},{6,30},{7,31},{8,16},{9,... | collective-permute-start | bytes 491528 | tf_op jit(solution)/shard_map/ppermute | solution.py:494
  168.9 8.5 %collective-permute-done.28.refs_2_ = bf16[2,80,512]{2,1,0:T(8,128)(2,1)S(1)} collective-permute-done((bf16[2,80,512]{2,1,0:T(8,128)(2,1)S(1)}, bf16[2,80,512]{2,1,0:T(8,128)(2,1)S(1)}, u32[]{:S(2)}, u32[]{:S(2)}) %collective-permute-start.28) | collective-permute-done | bytes 163872 | tf_op jit(solution)/shard_map/ppermute | solution.py:494
  185.3 5.5 %collective-permute-done.31 = bf16[2,48,512]{2,1,0:T(8,128)(2,1)S(1)} collective-permute-done((bf16[2,48,512]{2,1,0:T(8,128)(2,1)S(1)}, bf16[2,48,512]{2,1,0:T(8,128)(2,1)S(1)}, u32[]{:S(2)}, u32[]{:S(2)}) %collective-permute-start.31) | collective-permute-done | bytes 98336 | tf_op jit(solution)/shard_map/ppermute | solution.py:494
  202.6 3.6 %collective-permute-done.37.refs_3_ = bf16[1,96,256]{2,1,0:T(8,128)(2,1)S(1)} collective-permute-done((bf16[1,96,256]{2,1,0:T(8,128)(2,1)S(1)}, bf16[1,96,256]{2,1,0:T(8,128)(2,1)S(1)}, u32[]{:S(2)}, u32[]{:S(2)}) %collective-permute-start.37) | collective-permute-done | bytes 49184 | tf_op jit(solution)/shard_map/ppermute | solution.py:494
  206.2 4.0 %collective-permute-start.40 = (bf16[2,48,512]{2,1,0:T(8,128)(2,1)S(1)}, bf16[2,48,512]{2,1,0:T(8,128)(2,1)S(1)}, u32[]{:S(2)}, u32[]{:S(2)}) collective-permute-start(bf16[2,48,512]{2,1,0:T(8,128)(2,1)S(1)} %bitcast.154), channel_id=1, source_target_pairs={{0,24},{1,25},{2,26},{3,27},{4,28},{5,29},{6,30},{7,31},{8,16},{9,... | collective-permute-start | bytes 294920 | tf_op jit(solution)/shard_map/ppermute | solution.py:494
  220.3 3.2 %collective-permute-done.43.refs_3_ = bf16[1,96,256]{2,1,0:T(8,128)(2,1)S(1)} collective-permute-done((bf16[1,96,256]{2,1,0:T(8,128)(2,1)S(1)}, bf16[1,96,256]{2,1,0:T(8,128)(2,1)S(1)}, u32[]{:S(2)}, u32[]{:S(2)}) %collective-permute-start.43) | collective-permute-done | bytes 49184 | tf_op jit(solution)/shard_map/ppermute | solution.py:494
  223.6 3.2 %collective-permute-start.47 = (bf16[192,512]{1,0:T(8,128)(2,1)S(1)}, bf16[192,512]{1,0:T(8,128)(2,1)S(1)}, u32[]{:S(2)}, u32[]{:S(2)}) collective-permute-start(bf16[192,512]{1,0:T(8,128)(2,1)S(1)} %bitcast.174), channel_id=1, source_target_pairs={{0,2},{1,3},{2,0},{3,1},{4,6},{5,7},{6,4},{7,5},{8,10},{9,11},{10,... | collective-permute-start | bytes 589832 | tf_op jit(solution)/shard_map/ppermute | solution.py:494
  238.7 8.2 %collective-permute-done.48.refs_1_ = bf16[384,256]{1,0:T(8,128)(2,1)S(1)} collective-permute-done((bf16[384,256]{1,0:T(8,128)(2,1)S(1)}, bf16[384,256]{1,0:T(8,128)(2,1)S(1)}, u32[]{:S(2)}, u32[]{:S(2)}) %collective-permute-start.48) | collective-permute-done | bytes 196640 | tf_op jit(solution)/shard_map/ppermute | solution.py:494
  246.9 3.4 %collective-permute-done.50.refs_3_ = bf16[384,256]{1,0:T(8,128)(2,1)S(1)} collective-permute-done((bf16[384,256]{1,0:T(8,128)(2,1)S(1)}, bf16[384,256]{1,0:T(8,128)(2,1)S(1)}, u32[]{:S(2)}, u32[]{:S(2)}) %collective-permute-start.50) | collective-permute-done | bytes 196640 | tf_op jit(solution)/shard_map/ppermute | solution.py:494
  261.3 4.2 %late_outputs.1 = (f32[1024,512]{1,0:T(8,128)}, f32[2048,512]{1,0:T(8,128)}, f32[512,2048]{1,0:T(8,128)}) custom-call(bf16[1280,512]{1,0:T(8,128)(2,1)S(1)} %bitcast.114, bf16[1280,512]{1,0:T(8,128)(2,1)S(1)} %bitcast.116, bf16[1280,512]{1,0:T(8,128)(2,1)S(1)} %collective-permute-done.56.refs_2_, bf16[1280,512]{1,0:T(8,128)(2,1)S(1)} %collective-permute-done.57.refs_3_), custom_call_target="tpu_custom_call" | custom-call | tf_op jit(solution)/shard_map/late_outputs/pallas_call | solution.py:31
  (312 shorter events, 119.3 us)
Async XLA Ops:
  1.2 18.3 %collective-permute-start = (bf16[512,512]{1,0:T(8,128)(2,1)}, bf16[512,512]{1,0:T(8,128)(2,1)}, u32[]{:S(2)}, u32[]{:S(2)}) collective-permute-start(bf16[512,512]{1,0:T(8,128)(2,1)} %bitcast.104), channel_id=1, source_target_pairs={{0,2},{1,3},{2,0},{3,1},{4,6},{5,7},{6,4},{7,5},{8,10},{9,11},{10,... | collective-permute-start | bytes 1572872 | tf_op jit(solution)/shard_map/ppermute | solution.py:658
  3.7 28.0 %collective-permute-start.4 = (bf16[256,512]{1,0:T(8,128)(2,1)}, bf16[256,512]{1,0:T(8,128)(2,1)}, u32[]{:S(2)}, u32[]{:S(2)}) collective-permute-start(bf16[256,512]{1,0:T(8,128)(2,1)} %bitcast.117), channel_id=1, source_target_pairs={{0,1},{1,0},{2,3},{3,2},{4,5},{5,4},{6,7},{7,6},{8,9},{9,8},{10,11... | collective-permute-start | bytes 786440 | tf_op jit(solution)/shard_map/ppermute | solution.py:658
  54.6 17.4 %collective-permute-start.8 = (bf16[2560,512]{1,0:T(8,128)(2,1)}, bf16[2560,512]{1,0:T(8,128)(2,1)}, u32[]{:S(2)}, u32[]{:S(2)}) collective-permute-start(bf16[2560,512]{1,0:T(8,128)(2,1)} %get-tuple-element.143), channel_id=1, source_target_pairs={{0,1},{1,0},{2,3},{3,2},{4,5},{5,4},{6,7},{7,6},{8,9},{9,8},{10,11... | collective-permute-start | bytes 7864328 | tf_op jit(solution)/shard_map/ppermute | solution.py:494
  79.2 21.1 %collective-permute-start.11 = (bf16[1536,512]{1,0:T(8,128)(2,1)S(1)}, bf16[1536,512]{1,0:T(8,128)(2,1)S(1)}, u32[]{:S(2)}, u32[]{:S(2)}) collective-permute-start(bf16[1536,512]{1,0:T(8,128)(2,1)S(1)} %get-tuple-element.154), channel_id=1, source_target_pairs={{0,1},{1,0},{2,3},{3,2},{4,5},{5,4},{6,7},{7,6},{8,9},{9,8},{10,11... | collective-permute-start | bytes 4718600 | tf_op jit(solution)/shard_map/ppermute | solution.py:494
  79.4 17.0 %collective-permute-start.9 = (bf16[640,512]{1,0:T(8,128)(2,1)S(1)}, bf16[640,512]{1,0:T(8,128)(2,1)S(1)}, u32[]{:S(2)}, u32[]{:S(2)}) collective-permute-start(bf16[640,512]{1,0:T(8,128)(2,1)S(1)} %get-tuple-element.160), channel_id=1, source_target_pairs={{0,2},{1,3},{2,0},{3,1},{4,6},{5,7},{6,4},{7,5},{8,10},{9,11},{10,... | collective-permute-start | bytes 1966088 | tf_op jit(solution)/shard_map/ppermute | solution.py:494
  81.1 16.7 %collective-permute-start.10 = (bf16[640,512]{1,0:T(8,128)(2,1)S(1)}, bf16[640,512]{1,0:T(8,128)(2,1)S(1)}, u32[]{:S(2)}, u32[]{:S(2)}) collective-permute-start(bf16[640,512]{1,0:T(8,128)(2,1)S(1)} %get-tuple-element.162), channel_id=1, source_target_pairs={{0,4},{1,5},{2,6},{3,7},{4,0},{5,1},{6,2},{7,3},{8,12},{9,13},{10,... | collective-permute-start | bytes 1966088 | tf_op jit(solution)/shard_map/ppermute | solution.py:494
  98.1 13.1 %collective-permute-start.12 = (bf16[320,512]{1,0:T(8,128)(2,1)S(1)}, bf16[320,512]{1,0:T(8,128)(2,1)S(1)}, u32[]{:S(2)}, u32[]{:S(2)}) collective-permute-start(bf16[320,512]{1,0:T(8,128)(2,1)S(1)} %get-tuple-element.170), channel_id=1, source_target_pairs={{0,4},{1,5},{2,6},{3,7},{4,0},{5,1},{6,2},{7,3},{8,12},{9,13},{10,... | collective-permute-start | bytes 983048 | tf_op jit(solution)/shard_map/ppermute | solution.py:494
  115.2 13.2 %collective-permute-start.16 = (bf16[1536,256]{1,0:T(8,128)(2,1)S(1)}, bf16[1536,256]{1,0:T(8,128)(2,1)S(1)}, u32[]{:S(2)}, u32[]{:S(2)}) collective-permute-start(bf16[1536,256]{1,0:T(8,128)(2,1)S(1)} %get-tuple-element.180), channel_id=1, source_target_pairs={{0,1},{1,0},{2,3},{3,2},{4,5},{5,4},{6,7},{7,6},{8,9},{9,8},{10,11... | collective-permute-start | bytes 2359304 | tf_op jit(solution)/shard_map/ppermute | solution.py:494
  132.1 32.7 %collective-permute-start.17 = (bf16[1536,512]{1,0:T(8,128)(2,1)S(1)}, bf16[1536,512]{1,0:T(8,128)(2,1)S(1)}, u32[]{:S(2)}, u32[]{:S(2)}) collective-permute-start(bf16[1536,512]{1,0:T(8,128)(2,1)S(1)} %get-tuple-element.190), channel_id=1, source_target_pairs={{0,1},{1,0},{2,3},{3,2},{4,5},{5,4},{6,7},{7,6},{8,9},{9,8},{10,11... | collective-permute-start | bytes 4718600 | tf_op jit(solution)/shard_map/ppermute | solution.py:494
  132.2 18.1 %collective-permute-start.18 = (bf16[2,80,512]{2,1,0:T(8,128)(2,1)S(1)}, bf16[2,80,512]{2,1,0:T(8,128)(2,1)S(1)}, u32[]{:S(2)}, u32[]{:S(2)}) collective-permute-start(bf16[2,80,512]{2,1,0:T(8,128)(2,1)S(1)} %get-tuple-element.193), channel_id=1, source_target_pairs={{0,8},{1,9},{2,10},{3,11},{4,12},{5,13},{6,14},{7,15},{8,0},{9,1},... | collective-permute-start | bytes 491528 | tf_op jit(solution)/shard_map/ppermute | solution.py:494
  144.4 14.7 %collective-permute-start.21 = (bf16[192,512]{1,0:T(8,128)(2,1)S(1)}, bf16[192,512]{1,0:T(8,128)(2,1)S(1)}, u32[]{:S(2)}, u32[]{:S(2)}) collective-permute-start(bf16[192,512]{1,0:T(8,128)(2,1)S(1)} %get-tuple-element.197), channel_id=1, source_target_pairs={{0,4},{1,5},{2,6},{3,7},{4,0},{5,1},{6,2},{7,3},{8,12},{9,13},{10,... | collective-permute-start | bytes 589832 | tf_op jit(solution)/shard_map/ppermute | solution.py:494
  144.6 12.8 %collective-permute-start.20 = (bf16[2,80,512]{2,1,0:T(8,128)(2,1)S(1)}, bf16[2,80,512]{2,1,0:T(8,128)(2,1)S(1)}, u32[]{:S(2)}, u32[]{:S(2)}) collective-permute-start(bf16[2,80,512]{2,1,0:T(8,128)(2,1)S(1)} %get-tuple-element.195), channel_id=1, source_target_pairs={{0,24},{1,25},{2,26},{3,27},{4,28},{5,29},{6,30},{7,31},{8,16},{9,... | collective-permute-start | bytes 491528 | tf_op jit(solution)/shard_map/ppermute | solution.py:494
  162.6 14.9 %collective-permute-start.28 = (bf16[2,80,512]{2,1,0:T(8,128)(2,1)S(1)}, bf16[2,80,512]{2,1,0:T(8,128)(2,1)S(1)}, u32[]{:S(2)}, u32[]{:S(2)}) collective-permute-start(bf16[2,80,512]{2,1,0:T(8,128)(2,1)S(1)} %bitcast.141), channel_id=1, source_target_pairs={{0,16},{1,17},{2,18},{3,19},{4,20},{5,21},{6,22},{7,23},{8,24},{9,... | collective-permute-start | bytes 491528 | tf_op jit(solution)/shard_map/ppermute | solution.py:494
  164.8 12.6 %collective-permute-start.29 = (bf16[2,80,512]{2,1,0:T(8,128)(2,1)S(1)}, bf16[2,80,512]{2,1,0:T(8,128)(2,1)S(1)}, u32[]{:S(2)}, u32[]{:S(2)}) collective-permute-start(bf16[2,80,512]{2,1,0:T(8,128)(2,1)S(1)} %bitcast.142), channel_id=1, source_target_pairs={{0,24},{1,25},{2,26},{3,27},{4,28},{5,29},{6,30},{7,31},{8,16},{9,... | collective-permute-start | bytes 491528 | tf_op jit(solution)/shard_map/ppermute | solution.py:494
  177.5 13.3 %collective-permute-start.33 = (bf16[320,512]{1,0:T(8,128)(2,1)S(1)}, bf16[320,512]{1,0:T(8,128)(2,1)S(1)}, u32[]{:S(2)}, u32[]{:S(2)}) collective-permute-start(bf16[320,512]{1,0:T(8,128)(2,1)S(1)} %bitcast.156), channel_id=1, source_target_pairs={{0,4},{1,5},{2,6},{3,7},{4,0},{5,1},{6,2},{7,3},{8,12},{9,13},{10,... | collective-permute-start | bytes 983048 | tf_op jit(solution)/shard_map/ppermute | solution.py:494
  178.5 12.3 %collective-permute-start.34 = (bf16[320,512]{1,0:T(8,128)(2,1)S(1)}, bf16[320,512]{1,0:T(8,128)(2,1)S(1)}, u32[]{:S(2)}, u32[]{:S(2)}) collective-permute-start(bf16[320,512]{1,0:T(8,128)(2,1)S(1)} %bitcast.158), channel_id=1, source_target_pairs={{0,2},{1,3},{2,0},{3,1},{4,6},{5,7},{6,4},{7,5},{8,10},{9,11},{10,... | collective-permute-start | bytes 983048 | tf_op jit(solution)/shard_map/ppermute | solution.py:494
  191.0 36.4 %collective-permute-start.44 = (bf16[640,512]{1,0:T(8,128)(2,1)S(1)}, bf16[640,512]{1,0:T(8,128)(2,1)S(1)}, u32[]{:S(2)}, u32[]{:S(2)}) collective-permute-start(bf16[640,512]{1,0:T(8,128)(2,1)S(1)} %bitcast.132), channel_id=1, source_target_pairs={{0,2},{1,3},{2,0},{3,1},{4,6},{5,7},{6,4},{7,5},{8,10},{9,11},{10,... | collective-permute-start | bytes 1966088 | tf_op jit(solution)/shard_map/ppermute | solution.py:494
  191.4 37.5 %collective-permute-start.45 = (bf16[640,512]{1,0:T(8,128)(2,1)S(1)}, bf16[640,512]{1,0:T(8,128)(2,1)S(1)}, u32[]{:S(2)}, u32[]{:S(2)}) collective-permute-start(bf16[640,512]{1,0:T(8,128)(2,1)S(1)} %bitcast.134), channel_id=1, source_target_pairs={{0,4},{1,5},{2,6},{3,7},{4,0},{5,1},{6,2},{7,3},{8,12},{9,13},{10,... | collective-permute-start | bytes 1966088 | tf_op jit(solution)/shard_map/ppermute | solution.py:494
  195.9 40.0 %collective-permute-start.23 = (bf16[768,512]{1,0:T(8,128)(2,1)S(1)}, bf16[768,512]{1,0:T(8,128)(2,1)S(1)}, u32[]{:S(2)}, u32[]{:S(2)}) collective-permute-start(bf16[768,512]{1,0:T(8,128)(2,1)S(1)} %facing.1), channel_id=1, source_target_pairs={{0,2},{1,3},{2,0},{3,1},{4,6},{5,7},{6,4},{7,5},{8,10},{9,11},{10,... | collective-permute-start | bytes 2359304 | tf_op jit(solution)/shard_map/ppermute | solution.py:494
  230.5 20.3 %collective-permute-start.52 = (bf16[384,512]{1,0:T(8,128)(2,1)S(1)}, bf16[384,512]{1,0:T(8,128)(2,1)S(1)}, u32[]{:S(2)}, u32[]{:S(2)}) collective-permute-start(bf16[384,512]{1,0:T(8,128)(2,1)S(1)} %bitcast.144), channel_id=1, source_target_pairs={{0,2},{1,3},{2,0},{3,1},{4,6},{5,7},{6,4},{7,5},{8,10},{9,11},{10,... | collective-permute-start | bytes 1179656 | tf_op jit(solution)/shard_map/ppermute | solution.py:494
  232.6 18.3 %collective-permute-start.53 = (bf16[384,512]{1,0:T(8,128)(2,1)S(1)}, bf16[384,512]{1,0:T(8,128)(2,1)S(1)}, u32[]{:S(2)}, u32[]{:S(2)}) collective-permute-start(bf16[384,512]{1,0:T(8,128)(2,1)S(1)} %bitcast.146), channel_id=1, source_target_pairs={{0,4},{1,5},{2,6},{3,7},{4,0},{5,1},{6,2},{7,3},{8,12},{9,13},{10,... | collective-permute-start | bytes 1179656 | tf_op jit(solution)/shard_map/ppermute | solution.py:494
  234.8 12.0 %collective-permute-start.48 = (bf16[384,256]{1,0:T(8,128)(2,1)S(1)}, bf16[384,256]{1,0:T(8,128)(2,1)S(1)}, u32[]{:S(2)}, u32[]{:S(2)}) collective-permute-start(bf16[384,256]{1,0:T(8,128)(2,1)S(1)} %bitcast.121), channel_id=1, source_target_pairs={{0,2},{1,3},{2,0},{3,1},{4,6},{5,7},{6,4},{7,5},{8,10},{9,11},{10,... | collective-permute-start | bytes 589832 | tf_op jit(solution)/shard_map/ppermute | solution.py:494
  236.0 14.2 %collective-permute-start.50 = (bf16[384,256]{1,0:T(8,128)(2,1)S(1)}, bf16[384,256]{1,0:T(8,128)(2,1)S(1)}, u32[]{:S(2)}, u32[]{:S(2)}) collective-permute-start(bf16[384,256]{1,0:T(8,128)(2,1)S(1)} %bitcast.123), channel_id=1, source_target_pairs={{0,6},{1,7},{2,4},{3,5},{4,2},{5,3},{6,0},{7,1},{8,14},{9,15},{10,... | collective-permute-start | bytes 589832 | tf_op jit(solution)/shard_map/ppermute | solution.py:494
  246.8 14.4 %collective-permute-start.56 = (bf16[1280,512]{1,0:T(8,128)(2,1)S(1)}, bf16[1280,512]{1,0:T(8,128)(2,1)S(1)}, u32[]{:S(2)}, u32[]{:S(2)}) collective-permute-start(bf16[1280,512]{1,0:T(8,128)(2,1)S(1)} %bitcast.113), channel_id=1, source_target_pairs={{0,1},{1,0},{2,3},{3,2},{4,5},{5,4},{6,7},{7,6},{8,9},{9,8},{10,11... | collective-permute-start | bytes 3932168 | tf_op jit(solution)/shard_map/ppermute | solution.py:494
  (90 other events, 764.1 us)

commit v3 on v2

--- a/solution.py
+++ b/solution.py
@@ -218,7 +218,12 @@
     return kernel_call(body, "attend_memory", outs, args, 20, scratch=scratch)
 
 
-def attend_backward(queries, keyed, outs, grads, first, heads, name):
+def run(name, piece):
+    body, outs, args, mib = piece
+    return kernel_call(body, name, outs, args, mib)
+
+
+def attend_backward(queries, keyed, outs, grads, first, heads):
     rows = queries.shape[0]
     sizes = [k.shape[1] for k, _, _ in keyed]
     group = 2
@@ -272,7 +277,109 @@
     keys = sum(sizes)
     made = [shape(features, rows), shape(features, keys), shape(features, keys)]
     args = (queries, outs, grads, *[array for part in keyed for array in part])
-    return kernel_call(body, name, made, args, 20)
+    return body, made, args, 20
+
+
+def back_through_norm(x, inverse, gain, upstream):
+    g = upstream * gain
+    mean_g = jnp.mean(g, axis=1, keepdims=True)
+    mean_gx = jnp.mean(g * x, axis=1, keepdims=True)
+    sums = [jnp.sum(part, axis=0, keepdims=True) for part in (upstream * x, upstream)]
+    return inverse * (g - mean_g - x * mean_gx), *sums
+
+
+def cross_and_first_backward(attention, upstream, first_in, gain, cross_q, self_out):
+    inner, made, ins, mib = attention
+    rows, d = first_in.shape
+    args = (upstream, first_in, gain, cross_q, self_out, *ins)
+
+    def body(u_ref, f_ref, g_ref, wq_ref, wo_ref, *refs):
+        inner(*refs[: len(ins) + len(made)])
+        dq_ref = refs[len(ins)]
+        grad_ref, branch_ref, back_ref, sums_ref = refs[len(ins) + len(made) :]
+        x, inverse = normed(f_ref[...])
+        up = u_ref[...] + dot(dq_ref[...], wq_ref[...], 0, 1)
+        grad, sums_ref[0:1], sums_ref[1:2] = back_through_norm(x, inverse, g_ref[...], up)
+        grad_ref[...] = grad
+        branch = grad.astype(bf16)
+        branch_ref[...] = branch
+        back_ref[...] = dot(branch, wo_ref[...], 1, 1).astype(bf16)
+
+    outs = [*made, shape(rows, d, f32), shape(rows, d), shape(rows, d), shape(2, d, f32)]
+    return body, outs, args, mib
+
+
+def feed_forward(context, first_norm, third_grad, slot_grads, weights, biases, gains, shifts):
+    rows, d = first_norm.shape
+    cross_out, ffn_in, ffn_out = weights
+    ff = ffn_in.shape[1]
+    half = ff // 2
+    block = rows // 2
+    bend, slope = 0.044715, (2.0 / jnp.pi) ** 0.5
+    slope = float(slope)
+
+    def body(*refs):
+        c_ref, f_ref, u_ref, s_ref, wc_ref, wi_ref, wo_ref, bi_ref, bo_ref, g_ref, t_ref = refs[:11]
+        third_ref, grad_ref, branch_ref, back_ref, sums_ref, in_ref, send_ref, keep_ref = refs[11:19]
+        second_ref, hidden_ref, slope_ref, fg_ref, hg_ref = refs[19:]
+        sums_ref[...] = jnp.zeros_like(sums_ref)
+        in_ref[...] = jnp.zeros_like(in_ref)
+        def step(n, carry):
+            to = span(n * block, block)
+            x2, inverse2 = normed(f_ref[to] + dot(c_ref[to], wc_ref[...]))
+            second = x2 * g_ref[1:2] + t_ref[1:2]
+            low = second.astype(bf16)
+            second_ref[to] = low
+            total = second + bo_ref[...].astype(f32)
+            for start in range(0, ff, d):
+                part = pl.ds(start, d)
+                pre = dot(low, wi_ref[:, part]) + bi_ref[:, part].astype(f32)
+                square = pre * pre
+                tanh = jnp.tanh(slope * pre * (1.0 + bend * square))
+                hidden = (0.5 * pre * (1.0 + tanh)).astype(bf16)
+                hidden_ref[to, part] = hidden
+                steep = slope * (1.0 + 3.0 * bend * square)
+                slope_ref[:, part] = 0.5 * (1.0 + tanh) + 0.5 * pre * (1.0 - tanh * tanh) * steep
+                total = total + dot(hidden, wo_ref[part])
+            x3, inverse3 = normed(total)
+            third_ref[to] = (x3 * g_ref[2:3] + t_ref[2:3]).astype(bf16)
+            grad3, gain3, shift3 = back_through_norm(x3, inverse3, g_ref[2:3], u_ref[to])
+            ffn_grad = grad3.astype(bf16)
+            fg_ref[to] = ffn_grad
+            sums_ref[0:1] += gain3
+            sums_ref[1:2] += shift3
+            sums_ref[4:5] += jnp.sum(ffn_grad.astype(f32), axis=0, keepdims=True)
+            total = grad3
+            for start in range(0, ff, d):
+                part = pl.ds(start, d)
+                back = (dot(ffn_grad, wo_ref[part], 1, 1) * slope_ref[:, part]).astype(bf16)
+                hg_ref[to, part] = back
+                in_ref[:, part] += jnp.sum(back.astype(f32), axis=0, keepdims=True)
+                total = total + dot(back, wi_ref[:, part], 1, 1)
+            grad2, gain2, shift2 = back_through_norm(x2, inverse2, g_ref[1:2], total)
+            sums_ref[2:3] += gain2
+            sums_ref[3:4] += shift2
+            grad_ref[to] = grad2
+            branch = grad2.astype(bf16)
+            branch_ref[to] = branch
+            back_ref[to] = dot(branch, wc_ref[...], 1, 1).astype(bf16)
+            return carry
+
+        lax.fori_loop(0, rows // block, step, 0)
+        core = core_index()
+        for side, out_ref in ((1 - core, send_ref), (core, keep_ref)):
+            columns = span(side * half, half)
+            out_ref[:d] = dot(third_ref[...], s_ref[side], 0, 0).astype(bf16)
+            out_ref[d : d + half] = dot(hidden_ref[:, columns], fg_ref[...], 0, 0).astype(bf16)
+            out_ref[d + half :] = dot(hg_ref[:, columns], second_ref[...], 0, 0).astype(bf16)
+
+    outs = [shape(rows, d), shape(rows, d, f32), shape(rows, d), shape(rows, d)]
+    outs += [shape(8, d, f32), shape(1, ff, f32)] + [shape(d + 2 * half, d)] * 2
+    args = (context, first_norm, third_grad, slot_grads, *weights, *biases, gains, shifts)
+    scratch = [pltpu.VMEM((rows, d), bf16), pltpu.VMEM((rows, ff), bf16)]
+    scratch += [pltpu.VMEM((block, ff), f32), pltpu.VMEM((rows, d), bf16)]
+    scratch += [pltpu.VMEM((rows, ff), bf16)]
+    return kernel_call(body, "feed_forward", outs, args, 30, scratch=scratch)
 
 
 def project_back(pairs, weights, name):
@@ -307,23 +414,6 @@
     return lax.axis_index("head") % 2
 
 
-def late_grads(third, slot_grads, hidden, ffn_grad, hidden_grad, second):
-    rows, d = third.shape
-    half = hidden.shape[1] // 2
-
-    def body(t_ref, s_ref, h_ref, f_ref, g_ref, n_ref, send_ref, keep_ref):
-        core = core_index()
-        for side, out_ref in ((1 - core, send_ref), (core, keep_ref)):
-            columns = span(side * half, half)
-            out_ref[:d] = dot(t_ref[...], s_ref[side], 0, 0).astype(bf16)
-            out_ref[d : d + half] = dot(h_ref[:, columns], f_ref[...], 0, 0).astype(bf16)
-            out_ref[d + half :] = dot(g_ref[:, columns], n_ref[...], 0, 0).astype(bf16)
-
-    out = shape(d + 2 * half, d)
-    args = (third, slot_grads, hidden, ffn_grad, hidden_grad, second)
-    return kernel_call(body, "late_grads", [out, out], args, 16)
-
-
 def keyed_grad(ref, rows, blocks):
     total, start = None, 0
     for block in blocks:
@@ -334,15 +424,22 @@
     return total.astype(bf16)
 
 
-def middle_grads(outs, out_grads, dq_t, inputs, dk_t, dv_t, blocks, context, branch, small):
+def middle_grads(outs, out_grads, dq_t, inputs, dk_t, dv_t, blocks, context, branch, sums):
     d = branch.shape[1]
     half = d // 2
     count = len(blocks)
-    args = (*blocks, outs, out_grads, dq_t, inputs, dk_t, dv_t, context, branch, small)
+    args = (*blocks, outs, out_grads, dq_t, inputs, dk_t, dv_t, context, branch, *sums)
 
     def body(*refs):
-        o_ref, og_ref, q_ref, x_ref, k_ref, v_ref, c_ref, b_ref, s_ref, *to = refs[count:]
+        o_ref, og_ref, q_ref, x_ref, k_ref, v_ref, c_ref, b_ref, *rest = refs[count:]
+        in_bias, late, early, slot_bias, *to = rest
         core = core_index()
+        small = [in_bias[:, n : n + d] for n in range(0, in_bias.shape[1], d)]
+        small += [late[4:5], slot_bias[...], early[0:1], late[2:3], late[0:1]]
+        small += [early[1:2], late[3:4], late[1:2]]
+        rows = -(-len(small) // PAIR) * PAIR
+        small.append(jnp.zeros((rows - len(small), d), f32))
+        small = jnp.concatenate(small, axis=0)
         for side, out_ref in ((1 - core, to[0]), (core, to[1])):
             at = span(side * half, half)
             out_ref[:half] = dot(o_ref[:, at], og_ref[...], 0, 0).astype(bf16)
@@ -355,9 +452,8 @@
                     out_ref[d : 2 * d] = keyed_grad(ref, slice(None), memory)
 
             out_ref[2 * d : 2 * d + half] = dot(c_ref[:, at], b_ref[...], 0, 0).astype(bf16)
-            rows = s_ref.shape[0]
             out_ref[2 * d + half + rows :] = jnp.zeros((half - rows, d), bf16)
-            mine = jnp.where(side == 0, s_ref[...], 0.0)
+            mine = jnp.where(side == 0, small, 0.0)
             out_ref[2 * d + half : 2 * d + half + rows] = mine.astype(bf16)
 
     out = shape(3 * d, d)
@@ -367,24 +463,22 @@
 def early_grads(dqs_t, dks_t, dvs_t, blocks):
     rows, d = blocks[0].shape
     half = d // 2
-    calls = len(dqs_t)
-    part_rows = d // calls
     count = len(blocks)
 
     def body(*refs):
-        rest = refs[count:]
+        calls = [refs[count + n : count + 6 : 2] for n in range(2)]
         core = core_index()
-        for side, out_ref in ((1 - core, rest[-2]), (core, rest[-1])):
-            at = span(side * half, half)
-            cut = [block[:, at] for block in refs[:count]]
-            for n in range(calls):
-                to = pl.ds(n * part_rows, part_rows)
-                out_ref[to] = dot(rest[n][...], cut[0]).astype(bf16)
-                for m in (1, 2):
-                    to = pl.ds(m * d + n * part_rows, part_rows)
-                    out_ref[to] = keyed_grad(rest[m * calls + n], slice(None), cut)
-
-    out = shape(3 * d, half)
+        for side, out_ref in ((1 - core, refs[-2]), (core, refs[-1])):
+            for n, (q_ref, k_ref, v_ref) in enumerate(calls):
+
+                @pl.when(side == n)
+                def _():
+                    inputs = [block[...] for block in refs[:count]]
+                    out_ref[:half] = dot(q_ref[...], inputs[0]).astype(bf16)
+                    out_ref[half:d] = keyed_grad(k_ref, slice(None), inputs)
+                    out_ref[d:] = keyed_grad(v_ref, slice(None), inputs)
+
+    out = shape(3 * half, d)
     args = (*blocks, *dqs_t, *dks_t, *dvs_t)
     return kernel_call(body, "early_grads", [out, out], args, 16)
 
@@ -506,17 +600,25 @@
     return [block] + [send_to(block, mask_of(group, n)) for n in range(1, 1 << len(group))]
 
 
-def groups_of():
+def groups_of(at_once):
     bits = list(range(1, count_bits("dp") + count_bits("head")))
     plane = [1, count_bits("head")]
     rest = [bit for bit in bits if bit not in plane]
-    return plane, [rest[n : n + 2] for n in range(0, len(rest), 2)]
+    return plane, [rest[n : n + at_once] for n in range(0, len(rest), at_once)]
+
+
+AT_ONCE = (2, 1)
+ORDER = (
+    "xb", "L1", "mg", "sa", "L2", "M1", "sb", "L3", "M2", "eg", "E1", "tp",
+    "L4", "T1", "S1", "J1", "S2", "L5", "J2", "L6", "J3", "J4", "T2", "J5",
+    "J6", "L7", "Lo", "J7", "Jo",
+)
 
 
 class Sum:
-    def __init__(self, send, keep, name, two):
+    def __init__(self, send, keep, name, two, at_once):
         self.name, self.two = name, two
-        self.plane, self.lines = groups_of()
+        self.plane, self.lines = groups_of(at_once)
         self.steps = 0
         self.jobs = [[keep, send_to(send, 1)]]
 
@@ -579,22 +681,92 @@
         return wholes[0]
 
 
-def cast_outputs(total, shapes, pieces, name):
+class Joint:
+    def __init__(self, halves, whole):
+        self.jobs = [*halves.jobs, whole.jobs[0]]
+        self.plane, self.lines = halves.plane, halves.lines
+        self.name, self.steps = "joint", 0
+        self.rows = whole.jobs[0][0].shape[0]
+
+    tie, label = Sum.tie, Sum.label
+    cut_line, sum_line = Sum.cut_line, Sum.sum_line
+
+    def join_line(self, n):
+        if n > 0:
+            whole = put_together(self.jobs, [self.lines[n]], self.label())[0]
+            whole = whole.reshape(3, -1, whole.shape[-1])
+            self.jobs = [share(whole, self.lines[n - 1])]
+            return whole
+        parts = self.jobs[0]
+        head_bits = count_bits("head")
+        members = len(parts)
+        _, rows, d = parts[0].shape
+        most = members * rows
+        group = self.lines[0]
+
+        def body(*refs):
+            place = place_in(group, head_bits)
+            sorted_ref = refs[-1]
+            for m in range(3):
+                for n in range(members):
+                    at = pl.multiple_of((place ^ n) * rows, rows)
+                    to = refs[members + m] if m < 2 else sorted_ref
+                    to[pl.ds(at, rows)] = refs[n][m]
+            for m in range(2):
+                refs[members + m][most:] = sorted_ref[m * most // 2 : (m + 1) * most // 2]
+
+        outs = [shape(most + most // 2, d)] * 2
+        scratch = [pltpu.VMEM((most, d), bf16)]
+        wholes = kernel_call(body, self.label(), outs, parts, 8, scratch=scratch)
+        a, b = self.plane
+        self.orders = [[[a], [b]], [[b], [a]]]
+        self.jobs = [share(whole, order[1]) for whole, order in zip(wholes, self.orders)]
+        return wholes[0]
+
+    def join_plane(self, n):
+        wholes = put_together(self.jobs, [order[n] for order in self.orders], self.label())
+        if n > 0:
+            self.jobs = [share(w, order[0]) for w, order in zip(wholes, self.orders)]
+        else:
+            self.own = wholes
+            self.got = [send_to(whole, 1) for whole in wholes]
+        return wholes[0]
+
+    def homes(self):
+        most = self.rows
+        homes = []
+        for part in range(2):
+            for first in range(2):
+                for second in range(2):
+                    at = (2 * first + second) * (most + most // 2)
+                    row = part * 4 * most + (2 * first + second) * most
+                    homes.append((part, at, 0, row, most))
+                    x, y = (first, second) if part == 0 else (second, first)
+                    row = (x + 2 * y) * most + part * most // 2
+                    homes.append((part, at + most, 1, row, most // 2))
+        return homes
+
+
+def cast_outputs(total, homes, lengths, shapes, pieces, name):
+    args = [*total.own, *total.got]
     count = len(total.own)
-    part_rows = total.own[0].shape[0]
+    d = total.own[0].shape[1]
 
     def body(*refs):
         core = core_index()
-        own, got, rest = refs[:count], refs[count : 2 * count], refs[2 * count :]
-        outs, held, sems = rest[: len(shapes)], rest[len(shapes) : -1], rest[-1]
+        outs, rest = refs[len(args) : len(args) + len(shapes)], refs[len(args) + len(shapes) :]
+        held, ready, sems = rest[: len(shapes)], rest[len(shapes) : -1], rest[-1]
         copies = []
-        for side, start, size, n, place, turned, at in pieces:
-            part, row = divmod(start, part_rows)
-            rows = pl.ds(row, size)
-            block = jnp.where(core == side, own[part][rows], got[part][rows])
+        for part, at, which, row, size in homes:
+            mine, other = refs[part][at : at + size], refs[count + part][at : at + size]
+            to = slice(row, row + size)
+            ready[which][0, to] = jnp.where(core == 0, mine, other)
+            ready[which][1, to] = jnp.where(core == 0, other, mine)
+        for which, side, start, size, n, place, turned in pieces:
+            block = ready[which][side, start : start + size]
             to = pl.ds(place, size)
             if turned:
-                index = (pl.ds(at, block.shape[1]), to)
+                index = (slice(None), to)
                 held[n][index] = block.T.astype(f32)
             else:
                 index = (to, slice(None))
@@ -609,48 +781,44 @@
             copy.wait()
 
     scratch = [pltpu.VMEM(s.shape, f32) for s in shapes]
+    scratch += [pltpu.VMEM((2, rows, d), bf16) for rows in lengths]
     scratch.append(pltpu.SemaphoreType.DMA((len(pieces),)))
     outs = [ANY] * len(shapes)
-    args = (*total.own, *total.got)
-    mib = 6 + sum(s.shape[0] * s.shape[1] * 4 for s in shapes) // 2**20
+    mib = 14 + sum(s.shape[0] * s.shape[1] * 4 for s in shapes) // 2**20
     return kernel_call(body, name, shapes, args, mib, None, outs, scratch)
 
 
 def late_outputs(total, d, ff):
     half, size = ff // 2, d // 2
+    rows = total.own[0].shape[0]
     pieces = []
     for side in range(2):
         for start in range(0, d, size):
-            pieces.append((side, start, size, 0, side * d + start, False, 0))
+            pieces.append((0, side, start, size, 0, side * d + start, False))
         for start in range(0, half, size):
-            pieces.append((side, d + start, size, 1, side * half + start, False, 0))
-            pieces.append((side, d + half + start, size, 2, side * half + start, True, 0))
+            pieces.append((0, side, d + start, size, 1, side * half + start, False))
+            pieces.append((0, side, d + half + start, size, 2, side * half + start, True))
     shapes = [shape(2 * d, d, f32), shape(ff, d, f32), shape(d, ff, f32)]
-    return cast_outputs(total, shapes, pieces, "late_outputs")
-
-
-def middle_outputs(total, d, count):
+    homes = [(part, 0, 0, part * rows, rows) for part in range(2)]
+    return cast_outputs(total, homes, [2 * rows], shapes, pieces, "late_outputs")
+
+
+def joint_outputs(total, d, count):
     half = d // 2
     pieces = []
     for side in range(2):
-        pieces.append((side, 0, half, 0, side * half, False, 0))
-        pieces.append((side, half, half, 1, side * half, True, 0))
-        pieces.append((side, d, half, 2, side * d, True, 0))
-        pieces.append((side, d + half, half, 2, side * d + half, True, 0))
-        pieces.append((side, 2 * d, half, 3, side * half, False, 0))
-    pieces.append((0, 2 * d + half, count, 4, 0, False, 0))
+        for n in range(3):
+            pieces.append((1, side, n * half, half, 5, n * d + side * half, True))
+        pieces.append((0, side, 0, half, 0, side * half, False))
+        pieces.append((0, side, half, half, 1, side * half, True))
+        pieces.append((0, side, d, half, 2, side * d, True))
+        pieces.append((0, side, d + half, half, 2, side * d + half, True))
+        pieces.append((0, side, 2 * d, half, 3, side * half, False))
+    pieces.append((0, 0, 2 * d + half, count, 4, 0, False))
     shapes = [shape(d, d, f32), shape(d, d, f32), shape(d, 2 * d, f32), shape(d, d, f32)]
-    shapes.append(shape(count, d, f32))
-    return cast_outputs(total, shapes, pieces, "middle_outputs")
-
-
-def early_outputs(total, d):
-    half = d // 2
-    pieces = []
-    for side in range(2):
-        for start in range(0, 3 * d, half):
-            pieces.append((side, start, half, 0, start, True, side * half))
-    return cast_outputs(total, [shape(d, 3 * d, f32)], pieces, "early_outputs")[0]
+    shapes += [shape(count, d, f32), shape(d, 3 * d, f32)]
+    lengths = [3 * d, 3 * half]
+    return cast_outputs(total, total.homes(), lengths, shapes, pieces, "joint_outputs")
 
 
 def swap(block, axis, bit):
@@ -673,13 +841,6 @@
     spread = jnp.mean(centred * centred, axis=-1, keepdims=True)
     inverse = lax.rsqrt(spread + epsilon)
     return centred * inverse, inverse
-
-
-def norm_backward(xhat, inverse, gain, upstream):
-    g = upstream * gain
-    mean_g = jnp.mean(g, axis=-1, keepdims=True)
-    dv = inverse * (g - mean_g - xhat * jnp.mean(g * xhat, axis=-1, keepdims=True))
-    return dv, jnp.sum(upstream * xhat, axis=0), jnp.sum(upstream, axis=0)
 
 
 def shards(
@@ -729,7 +890,7 @@
     third_grad = dot(slot_grads[0], slot_weight[:d], 1, 1) + dot(
         slot_grads[1], slot_weight[d:], 1, 1
     )
-    grad_slot_bias = jnp.sum(slot_grad.astype(f32), axis=0)
+    grad_slot_bias = jnp.sum(slot_grad.astype(f32), axis=0, keepdims=True)
 
     facing_tokens = after(facing_tokens, third_grad)
     token_blocks = (tokens, other_tokens, facing_tokens, swap(facing_tokens, "head", 1))
@@ -744,160 +905,182 @@
         facing_memory,
         swap(facing_memory, "head", 1),
     )
-    first_hat, first_inv = normed(tokens.astype(f32) + dot(context, self_out))
-    first_norm = first_hat * norm_gain[0] + norm_shift[0]
+    first_in = tokens.astype(f32) + dot(context, self_out)
+    first_norm = normed(first_in)[0] * norm_gain[0] + norm_shift[0]
     first_low = first_norm.astype(bf16)
 
     mem_k, mem_v, cross_context, cross_queries = attend_memory(
         memory_blocks, cross_kv, first_low, cross_q, cross_extra
     )
-    second_hat, second_inv = normed(first_norm + dot(cross_context, cross_out))
-    second_norm = second_hat * norm_gain[1] + norm_shift[1]
-    second_low = second_norm.astype(bf16)
-    hidden_pre = dot(second_low, ffn_in) + ffn_in_bias.astype(f32)
-    hidden, gelu_pull = jax.vjp(jax.nn.gelu, hidden_pre)
-    hidden_low = hidden.astype(bf16)
-    third_hat, third_inv = normed(
-        second_norm + dot(hidden_low, ffn_out) + ffn_out_bias.astype(f32)
+    third_low, second_in_grad, cross_branch, cross_grad, late_sums, in_bias, *late_grads = (
+        feed_forward(
+            cross_context,
+            first_norm,
+            third_grad,
+            slot_grads,
+            (cross_out, ffn_in, ffn_out),
+            (ffn_in_bias[None], ffn_out_bias[None]),
+            norm_gain,
+            norm_shift,
+        )
     )
-    third_low = (third_hat * norm_gain[2] + norm_shift[2]).astype(bf16)
-    arriving = shifted(third_low[:1], "head", -1)
-    following = jnp.concatenate([third_low[1:], arriving], axis=0)
-    slot_pre = (
-        dot(third_low, slot_weight[:d])
-        + dot(following, slot_weight[d:])
-        + slot_bias.astype(f32)
-    )
-    slots = jnp.where(live_slots, slot_pre, 0.0).astype(bf16)
-
-    third_in_grad, gain_late, shift_late = norm_backward(
-        third_hat, third_inv, norm_gain[2], third_grad
-    )
-    ffn_grad = third_in_grad.astype(bf16)
-    grad_out_bias = jnp.sum(ffn_grad.astype(f32), axis=0)
-    hidden_grad = gelu_pull(dot(ffn_grad, ffn_out, 1, 1))[0].astype(bf16)
-    grad_in_bias = jnp.sum(hidden_grad.astype(f32), axis=0)
-    late_send, late_keep = late_grads(
-        third_low, slot_grads, hidden_low, ffn_grad, hidden_grad, second_low
-    )
-    late = Sum(late_send, late_keep, "late", True)
-    second_grad = third_in_grad + dot(hidden_grad, ffn_in, 1, 1)
-    second_in_grad, gain_middle, shift_middle = norm_backward(
-        second_hat, second_inv, norm_gain[1], second_grad
-    )
-    cross_branch = second_in_grad.astype(bf16)
-    cross_grad = dot(cross_branch, cross_out, 1, 1).astype(bf16)
+    late = Sum(*late_grads, "late", True, AT_ONCE[0])
     heads = d // HEAD_DIM
-    cross_dq, mem_dk, mem_dv = attend_backward(
-        cross_queries,
-        [(mem_k, mem_v, cross_extra)],
-        cross_context,
-        after(cross_grad, late_send),
-        0,
-        heads,
-        "cross_backward",
-    )
-    late.tie(cross_dq)
-    token = late.cut_plane(0)
-    first_grad = second_in_grad + dot(cross_dq, cross_q, 0, 1)
-    first_in_grad, gain_early, shift_early = norm_backward(
-        first_hat, first_inv, norm_gain[0], first_grad
-    )
-    self_branch = first_in_grad.astype(bf16)
-    self_grad = dot(self_branch, self_out, 1, 1).astype(bf16)
-    small = [grad_in_bias, grad_out_bias, grad_slot_bias, gain_early, gain_middle, gain_late]
-    small = jnp.concatenate(small + [shift_early, shift_middle, shift_late]).reshape(-1, d)
-    count = small.shape[0]
-    padded = -(-count // PAIR) * PAIR
-    middle_send, middle_keep = middle_grads(
-        cross_context,
-        cross_branch,
-        cross_dq,
-        first_low,
-        mem_dk,
-        mem_dv,
-        memory_blocks,
-        context,
-        self_branch,
-        after(jnp.pad(small, ((0, padded - count), (0, 0))), token),
-    )
-    middle = Sum(middle_send, middle_keep, "middle", True)
-    token = middle_send
     keyed = [(*near_keyed, near_extra), (*far_keyed, far_extra)]
-
-    def self_backward(first, token):
-        return attend_backward(
-            queries, keyed, context, after(self_grad, token), first, heads // 2, "self_backward"
+    made = {}
+    state = {"token": late_grads[0]}
+
+    def later(value):
+        return after(value, state["token"])
+
+    def cross_backward():
+        attention = attend_backward(
+            cross_queries,
+            [(mem_k, mem_v, cross_extra)],
+            cross_context,
+            later(cross_grad),
+            0,
+            heads,
         )
-
-    self_parts = [self_backward(0, token)]
-    late.tie(self_parts[0][0])
-    token = late.cut_plane(1)
-    middle.tie(token)
-    token = middle.cut_plane(0)
-    self_parts.append(self_backward(heads // 2, token))
-    dqs, dks, dvs = zip(*self_parts)
-    late.tie(dqs[1])
-    token = late.cut_line(0)
-    early_send, early_keep = early_grads(
-        dqs, dks, dvs, (after(tokens, token), *token_blocks[1:])
-    )
-    early = Sum(early_send, early_keep, "early", False)
-    middle.tie(early_send)
-    token = middle.cut_plane(1)
-    early.tie(token)
-    token = early.cut_plane(0)
-    near, facing, other = project_back(
-        [(dks, dvs), ((mem_dk,), (mem_dv,))],
-        [after(self_qkv, token), cross_kv],
-        "input_partial",
-    )
-    got = send_to(other, 1)
-    near = near.astype(f32) + got[: near.shape[0]].astype(f32)
-    lines = len(late.lines)
-    late.tie(facing)
-    for n in range(1, lines):
-        token = late.cut_line(n)
-        late.tie(token)
-    token = late.sum_line()
-    middle.tie(token)
-    for n in range(lines):
-        token = middle.cut_line(n)
-        middle.tie(token)
-    facing = add_up([[facing, after(got[near.shape[0] :], token)]], [[]], "facing")[0][0]
-    got = send_to(facing, 2)
-    early.tie(facing)
-    for n in range(lines):
-        token = early.cut_line(n)
-        early.tie(token)
-    late.tie(token)
-    for n in reversed(range(lines)):
-        token = late.join_line(n)
-    near = near + after(got, token).astype(f32)
-    size = dqs[0].shape[0]
-    own_part = first_in_grad + near[:rows]
-    for n, part in enumerate(dqs):
-        own_part = own_part + dot(part, self_qkv[:, n * size : (n + 1) * size], 0, 1)
-    token_grad = own_part
-    memory_grad = near[rows:]
-    order = [(middle, "sum_line", None), (late, "join_plane", 1), (early, "sum_line", None)]
-    order += [(middle, "join_line", n) for n in reversed(range(lines))]
-    order += [(early, "join_line", n) for n in reversed(range(lines))]
-    order += [(late, "join_plane", 0), (middle, "join_plane", 1), (early, "join_plane", 0)]
-    order += [(middle, "join_plane", 0)]
-    for total, step, n in order:
-        total.tie(token)
-        token = getattr(total, step)(*([] if n is None else [n]))
-    grad_self_qkv = early_outputs(early, d)
-    grad_cross_out, grad_cross_q, grad_cross_kv, grad_self_out, sums = middle_outputs(
-        middle, d, padded
-    )
-    grad_slot_weight, grad_ffn_out, grad_ffn_in = late_outputs(late, d, ff)
+        *made["cross"], grad, made["branch"], made["back"], made["early_sums"] = run(
+            "cross_backward",
+            cross_and_first_backward(
+                attention, second_in_grad, first_in, norm_gain[:1], cross_q, self_out
+            ),
+        )
+        made["first"] = grad
+        return grad
+
+    def middle_part():
+        cross_dq, mem_dk, mem_dv = made["cross"]
+        send, keep = middle_grads(
+            cross_context,
+            cross_branch,
+            cross_dq,
+            first_low,
+            mem_dk,
+            mem_dv,
+            memory_blocks,
+            context,
+            made["branch"],
+            (in_bias, later(late_sums), made["early_sums"], grad_slot_bias),
+        )
+        made["M"] = Sum(send, keep, "middle", True, AT_ONCE[1])
+        return send
+
+    def self_backward(n):
+        half = heads // 2
+        made["self", n] = run(
+            "self_backward",
+            attend_backward(queries, keyed, context, later(made["back"]), n * half, half),
+        )
+        return made["self", n][0]
+
+    def early_part():
+        dqs, dks, dvs = zip(made["self", 0], made["self", 1])
+        send, keep = early_grads(dqs, dks, dvs, (later(tokens), *token_blocks[1:]))
+        made["E"] = Sum(send, keep, "early", False, AT_ONCE[1])
+        return send
+
+    def partial_part():
+        _, dks, dvs = zip(made["self", 0], made["self", 1])
+        _, mem_dk, mem_dv = made["cross"]
+        near, facing, other = project_back(
+            [(dks, dvs), ((mem_dk,), (mem_dv,))], [later(self_qkv), cross_kv], "input_partial"
+        )
+        got = send_to(other, 1)
+        made["near"] = near.astype(f32) + got[: near.shape[0]].astype(f32)
+        made["facing"] = [facing, got[near.shape[0] :]]
+        return near
+
+    def send_facing():
+        facing, got = made["facing"]
+        facing = add_up([[facing, later(got)]], [[]], "facing")[0][0]
+        made["got"] = send_to(facing, 2)
+        return facing
+
+    def send_first_row():
+        first = later(third_low[:1])
+        made["arriving"] = shifted(first, "head", -1)
+        return first
+
+    def slots_done():
+        following = jnp.concatenate([third_low[1:], later(made["arriving"])], axis=0)
+        slot_pre = (
+            dot(third_low, slot_weight[:d])
+            + dot(following, slot_weight[d:])
+            + slot_bias.astype(f32)
+        )
+        made["slots"] = jnp.where(live_slots, slot_pre, 0.0).astype(bf16)
+        return made["slots"]
+
+    def inputs_done():
+        near = made["near"] + later(made["got"]).astype(f32)
+        total = made["first"] + near[:rows]
+        for n in range(2):
+            part = made["self", n][0]
+            size = part.shape[0]
+            total = total + dot(part, self_qkv[:, n * size : (n + 1) * size], 0, 1)
+        made["token_grad"] = total.astype(bf16)
+        made["memory_grad"] = near[rows:].astype(bf16)
+        return made["token_grad"]
+
+    made["L"] = late
+    def along(count, usual):
+        lines = list(range(count))
+        cuts = [lines[n : n + 1] for n in range(usual - 1)] + [lines[usual - 1 :]]
+        steps = [[("cut_line", n) for n in cut] for cut in cuts] + [[("sum_line", None)]]
+        return steps + [[("join_line", n) for n in reversed(cut)] for cut in reversed(cuts)]
+
+    across = [[("cut_plane", 0)], [("cut_plane", 1)]]
+    back = [[("join_plane", 1)], [("join_plane", 0)]]
+    late_along = along(len(late.lines), 2 // AT_ONCE[0])
+    joint_along = along(len(groups_of(AT_ONCE[1])[1]), 2 // AT_ONCE[1])
+    steps = {"L": across + late_along + back, "M": across, "E": across[:1]}
+    steps["J"] = joint_along + back
+
+    parts = {
+        "xb": cross_backward,
+        "mg": middle_part,
+        "sa": lambda: self_backward(0),
+        "sb": lambda: self_backward(1),
+        "eg": early_part,
+        "tp": partial_part,
+        "T1": send_facing,
+        "T2": inputs_done,
+        "S1": send_first_row,
+        "S2": slots_done,
+    }
+
+    def outputs(name):
+        total = made[name]
+        total.own[0] = later(total.own[0])
+        if name == "L":
+            made["late"] = late_outputs(total, d, ff)
+            return made["late"][0]
+        made["joint"] = joint_outputs(total, d, -(-(ff // d + 8) // PAIR) * PAIR)
+        return made["joint"][0]
+
+    for name in ORDER:
+        if name in parts:
+            state["token"] = parts[name]()
+        elif name[1] == "o":
+            state["token"] = outputs(name[0])
+        else:
+            if name == "J1":
+                made["J"] = Joint(made["M"], made["E"])
+            total = made[name[0]]
+            for step, n in steps[name[0]][int(name[1]) - 1]:
+                total.tie(state["token"])
+                state["token"] = getattr(total, step)(*([] if n is None else [n]))
+    grad_cross_out, grad_cross_q, grad_cross_kv, grad_self_out, sums, grad_self_qkv = made["joint"]
+    grad_slot_weight, grad_ffn_out, grad_ffn_in = made["late"]
+    token_grad, memory_grad = made["token_grad"], made["memory_grad"]
     small = sums.reshape(-1)
     return (
-        slots[None],
-        token_grad.astype(bf16)[None],
-        memory_grad.astype(bf16)[None],
+        made["slots"][None],
+        token_grad[None],
+        memory_grad[None],
         grad_self_qkv,
         grad_self_out,
         grad_cross_q,

time: 271 us -> 232 us (0.86)
  starting transfers between devices: 84.7 us -> 71.7 us
  matrix products: 16.9 us -> 4.64 us
  waiting for transfers between devices: 64.2 us -> 58.2 us
  local copies, waits for them, and re-layouts: 10.8 us -> 5.34 us
  Pallas kernels: 80.6 us -> 85.1 us
  other arithmetic: 5.65 us -> 1.43 us
    ppermute x50 -> x38, starting transfers between devices: 75 us -> 61.1 us  [send_to(): return lax.ppermute(block, ('dp', 'head'), [(i, i ^ mask) for i in devices])]
    dot_general x15 -> x7, matrix products: 16.9 us -> 4.64 us  [dot(): lax.dot_general(a, b, (((ca,), (cb,)), ((), ())), preferred_element_type=...]
    ppermute x50 -> x38, waiting for transfers between devices: 63.3 us -> 56.5 us  [send_to(): return lax.ppermute(block, ('dp', 'head'), [(i, i ^ mask) for i in devices])]
    unnamed x122 -> x40, local copies, waits for them, and re-layouts: 7.81 us -> 3.13 us
    pallas_call x33 -> x30, Pallas kernels: 80.6 us -> 85.1 us  [kernel_call(): pl.pallas_call(body, out_shape=tuple(outs), in_specs=specs or [VMEM] * le...]
  transfers between devices with their start and end apart: 58 -> 46, of which waited for: 21 -> 22; matrix products, arithmetic and copies ran while one was open for 6% -> 3% of each run, Pallas kernels for 19% -> 22%
where the time goes in v3:
time: 232 us; the launch traced here: 229 us
  Pallas kernels  85.1 us (37%)
  starting transfers between devices  71.7 us (31%)
  waiting for transfers between devices  58.2 us (25%)
  local copies, waits for them, and re-layouts  5.34 us (2%)
  matrix products  4.64 us (2%)
    pallas_call x30, Pallas kernels, kernel_call(): pl.pallas_call(body, out_shape=tuple(outs), in_specs=specs or [VMEM] * le...  85.1 us
    ppermute x38, starting transfers between devices, send_to(): return lax.ppermute(block, ('dp', 'head'), [(i, i ^ mask) for i in devices])  61.1 us
    ppermute x38, waiting for transfers between devices, send_to(): return lax.ppermute(block, ('dp', 'head'), [(i, i ^ mask) for i in devices])  56.5 us
    ppermute x6, starting transfers between devices, swap(): return lax.ppermute(block, axis, [(i, i ^ bit) for i in devices])  6.96 us
  transfers between devices with their start and end apart: 46, of which 22 were waited for; matrix products, arithmetic and copies ran while one was open for 3% of the time, Pallas kernels for 22%

profile of v3, /device:TPU:0, one launch (start us, length us, event | category | flops | bytes accessed | tf_op | source)
XLA Modules:
  0.0 228.5 jit_solution(17448469629688975437)
XLA Ops:
  7.1 5.7 %attend_near.1 = (bf16[512,512]{1,0:T(8,128)(2,1)S(1)}, bf16[512,1024]{1,0:T(8,128)(2,1)S(1)}, bf16[512,1024]{1,0:T(8,128)(2,1)S(1)}, f32[8,80,512]{2,1,0:T(8,128)S(1)}) custom-call(bf16[512,512]{1,0:T(8,128)(2,1)S(1)} %bitcast.78, bf16[512,512]{1,0:T(8,128)(2,1)S(1)} %collective-permute-done.2.b_ref.refs_1_, bf16[512,1536]{1,0:T(8,128)(2,1)S(1)} %copy-done, ...), custom_call_target="tpu_custom_call" | custom-call | tf_op jit(solution)/shard_map/attend_near/pallas_call | solution.py:31
  20.5 6.8 %attend_far.1 = (bf16[512,1024]{1,0:T(8,128)(2,1)S(1)}, bf16[512,1024]{1,0:T(8,128)(2,1)S(1)}, bf16[512,512]{1,0:T(8,128)(2,1)S(1)}, bf16[512,1024]{1,0:T(8,128)(2,1)S(1)}) custom-call(bf16[512,512]{1,0:T(8,128)(2,1)S(1)} %collective-permute-done.1.a_ref.refs_2_, bf16[512,512]{1,0:T(8,128)(2,1)S(1)} %collective-permute-done.5.b_ref.refs_3_, ...), custom_call_target="tpu_custom_call" | custom-call | tf_op jit(solution)/shard_map/attend_far/pallas_call | solution.py:31
  29.9 6.4 %attend_memory.1 = (bf16[512,1024]{1,0:T(8,128)(2,1)S(1)}, bf16[512,1024]{1,0:T(8,128)(2,1)S(1)}, bf16[512,512]{1,0:T(8,128)(2,1)S(1)}, bf16[512,1024]{1,0:T(8,128)(2,1)S(1)}) custom-call(bf16[256,512]{1,0:T(8,128)(2,1)S(1)} %bitcast.97, bf16[256,512]{1,0:T(8,128)(2,1)S(1)} %collective-permute-done.refs_1_, ...), custom_call_target="tpu_custom_call" | custom-call | tf_op jit(solution)/shard_map/attend_memory/pallas_call | solution.py:31
  36.3 12.8 %feed_forward.1 = (bf16[512,512]{1,0:T(8,128)(2,1)S(1)}, f32[512,512]{1,0:T(8,128)S(1)}, bf16[512,512]{1,0:T(8,128)(2,1)S(1)}, bf16[512,512]{1,0:T(8,128)(2,1)S(...) custom-call(bf16[512,512]{1,0:T(8,128)(2,1)S(1)} %get-tuple-element., ...), custom_call_target="tpu_custom_call" | custom-call | tf_op jit(solution)/shard_map/feed_forward/pallas_call | solution.py:31
  49.4 12.1 %cross_backward.1 = (bf16[512,512]{1,0:T(8,128)(2,1)S(1)}, bf16[512,1024]{1,0:T(8,128)(2,1)S(1)}, bf16[512,1024]{1,0:T(8,128)(2,1)S(1)}, f32[512,512]{1,0:T(8,12...) custom-call(f32[512,512]{1,0:T(8,128)S(1)} %get-tuple-element.151.u_ref, ...), custom_call_target="tpu_custom_call" | custom-call | tf_op jit(solution)/shard_map/cross_backward/pallas_call | solution.py:31
  66.7 6.4 %collective-permute-start.9 = (bf16[640,512]{1,0:T(8,128)(2,1)S(1)}, bf16[640,512]{1,0:T(8,128)(2,1)S(1)}, u32[]{:S(2)}, u32[]{:S(2)}) collective-permute-start(bf16[640,512]{1,0:T(8,128)(2,1)S(1)} %get-tuple-element.180), channel_id=1, source_target_pairs={{0,4},{1,5},{2,6},{3,7},{4,0},{5,1},{6,2},{7,3},{8,12},{9,13},{10,... | collective-permute-start | bytes 1966088 | tf_op jit(solution)/shard_map/ppermute | solution.py:588
  73.1 10.2 %self_backward.2 = (bf16[256,512]{1,0:T(8,128)(2,1)S(1)}, bf16[256,2048]{1,0:T(8,128)(2,1)S(1)}, bf16[256,2048]{1,0:T(8,128)(2,1)S(1)}) custom-call(bf16[512,1024]{1,0:T(8,128)(2,1)S(1)} %get-tuple-element.145.q_ref, bf16[512,512]{1,0:T(8,128)(2,1)S(1)} %get-tuple-element.147.refs_10_.o_ref, bf16[512,512]{1,0:T(8,128)(2,1)S(1)} %get-tuple-element.184.g_ref, ...), custom_call_target="tpu_custom_call" | custom-call | tf_op jit(solution)/shard_map/self_backward/pallas_call | solution.py:31
  83.3 4.5 %collective-permute-done.9 = bf16[640,512]{1,0:T(8,128)(2,1)S(1)} collective-permute-done((bf16[640,512]{1,0:T(8,128)(2,1)S(1)}, bf16[640,512]{1,0:T(8,128)(2,1)S(1)}, u32[]{:S(2)}, u32[]{:S(2)}) %collective-permute-start.9) | collective-permute-done | bytes 655392 | tf_op jit(solution)/shard_map/ppermute | solution.py:588
  92.7 10.3 %self_backward.3 = (bf16[256,512]{1,0:T(8,128)(2,1)S(1)}, bf16[256,2048]{1,0:T(8,128)(2,1)S(1)}, bf16[256,2048]{1,0:T(8,128)(2,1)S(1)}) custom-call(bf16[512,1024]{1,0:T(8,128)(2,1)S(1)} %get-tuple-element.145.q_ref, bf16[512,512]{1,0:T(8,128)(2,1)S(1)} %get-tuple-element.147.refs_10_.o_ref, bf16[512,512]{1,0:T(8,128)(2,1)S(1)} %get-tuple-element.184.g_ref, ...), custom_call_target="tpu_custom_call" | custom-call | tf_op jit(solution)/shard_map/self_backward/pallas_call | solution.py:31
  103.0 3.3 %collective-permute-done.11 = bf16[320,512]{1,0:T(8,128)(2,1)S(1)} collective-permute-done((bf16[320,512]{1,0:T(8,128)(2,1)S(1)}, bf16[320,512]{1,0:T(8,128)(2,1)S(1)}, u32[]{:S(2)}, u32[]{:S(2)}) %collective-permute-start.11) | collective-permute-done | bytes 327712 | tf_op jit(solution)/shard_map/ppermute | solution.py:588
  106.7 3.2 %early_grads.1 = (bf16[768,512]{1,0:T(8,128)(2,1)S(1)}, bf16[768,512]{1,0:T(8,128)(2,1)S(1)}) custom-call(bf16[512,512]{1,0:T(8,128)(2,1)S(1)} %bitcast.79, bf16[512,512]{1,0:T(8,128)(2,1)S(1)} %collective-permute-done.2.b_ref.refs_1_, bf16[512,512]{1,0:T(8,128)(2,1)S(1)} %collective-permute-done.1.a_ref.refs_2_, ...), custom_call_target="tpu_custom_call" | custom-call | tf_op jit(solution)/shard_map/early_grads/pallas_call | solution.py:31
  112.5 3.5 %input_partial.1 = (bf16[768,512]{1,0:T(8,128)(2,1)S(1)}, bf16[768,512]{1,0:T(8,128)(2,1)S(1)}, bf16[1536,512]{1,0:T(8,128)(2,1)S(1)}) custom-call(bf16[512,1536]{1,0:T(8,128)(2,1)S(1)} %copy-done.1, bf16[512,1024]{1,0:T(8,128)(2,1)S(1)} %copy-done.4, bf16[256,2048]{1,0:T(8,128)(2,1)S(1)} %get-tuple-element.197.refs_6_.refs_2_, ...), custom_call_target="tpu_custom_call" | custom-call | tf_op jit(solution)/shard_map/input_partial/pallas_call | solution.py:31
  116.2 7.8 %collective-permute-start.18 = (bf16[2,80,512]{2,1,0:T(8,128)(2,1)S(1)}, bf16[2,80,512]{2,1,0:T(8,128)(2,1)S(1)}, u32[]{:S(2)}, u32[]{:S(2)}) collective-permute-start(bf16[2,80,512]{2,1,0:T(8,128)(2,1)S(1)} %get-tuple-element.211), channel_id=1, source_target_pairs={{0,16},{1,17},{2,18},{3,19},{4,20},{5,21},{6,22},{7,23},{8,24},{9,... | collective-permute-start | bytes 491528 | tf_op jit(solution)/shard_map/ppermute | solution.py:588
  130.6 6.4 %collective-permute-done.19 = bf16[2,80,512]{2,1,0:T(8,128)(2,1)S(1)} collective-permute-done((bf16[2,80,512]{2,1,0:T(8,128)(2,1)S(1)}, bf16[2,80,512]{2,1,0:T(8,128)(2,1)S(1)}, u32[]{:S(2)}, u32[]{:S(2)}) %collective-permute-start.19) | collective-permute-done | bytes 163872 | tf_op jit(solution)/shard_map/ppermute | solution.py:588
  147.5 4.1 %collective-permute-start.29 = (bf16[2,80,512]{2,1,0:T(8,128)(2,1)S(1)}, bf16[2,80,512]{2,1,0:T(8,128)(2,1)S(1)}, u32[]{:S(2)}, u32[]{:S(2)}) collective-permute-start(bf16[2,80,512]{2,1,0:T(8,128)(2,1)S(1)} %bitcast.112), channel_id=1, source_target_pairs={{0,24},{1,25},{2,26},{3,27},{4,28},{5,29},{6,30},{7,31},{8,16},{9,... | collective-permute-start | bytes 491528 | tf_op jit(solution)/shard_map/ppermute | solution.py:588
  151.8 3.5 %collective-permute-start.30 = (bf16[3,96,512]{2,1,0:T(8,128)(2,1)S(1)}, bf16[3,96,512]{2,1,0:T(8,128)(2,1)S(1)}, u32[]{:S(2)}, u32[]{:S(2)}) collective-permute-start(bf16[3,96,512]{2,1,0:T(8,128)(2,1)S(1)} %get-tuple-element.227), channel_id=1, source_target_pairs={{0,8},{1,9},{2,10},{3,11},{4,12},{5,13},{6,14},{7,15},{8,0},{9,1},... | collective-permute-start | bytes 884744 | tf_op jit(solution)/shard_map/ppermute | solution.py:588
  157.0 3.7 %collective-permute-done.29.refs_3_ = bf16[2,80,512]{2,1,0:T(8,128)(2,1)S(1)} collective-permute-done((bf16[2,80,512]{2,1,0:T(8,128)(2,1)S(1)}, bf16[2,80,512]{2,1,0:T(8,128)(2,1)S(1)}, u32[]{:S(2)}, u32[]{:S(2)}) %collective-permute-start.29) | collective-permute-done | bytes 163872 | tf_op jit(solution)/shard_map/ppermute | solution.py:588
  164.7 3.7 %collective-permute-start.33 = (bf16[1,144,512]{2,1,0:T(8,128)(2,1)S(1)}, bf16[1,144,512]{2,1,0:T(8,128)(2,1)S(1)}, u32[]{:S(2)}, u32[]{:S(2)}) collective-permute-start(bf16[1,144,512]{2,1,0:T(8,128)(2,1)S(1)} %get-tuple-element.233), channel_id=1, source_target_pairs={{0,16},{1,17},{2,18},{3,19},{4,20},{5,21},{6,22},{7,23},{8,24},{9,... | collective-permute-start | bytes 442376 | tf_op jit(solution)/shard_map/ppermute | solution.py:588
  170.5 5.2 %collective-permute-done.32.refs_3_ = bf16[320,512]{1,0:T(8,128)(2,1)S(1)} collective-permute-done((bf16[320,512]{1,0:T(8,128)(2,1)S(1)}, bf16[320,512]{1,0:T(8,128)(2,1)S(1)}, u32[]{:S(2)}, u32[]{:S(2)}) %collective-permute-start.32) | collective-permute-done | bytes 327712 | tf_op jit(solution)/shard_map/ppermute | solution.py:588
  186.8 5.0 %collective-permute-done.35.refs_1_ = bf16[3,96,512]{2,1,0:T(8,128)(2,1)S(1)} collective-permute-done((bf16[3,96,512]{2,1,0:T(8,128)(2,1)S(1)}, bf16[3,96,512]{2,1,0:T(8,128)(2,1)S(1)}, u32[]{:S(2)}, u32[]{:S(2)}) %collective-permute-start.35) | collective-permute-done | bytes 294944 | tf_op jit(solution)/shard_map/ppermute | solution.py:588
  194.8 6.6 %collective-permute-done.36.refs_1_ = bf16[288,512]{1,0:T(8,128)(2,1)S(1)} collective-permute-done((bf16[288,512]{1,0:T(8,128)(2,1)S(1)}, bf16[288,512]{1,0:T(8,128)(2,1)S(1)}, u32[]{:S(2)}, u32[]{:S(2)}) %collective-permute-start.36) | collective-permute-done | bytes 294944 | tf_op jit(solution)/shard_map/ppermute | solution.py:588
  206.8 4.3 %late_outputs.1 = (f32[1024,512]{1,0:T(8,128)}, f32[2048,512]{1,0:T(8,128)}, f32[512,2048]{1,0:T(8,128)}) custom-call(bf16[1280,512]{1,0:T(8,128)(2,1)S(1)} %bitcast.86, bf16[1280,512]{1,0:T(8,128)(2,1)S(1)} %bitcast.88, bf16[1280,512]{1,0:T(8,128)(2,1)S(1)} %collective-permute-done.40.refs_2_, bf16[1280,512]{1,0:T(8,128)(2,1)S(1)} %collective-permute-done.41.refs_3_), custom_call_target="tpu_custom_call" | custom-call | tf_op jit(solution)/shard_map/late_outputs/pallas_call | solution.py:31
  211.1 6.6 %collective-permute-done.42.refs_1_ = bf16[576,512]{1,0:T(8,128)(2,1)S(1)} collective-permute-done((bf16[576,512]{1,0:T(8,128)(2,1)S(1)}, bf16[576,512]{1,0:T(8,128)(2,1)S(1)}, u32[]{:S(2)}, u32[]{:S(2)}) %collective-permute-start.42) | collective-permute-done | bytes 589856 | tf_op jit(solution)/shard_map/ppermute | solution.py:588
  223.0 3.6 %joint_outputs.1 = (f32[512,512]{1,0:T(8,128)}, f32[512,512]{1,0:T(8,128)}, f32[512,1024]{1,0:T(8,128)}, f32[512,512]{1,0:T(8,128)}, f32[16,512]{1,0:T(8,128)S(1)}, /*index=5*/f32[512,1536]{1,0:T(8,128)}) custom-call(bf16[1152,512]{1,0:T(8,128)(2,1)S(1)} %bitcast.92, bf16[1152,512]{1,0:T(8,128)(2,1)S(1)} %bitcast.94, ...), custom_call_target="tpu_custom_call" | custom-call | tf_op jit(solution)/shard_map/joint_outputs/pallas_call | solution.py:31
  (176 shorter events, 80.7 us)
Async XLA Ops:
  1.2 15.3 %collective-permute-start.1 = (bf16[512,512]{1,0:T(8,128)(2,1)}, bf16[512,512]{1,0:T(8,128)(2,1)S(1)}, u32[]{:S(2)}, u32[]{:S(2)}) collective-permute-start(bf16[512,512]{1,0:T(8,128)(2,1)} %bitcast.77), channel_id=1, source_target_pairs={{0,2},{1,3},{2,0},{3,1},{4,6},{5,7},{6,4},{7,5},{8,10},{9,11},{10,... | collective-permute-start | bytes 1572872 | tf_op jit(solution)/shard_map/ppermute | solution.py:826
  65.2 22.9 %collective-permute-start.10 = (bf16[1536,512]{1,0:T(8,128)(2,1)S(1)}, bf16[1536,512]{1,0:T(8,128)(2,1)S(1)}, u32[]{:S(2)}, u32[]{:S(2)}) collective-permute-start(bf16[1536,512]{1,0:T(8,128)(2,1)S(1)} %get-tuple-element.172), channel_id=1, source_target_pairs={{0,1},{1,0},{2,3},{3,2},{4,5},{5,4},{6,7},{7,6},{8,9},{9,8},{10,11... | collective-permute-start | bytes 4718600 | tf_op jit(solution)/shard_map/ppermute | solution.py:588
  65.6 17.7 %collective-permute-start.8 = (bf16[640,512]{1,0:T(8,128)(2,1)S(1)}, bf16[640,512]{1,0:T(8,128)(2,1)S(1)}, u32[]{:S(2)}, u32[]{:S(2)}) collective-permute-start(bf16[640,512]{1,0:T(8,128)(2,1)S(1)} %get-tuple-element.178), channel_id=1, source_target_pairs={{0,2},{1,3},{2,0},{3,1},{4,6},{5,7},{6,4},{7,5},{8,10},{9,11},{10,... | collective-permute-start | bytes 1966088 | tf_op jit(solution)/shard_map/ppermute | solution.py:588
  66.7 21.1 %collective-permute-start.9 = (bf16[640,512]{1,0:T(8,128)(2,1)S(1)}, bf16[640,512]{1,0:T(8,128)(2,1)S(1)}, u32[]{:S(2)}, u32[]{:S(2)}) collective-permute-start(bf16[640,512]{1,0:T(8,128)(2,1)S(1)} %get-tuple-element.180), channel_id=1, source_target_pairs={{0,4},{1,5},{2,6},{3,7},{4,0},{5,1},{6,2},{7,3},{8,12},{9,13},{10,... | collective-permute-start | bytes 1966088 | tf_op jit(solution)/shard_map/ppermute | solution.py:588
  88.5 17.9 %collective-permute-start.13 = (bf16[384,512]{1,0:T(8,128)(2,1)S(1)}, bf16[384,512]{1,0:T(8,128)(2,1)S(1)}, u32[]{:S(2)}, u32[]{:S(2)}) collective-permute-start(bf16[384,512]{1,0:T(8,128)(2,1)S(1)} %get-tuple-element.192), channel_id=1, source_target_pairs={{0,2},{1,3},{2,0},{3,1},{4,6},{5,7},{6,4},{7,5},{8,10},{9,11},{10,... | collective-permute-start | bytes 1179656 | tf_op jit(solution)/shard_map/ppermute | solution.py:588
  88.9 17.6 %collective-permute-start.14 = (bf16[384,512]{1,0:T(8,128)(2,1)S(1)}, bf16[384,512]{1,0:T(8,128)(2,1)S(1)}, u32[]{:S(2)}, u32[]{:S(2)}) collective-permute-start(bf16[384,512]{1,0:T(8,128)(2,1)S(1)} %get-tuple-element.194), channel_id=1, source_target_pairs={{0,4},{1,5},{2,6},{3,7},{4,0},{5,1},{6,2},{7,3},{8,12},{9,13},{10,... | collective-permute-start | bytes 1179656 | tf_op jit(solution)/shard_map/ppermute | solution.py:588
  90.7 15.7 %collective-permute-start.11 = (bf16[320,512]{1,0:T(8,128)(2,1)S(1)}, bf16[320,512]{1,0:T(8,128)(2,1)S(1)}, u32[]{:S(2)}, u32[]{:S(2)}) collective-permute-start(bf16[320,512]{1,0:T(8,128)(2,1)S(1)} %get-tuple-element.187), channel_id=1, source_target_pairs={{0,4},{1,5},{2,6},{3,7},{4,0},{5,1},{6,2},{7,3},{8,12},{9,13},{10,... | collective-permute-start | bytes 983048 | tf_op jit(solution)/shard_map/ppermute | solution.py:588
  90.9 15.4 %collective-permute-start.12 = (bf16[320,512]{1,0:T(8,128)(2,1)S(1)}, bf16[320,512]{1,0:T(8,128)(2,1)S(1)}, u32[]{:S(2)}, u32[]{:S(2)}) collective-permute-start(bf16[320,512]{1,0:T(8,128)(2,1)S(1)} %get-tuple-element.189), channel_id=1, source_target_pairs={{0,2},{1,3},{2,0},{3,1},{4,6},{5,7},{6,4},{7,5},{8,10},{9,11},{10,... | collective-permute-start | bytes 983048 | tf_op jit(solution)/shard_map/ppermute | solution.py:588
  116.0 22.6 %collective-permute-start.16 = (bf16[1536,512]{1,0:T(8,128)(2,1)S(1)}, bf16[1536,512]{1,0:T(8,128)(2,1)S(1)}, u32[]{:S(2)}, u32[]{:S(2)}) collective-permute-start(bf16[1536,512]{1,0:T(8,128)(2,1)S(1)} %get-tuple-element.207), channel_id=1, source_target_pairs={{0,1},{1,0},{2,3},{3,2},{4,5},{5,4},{6,7},{7,6},{8,9},{9,8},{10,11... | collective-permute-start | bytes 4718600 | tf_op jit(solution)/shard_map/ppermute | solution.py:588
  116.2 12.9 %collective-permute-start.18 = (bf16[2,80,512]{2,1,0:T(8,128)(2,1)S(1)}, bf16[2,80,512]{2,1,0:T(8,128)(2,1)S(1)}, u32[]{:S(2)}, u32[]{:S(2)}) collective-permute-start(bf16[2,80,512]{2,1,0:T(8,128)(2,1)S(1)} %get-tuple-element.211), channel_id=1, source_target_pairs={{0,16},{1,17},{2,18},{3,19},{4,20},{5,21},{6,22},{7,23},{8,24},{9,... | collective-permute-start | bytes 491528 | tf_op jit(solution)/shard_map/ppermute | solution.py:588
  124.0 13.0 %collective-permute-start.19 = (bf16[2,80,512]{2,1,0:T(8,128)(2,1)S(1)}, bf16[2,80,512]{2,1,0:T(8,128)(2,1)S(1)}, u32[]{:S(2)}, u32[]{:S(2)}) collective-permute-start(bf16[2,80,512]{2,1,0:T(8,128)(2,1)S(1)} %get-tuple-element.212), channel_id=1, source_target_pairs={{0,24},{1,25},{2,26},{3,27},{4,28},{5,29},{6,30},{7,31},{8,16},{9,... | collective-permute-start | bytes 491528 | tf_op jit(solution)/shard_map/ppermute | solution.py:588
  125.5 15.1 %collective-permute-start.21 = (bf16[192,512]{1,0:T(8,128)(2,1)S(1)}, bf16[192,512]{1,0:T(8,128)(2,1)S(1)}, u32[]{:S(2)}, u32[]{:S(2)}) collective-permute-start(bf16[192,512]{1,0:T(8,128)(2,1)S(1)} %get-tuple-element.216), channel_id=1, source_target_pairs={{0,4},{1,5},{2,6},{3,7},{4,0},{5,1},{6,2},{7,3},{8,12},{9,13},{10,... | collective-permute-start | bytes 589832 | tf_op jit(solution)/shard_map/ppermute | solution.py:588
  127.0 15.1 %collective-permute-start.22 = (bf16[192,512]{1,0:T(8,128)(2,1)S(1)}, bf16[192,512]{1,0:T(8,128)(2,1)S(1)}, u32[]{:S(2)}, u32[]{:S(2)}) collective-permute-start(bf16[192,512]{1,0:T(8,128)(2,1)S(1)} %get-tuple-element.218), channel_id=1, source_target_pairs={{0,2},{1,3},{2,0},{3,1},{4,6},{5,7},{6,4},{7,5},{8,10},{9,11},{10,... | collective-permute-start | bytes 589832 | tf_op jit(solution)/shard_map/ppermute | solution.py:588
  129.1 16.1 %collective-permute-start.23 = (bf16[192,512]{1,0:T(8,128)(2,1)S(1)}, bf16[192,512]{1,0:T(8,128)(2,1)S(1)}, u32[]{:S(2)}, u32[]{:S(2)}) collective-permute-start(bf16[192,512]{1,0:T(8,128)(2,1)S(1)} %get-tuple-element.219), channel_id=1, source_target_pairs={{0,2},{1,3},{2,0},{3,1},{4,6},{5,7},{6,4},{7,5},{8,10},{9,11},{10,... | collective-permute-start | bytes 589832 | tf_op jit(solution)/shard_map/ppermute | solution.py:588
  138.6 13.0 %collective-permute-start.25 = (bf16[192,512]{1,0:T(8,128)(2,1)S(1)}, bf16[192,512]{1,0:T(8,128)(2,1)S(1)}, u32[]{:S(2)}, u32[]{:S(2)}) collective-permute-start(bf16[192,512]{1,0:T(8,128)(2,1)S(1)} %get-tuple-element.221), channel_id=1, source_target_pairs={{0,6},{1,7},{2,4},{3,5},{4,2},{5,3},{6,0},{7,1},{8,14},{9,15},{10,... | collective-permute-start | bytes 589832 | tf_op jit(solution)/shard_map/ppermute | solution.py:588
  142.2 14.8 %collective-permute-start.27 = (bf16[2,80,512]{2,1,0:T(8,128)(2,1)S(1)}, bf16[2,80,512]{2,1,0:T(8,128)(2,1)S(1)}, u32[]{:S(2)}, u32[]{:S(2)}) collective-permute-start(bf16[2,80,512]{2,1,0:T(8,128)(2,1)S(1)} %bitcast.110), channel_id=1, source_target_pairs={{0,8},{1,9},{2,10},{3,11},{4,12},{5,13},{6,14},{7,15},{8,0},{9,1},... | collective-permute-start | bytes 491528 | tf_op jit(solution)/shard_map/ppermute | solution.py:588
  147.5 13.1 %collective-permute-start.29 = (bf16[2,80,512]{2,1,0:T(8,128)(2,1)S(1)}, bf16[2,80,512]{2,1,0:T(8,128)(2,1)S(1)}, u32[]{:S(2)}, u32[]{:S(2)}) collective-permute-start(bf16[2,80,512]{2,1,0:T(8,128)(2,1)S(1)} %bitcast.112), channel_id=1, source_target_pairs={{0,24},{1,25},{2,26},{3,27},{4,28},{5,29},{6,30},{7,31},{8,16},{9,... | collective-permute-start | bytes 491528 | tf_op jit(solution)/shard_map/ppermute | solution.py:588
  151.6 33.8 %collective-permute-start.26 = (bf16[768,512]{1,0:T(8,128)(2,1)S(1)}, bf16[768,512]{1,0:T(8,128)(2,1)S(1)}, u32[]{:S(2)}, u32[]{:S(2)}) collective-permute-start(bf16[768,512]{1,0:T(8,128)(2,1)S(1)} %facing.1), channel_id=1, source_target_pairs={{0,2},{1,3},{2,0},{3,1},{4,6},{5,7},{6,4},{7,5},{8,10},{9,11},{10,... | collective-permute-start | bytes 2359304 | tf_op jit(solution)/shard_map/ppermute | solution.py:588
  151.8 12.8 %collective-permute-start.30 = (bf16[3,96,512]{2,1,0:T(8,128)(2,1)S(1)}, bf16[3,96,512]{2,1,0:T(8,128)(2,1)S(1)}, u32[]{:S(2)}, u32[]{:S(2)}) collective-permute-start(bf16[3,96,512]{2,1,0:T(8,128)(2,1)S(1)} %get-tuple-element.227), channel_id=1, source_target_pairs={{0,8},{1,9},{2,10},{3,11},{4,12},{5,13},{6,14},{7,15},{8,0},{9,1},... | collective-permute-start | bytes 884744 | tf_op jit(solution)/shard_map/ppermute | solution.py:588
  162.2 13.4 %collective-permute-start.32 = (bf16[320,512]{1,0:T(8,128)(2,1)S(1)}, bf16[320,512]{1,0:T(8,128)(2,1)S(1)}, u32[]{:S(2)}, u32[]{:S(2)}) collective-permute-start(bf16[320,512]{1,0:T(8,128)(2,1)S(1)} %bitcast.128), channel_id=1, source_target_pairs={{0,2},{1,3},{2,0},{3,1},{4,6},{5,7},{6,4},{7,5},{8,10},{9,11},{10,... | collective-permute-start | bytes 983048 | tf_op jit(solution)/shard_map/ppermute | solution.py:588
  179.2 22.4 %collective-permute-start.38 = (bf16[640,512]{1,0:T(8,128)(2,1)S(1)}, bf16[640,512]{1,0:T(8,128)(2,1)S(1)}, u32[]{:S(2)}, u32[]{:S(2)}) collective-permute-start(bf16[640,512]{1,0:T(8,128)(2,1)S(1)} %bitcast.102), channel_id=1, source_target_pairs={{0,2},{1,3},{2,0},{3,1},{4,6},{5,7},{6,4},{7,5},{8,10},{9,11},{10,... | collective-permute-start | bytes 1966088 | tf_op jit(solution)/shard_map/ppermute | solution.py:588
  180.8 20.8 %collective-permute-start.39 = (bf16[640,512]{1,0:T(8,128)(2,1)S(1)}, bf16[640,512]{1,0:T(8,128)(2,1)S(1)}, u32[]{:S(2)}, u32[]{:S(2)}) collective-permute-start(bf16[640,512]{1,0:T(8,128)(2,1)S(1)} %bitcast.104), channel_id=1, source_target_pairs={{0,4},{1,5},{2,6},{3,7},{4,0},{5,1},{6,2},{7,3},{8,12},{9,13},{10,... | collective-permute-start | bytes 1966088 | tf_op jit(solution)/shard_map/ppermute | solution.py:588
  202.4 15.3 %collective-permute-start.42 = (bf16[576,512]{1,0:T(8,128)(2,1)S(1)}, bf16[576,512]{1,0:T(8,128)(2,1)S(1)}, u32[]{:S(2)}, u32[]{:S(2)}) collective-permute-start(bf16[576,512]{1,0:T(8,128)(2,1)S(1)} %bitcast.116), channel_id=1, source_target_pairs={{0,2},{1,3},{2,0},{3,1},{4,6},{5,7},{6,4},{7,5},{8,10},{9,11},{10,... | collective-permute-start | bytes 1769480 | tf_op jit(solution)/shard_map/ppermute | solution.py:588
  203.2 15.0 %collective-permute-start.43 = (bf16[576,512]{1,0:T(8,128)(2,1)S(1)}, bf16[576,512]{1,0:T(8,128)(2,1)S(1)}, u32[]{:S(2)}, u32[]{:S(2)}) collective-permute-start(bf16[576,512]{1,0:T(8,128)(2,1)S(1)} %bitcast.118), channel_id=1, source_target_pairs={{0,4},{1,5},{2,6},{3,7},{4,0},{5,1},{6,2},{7,3},{8,12},{9,13},{10,... | collective-permute-start | bytes 1769480 | tf_op jit(solution)/shard_map/ppermute | solution.py:588
  (42 other events, 275.8 us)
